TPU v7x, 32 devices: a whole 2x2x4 slice. The times are simulated.
32 devices in a mesh: chan: 4 (over x, core), ctx: 8 (over z, y).
Axes of the slice: x: 2, y: 2, z: 4, core: 2. Of those that a mesh axis runs over, the one named last changes fastest.
Arguments:
- queries: bfloat16 [1024, 8192], P('ctx', 'chan'), may hold values from -6 to 6
- keys: bfloat16 [1024, 8192], P('ctx', 'chan'), may hold values from -6 to 6
- values: bfloat16 [1024, 8192], P('ctx', 'chan'), may hold values from -6 to 6
- filters: bfloat16 [4, 1024], P(None, 'ctx'), may hold values from -0.1875 to 0.1875
- cotangent: bfloat16 [1024, 8192], P('ctx', 'chan'), may hold values from -6 to 6
Outputs:
- output: bfloat16 [1024, 8192], P('ctx', 'chan')
- query_grad: bfloat16 [1024, 8192], P('ctx', 'chan')
- key_grad: bfloat16 [1024, 8192], P('ctx', 'chan')
- value_grad: bfloat16 [1024, 8192], P('ctx', 'chan')
- filter_grad: float32 [4, 1024], P(None, 'ctx')
All inputs are finite; a program needn't handle non-finite values.
Results may differ from a plain program's by a relative error of at most 0.015.
Values may be sent and summed in bfloat16 or wider, within the bound.
No kernel may reach another device: no remote copies, remote signals or barrier semaphores. Data moves between devices by JAX's collectives and lax.ppermute only.
A program may use at most 64 MiB of HBM per device.

v0:
```python
import jax
import jax.numpy as jnp
from jax import lax
from jax.sharding import PartitionSpec as P

D = 8192
NFILT = 4


def toeplitz(padded, base, height, breadth):
    middle = padded.shape[1] // 2
    span = height + breadth - 1
    window = lax.dynamic_slice_in_dim(padded, middle + base - breadth + 1, span, 1)
    flipped = window[:, ::-1]
    tiled = jnp.tile(flipped, (1, height + 1))
    flat = tiled[:, height - 1 : height - 1 + height * (span - 1)]
    return flat.reshape(padded.shape[0], height, span - 1)[:, :, :breadth]


def diagonal_sums(product):
    nfil, height, breadth = product.shape
    stride = height + breadth
    flipped = product[:, :, ::-1]
    padded = jnp.pad(flipped, ((0, 0), (0, 0), (0, height)))
    flat = padded.reshape(nfil, height * stride)[:, : height * (stride - 1)]
    return jnp.sum(flat.reshape(nfil, height, stride - 1), axis=1)


def add_lags(lag_acc, sums, first_lag):
    middle = lag_acc.shape[1] // 2
    where = middle + first_lag
    current = lax.dynamic_slice_in_dim(lag_acc, where, sums.shape[1], 1)
    return lax.dynamic_update_slice_in_dim(lag_acc, current + sums, where, 1)


def shards(queries, keys, values, filters, cotangent):
    rows, width = queries.shape
    nfil = filters.shape[0]
    gated = (keys.astype(jnp.float32) * values.astype(jnp.float32)).astype(jnp.bfloat16)
    back = (cotangent.astype(jnp.float32) * queries.astype(jnp.float32)).astype(jnp.bfloat16)
    taps = lax.all_gather(filters, "ctx", axis=1, tiled=True)
    total = taps.shape[1]
    padded = jnp.concatenate([jnp.zeros_like(taps), taps], axis=1)
    lag_start = jnp.zeros((nfil, 2 * total), jnp.float32)
    chan_gated, chan_back = (
        lax.all_to_all(gated, "ctx", split_axis=1, concat_axis=0, tiled=True),
        lax.all_to_all(back, "ctx", split_axis=1, concat_axis=0, tiled=True),
    )
    blocks = total // rows
    slim = chan_gated.shape[1] // nfil
    gated_cols = chan_gated.reshape(blocks, rows, slim, nfil)
    back_cols = chan_back.reshape(blocks, rows, slim, nfil)
    gated_pad = jnp.concatenate([jnp.zeros_like(gated_cols), gated_cols], axis=0)
    back_pad = jnp.concatenate([back_cols, jnp.zeros_like(back_cols)], axis=0)
    bundle = 4

    def turn(index, carry):
        mixed_acc, grad_acc, lag_acc = carry
        for member in range(bundle):
            offset = index * bundle + member
            tile = toeplitz(padded, offset * rows, rows, rows)
            earlier = lax.dynamic_slice_in_dim(gated_pad, blocks - offset, blocks, 0)
            later = lax.dynamic_slice_in_dim(back_pad, offset, blocks, 0)
            mixed_acc = mixed_acc + jnp.einsum(
                "fst,ntcf->nscf", tile, earlier, preferred_element_type=jnp.float32
            )
            grad_acc = grad_acc + jnp.einsum(
                "fst,nscf->ntcf", tile, later, preferred_element_type=jnp.float32
            )
            product = jnp.einsum(
                "nscf,ntcf->fst", back_cols, earlier, preferred_element_type=jnp.float32
            )
            lag_acc = add_lags(lag_acc, diagonal_sums(product), offset * rows - rows + 1)
        return (mixed_acc, grad_acc, lag_acc)

    blank = jnp.zeros((blocks, rows, slim, nfil), jnp.float32)
    mixed_acc, grad_acc, lag_part = lax.fori_loop(
        0, blocks // bundle, turn, (blank, blank, lag_start)
    )
    mixed_chan = mixed_acc.reshape(total, slim * nfil)
    grad_chan = grad_acc.reshape(total, slim * nfil)
    mixed, gated_grad = (
        lax.all_to_all(mixed_chan, "ctx", split_axis=0, concat_axis=1, tiled=True),
        lax.all_to_all(grad_chan, "ctx", split_axis=0, concat_axis=1, tiled=True),
    )
    lag_share = lax.psum_scatter(
        lag_part[:, total:].astype(jnp.bfloat16), "ctx", scatter_dimension=1, tiled=True
    ).astype(jnp.float32)
    lag_total = lax.psum(lag_share, "chan")
    scale = (total * (D // NFILT)) ** (-0.5)
    filter_grad = lag_total * scale
    output = (queries.astype(jnp.float32) * mixed).astype(jnp.bfloat16)
    query_grad = (cotangent.astype(jnp.float32) * mixed).astype(jnp.bfloat16)
    key_grad = (gated_grad * values.astype(jnp.float32)).astype(jnp.bfloat16)
    value_grad = (gated_grad * keys.astype(jnp.float32)).astype(jnp.bfloat16)
    return (output, query_grad, key_grad, value_grad, filter_grad)


def solution(mesh):
    placed = (
        P("ctx", "chan"),
        P("ctx", "chan"),
        P("ctx", "chan"),
        P(None, "ctx"),
        P("ctx", "chan"),
    )
    return jax.shard_map(
        shards,
        mesh=mesh,
        in_specs=placed,
        out_specs=(
            P("ctx", "chan"),
            P("ctx", "chan"),
            P("ctx", "chan"),
            P("ctx", "chan"),
            P(None, "ctx"),
        ),
        check_vma=False,
    )
```

profile of v0, /device:TPU:0, one launch (start us, length us, event | category | flops | bytes accessed | tf_op | source)
XLA Modules:
  0.0 252.5 jit_solution(15518346557554165049)
XLA Ops:
  7.2 1.4 copy.44
  10.3 7.4 %all-to-all-start.1 = ((bf16[128,8,256]{0,2,1:T(8,128)(2,1)}), bf16[128,8,256]{0,2,1:T(8,128)(2,1)S(1)}, u32[]{:S(2)}, u32[]{:S(2)}) async-start(bf16[128,8,256]{0,2,1:T(8,128)(2,1)} %bitcast.3), calls=%async_computation.1 | async-start | bytes 1048576 | tf_op jit(solution)/shard_map/all_to_all | solution.py:47
  20.0 12.2 %all-to-all-done.1 = bf16[128,8,256]{0,2,1:T(8,128)(2,1)S(1)} async-done(((bf16[128,8,256]{0,2,1:T(8,128)(2,1)}), bf16[128,8,256]{0,2,1:T(8,128)(2,1)S(1)}, u32[]{:S(2)}, u32[]{:S(2)}) %all-to-all-start.1) | async-done | bytes 524320 | tf_op jit(solution)/shard_map/all_to_all | solution.py:47
  32.2 3.6 %all-to-all-start = ((bf16[128,8,256]{0,2,1:T(8,128)(2,1)}), bf16[128,8,256]{0,2,1:T(8,128)(2,1)S(1)}, u32[]{:S(2)}, u32[]{:S(2)}) async-start(bf16[128,8,256]{0,2,1:T(8,128)(2,1)} %bitcast), calls=%async_computation | async-start | bytes 1048576 | tf_op jit(solution)/shard_map/all_to_all | solution.py:46
  36.6 22.6 %all_gather.3 = bf16[4,1024]{1,0:T(4,128)(2,1)S(1)} all-gather(bf16[4,128]{1,0:T(4,128)(2,1)S(1)} %copy-done.15), channel_id=1, replica_groups=mesh['chan'=4,'ctx'=8] {'ctx'}, dimensions={1}, use_global_device_ids=true | all-gather | bytes 9216 | tf_op jit(solution)/shard_map/all_gather | solution.py:41
  60.7 68.6 %while.23 = (s32[]{:T(128)}, f32[8,128,64,4]{1,2,0,3:T(8,128)}, f32[8,128,64,4]{1,2,0,3:T(8,128)}, f32[4,2048]{1,0:T(4,128)S(1)}, bf16[16,128,64,4]{1,2,0,3:T(8,...) while((s32[]{:T(128)}, f32[8,128,64,4]{1,2,0,3:T(8,128)}, ...), condition=%wide.region_5.6_spmd.clone, body=%wide.region_0.5_spmd.clone.sunk | while | flops 808450048 | bytes 61952348 | solution.py:77
  64.0 1.7 reshape.256
  67.6 1.7 reshape.255
  71.1 1.7 reshape.254
  75.8 1.7 reshape.257
  83.5 1.5 reshape.251
  86.2 1.9 slice.245
  88.1 1.7 reshape.250
  91.4 1.3 fusion.89
  93.6 1.3 fusion.85
  97.8 1.7 reshape.256
  101.4 1.7 reshape.255
  105.0 1.7 reshape.254
  109.6 1.7 reshape.257
  117.3 1.5 reshape.251
  120.0 1.9 slice.245
  121.9 1.7 reshape.250
  123.6 1.6 fusion.86
  125.8 1.3 fusion.89
  128.0 1.3 fusion.85
  129.3 1.8 copy.53
  132.3 3.7 %all-to-all-start.2 = ((f32[8,128,256]{1,2,0:T(8,128)}), f32[8,128,256]{1,2,0:T(8,128)S(1)}, u32[]{:S(2)}, u32[]{:S(2)}) async-start(f32[8,128,256]{1,2,0:T(8,128)} %copy.54), calls=%async_computation.2 | async-start | bytes 2097152 | tf_op jit(solution)/shard_map/all_to_all | solution.py:83
  137.8 21.0 %all-to-all-done.2 = f32[8,128,256]{1,2,0:T(8,128)S(1)} async-done(((f32[8,128,256]{1,2,0:T(8,128)}), f32[8,128,256]{1,2,0:T(8,128)S(1)}, u32[]{:S(2)}, u32[]{:S(2)}) %all-to-all-start.2) | async-done | bytes 1048608 | tf_op jit(solution)/shard_map/all_to_all | solution.py:83
  159.8 3.6 %all-to-all-start.3 = ((f32[8,128,256]{1,2,0:T(8,128)}), f32[8,128,256]{1,2,0:T(8,128)S(1)}, u32[]{:S(2)}, u32[]{:S(2)}) async-start(f32[8,128,256]{1,2,0:T(8,128)} %copy.56), calls=%async_computation.3 | async-start | bytes 2097152 | tf_op jit(solution)/shard_map/all_to_all | solution.py:84
  164.3 68.2 %reduce-scatter.4.cloned.1.call-done = bf16[128,4]{1,0:T(8,128)(2,1)} async-done(((bf16[1024,4]{1,0:T(8,128)(2,1)}), bf16[128,4]{1,0:T(8,128)(2,1)}) %reduce-scatter.4.cloned.1.call-update) | async-done | bytes 1040
  233.4 5.7 %psum.7 = f32[4,128]{1,0:T(4,128)S(1)} all-reduce(bf16[4,128]{1,0:T(4,128)(2,1)S(1)} %copy.70), channel_id=1, replica_groups=mesh['chan'=4,'ctx'=8] {'chan'}, use_global_device_ids=true, to_apply=%region_7.8 | all-reduce | flops 512 | bytes 3072 | tf_op jit(solution)/shard_map/psum | solution.py:89
  239.6 1.4 fusion.37
  (194 shorter events, 54.4 us)
Async XLA Ops:
  7.2 1.4 copy-start.12
  8.6 0.8 copy-start.7
  9.4 1.0 copy-start.9
  10.3 7.4 %copy-start.13 = (bf16[128,2048]{1,0:T(8,128)(2,1)S(1)}, bf16[128,2048]{1,0:T(8,128)(2,1)}, u32[]{:S(2)}) copy-start(bf16[128,2048]{1,0:T(8,128)(2,1)} %param.8) | copy-start | bytes 1572868
  10.3 21.9 %all-to-all-start.1 = ((bf16[128,8,256]{0,2,1:T(8,128)(2,1)}), bf16[128,8,256]{0,2,1:T(8,128)(2,1)S(1)}, u32[]{:S(2)}, u32[]{:S(2)}) async-start(bf16[128,8,256]{0,2,1:T(8,128)(2,1)} %bitcast.3), calls=%async_computation.1 | async-start | bytes 1048576 | tf_op jit(solution)/shard_map/all_to_all | solution.py:47
  17.7 1.0 copy-start.14
  18.8 1.2 copy-start.3
  19.1 1.0 copy-start.5
  32.2 27.5 %all-to-all-start = ((bf16[128,8,256]{0,2,1:T(8,128)(2,1)}), bf16[128,8,256]{0,2,1:T(8,128)(2,1)S(1)}, u32[]{:S(2)}, u32[]{:S(2)}) async-start(bf16[128,8,256]{0,2,1:T(8,128)(2,1)} %bitcast), calls=%async_computation | async-start | bytes 1048576 | tf_op jit(solution)/shard_map/all_to_all | solution.py:46
  35.9 0.7 copy-start.15
  89.8 1.0 copy-start.2
  91.4 1.3 copy-start.1
  123.6 1.6 copy-start.2
  125.8 1.3 copy-start.1
  132.3 3.7 %copy-start = (f32[8,128,64,4]{1,2,0,3:T(8,128)S(1)}, f32[8,128,64,4]{1,2,0,3:T(8,128)}, u32[]{:S(2)}) copy-start(f32[8,128,64,4]{1,2,0,3:T(8,128)} %get-tuple-element.345) | copy-start | bytes 3145732
  132.3 26.5 %all-to-all-start.2 = ((f32[8,128,256]{1,2,0:T(8,128)}), f32[8,128,256]{1,2,0:T(8,128)S(1)}, u32[]{:S(2)}, u32[]{:S(2)}) async-start(f32[8,128,256]{1,2,0:T(8,128)} %copy.54), calls=%async_computation.2 | async-start | bytes 2097152 | tf_op jit(solution)/shard_map/all_to_all | solution.py:83
  158.8 1.0 copy-start.11
  158.8 80.8 %copy-start.10 = (bf16[128,2048]{0,1:T(8,128)(2,1)S(1)}, bf16[128,2048]{0,1:T(8,128)(2,1)}, u32[]{:S(2)}) copy-start(bf16[128,2048]{0,1:T(8,128)(2,1)} %copy-done.9) | copy-start | bytes 1572868
  159.8 83.3 %all-to-all-start.3 = ((f32[8,128,256]{1,2,0:T(8,128)}), f32[8,128,256]{1,2,0:T(8,128)S(1)}, u32[]{:S(2)}, u32[]{:S(2)}) async-start(f32[8,128,256]{1,2,0:T(8,128)} %copy.56), calls=%async_computation.3 | async-start | bytes 2097152 | tf_op jit(solution)/shard_map/all_to_all | solution.py:84
  163.3 76.3 %copy-start.8 = (bf16[128,2048]{0,1:T(8,128)(2,1)S(1)}, bf16[128,2048]{0,1:T(8,128)(2,1)}, u32[]{:S(2)}) copy-start(bf16[128,2048]{0,1:T(8,128)(2,1)} %copy-done.7) | copy-start | bytes 1572868
  163.3 69.2 %reduce-scatter.4.cloned.1.call-start = ((), (), s32[]{:S(2)}) async-start(), calls=%async_computation.5 | async-start | bytes 294912
  242.0 1.0 copy-start.4
  242.0 1.4 copy-start.6
Sparse Core Ops, SparseCore 0:
  168.1 64.3 reduce-scatter.3
where the time goes:
time: 254 us; the launch traced here: 253 us
  waiting for transfers between devices  101 us (40%)
  local copies, waits for them, and re-layouts  71.4 us (28%)
  blocking collectives  28.3 us (11%)
  starting transfers between devices  18.3 us (7%)
  between operations  14.2 us (6%)
  matrix products  12.7 us (5%)
  other arithmetic  5.17 us (2%)
    unnamed x2, waiting for transfers between devices  68.2 us
    all_gather x1, blocking collectives, shards(): taps = lax.all_gather(filters, 'ctx', axis=1, tiled=True)  22.6 us
    all_to_all x1, waiting for transfers between devices, shards(): lax.all_to_all(mixed_chan, 'ctx', split_axis=0, concat_axis=1, tiled=True)  21 us
    reshape x8, local copies, waits for them, and re-layouts, diagonal_sums(): return jnp.sum(flat.reshape(nfil, height, stride - 1), axis=1)  13.4 us
    all_to_all x1, waiting for transfers between devices, shards(): lax.all_to_all(back, 'ctx', split_axis=1, concat_axis=0, tiled=True)  12.2 us
    unnamed x40, local copies, waits for them, and re-layouts  11.6 us
    reshape x8, local copies, waits for them, and re-layouts, toeplitz(): return flat.reshape(padded.shape[0], height, span - 1)[:, :, :breadth]  9.61 us
    all_to_all x1, starting transfers between devices, shards(): lax.all_to_all(back, 'ctx', split_axis=1, concat_axis=0, tiled=True)  7.41 us
  transfers between devices with their start and end apart: 5, of which 3 were waited for; matrix products, arithmetic and copies ran while one was open for 4% of the time, Pallas kernels for 0%

commit v1 on v0

--- a/solution.py
+++ b/solution.py
@@ -1,10 +1,289 @@
+import functools
+
 import jax
 import jax.numpy as jnp
 from jax import lax
+from jax.experimental import pallas as pl
+from jax.experimental.pallas import tpu as pltpu
 from jax.sharding import PartitionSpec as P
 
 D = 8192
 NFILT = 4
+LANES = 128
+
+
+def exchange(size, reverse, dtype):
+    row = lax.broadcasted_iota(jnp.int32, (size, size), 0)
+    col = lax.broadcasted_iota(jnp.int32, (size, size), 1)
+    target = jnp.where(reverse, size - 1 - row, row)
+    return jnp.where(col == target, 1.0, 0.0).astype(jnp.float32).astype(dtype)
+
+
+def exact_rows(matrix, values):
+    return jnp.dot(matrix, values, preferred_element_type=jnp.float32).astype(jnp.bfloat16)
+
+
+def gate_kernel(half, slim, me_ref, q_ref, k_ref, v_ref, g_ref, *refs):
+    outs, (within, across) = refs[:-2], refs[-2:]
+    rows = q_ref.shape[0]
+    me = me_ref[0]
+    upper = me >= half
+    gated = (k_ref[...].astype(jnp.float32) * v_ref[...].astype(jnp.float32)).astype(jnp.bfloat16)
+    back = (g_ref[...].astype(jnp.float32) * q_ref[...].astype(jnp.float32)).astype(jnp.bfloat16)
+    first = jnp.where(upper, gated, back)
+    second = jnp.where(upper, back, gated)
+    turn = exchange(rows, upper, jnp.bfloat16)
+    turn_other = exchange(rows, jnp.logical_not(upper), jnp.bfloat16)
+    within[0:rows, :] = exact_rows(turn, first)
+    within[rows : 2 * rows, :] = exact_rows(turn, second)
+    across[...] = exact_rows(turn_other, second)
+    for step in range(2 * half):
+        part = (me ^ step) & (half - 1)
+        lanes = pl.ds(pl.multiple_of(part * slim, LANES), slim)
+        source = within if step < half else across
+        outs[step][...] = source[:, lanes]
+
+
+def taps_kernel(me_ref, taps_ref, near_ref, far_ref, line):
+    blocks = line.shape[1] // LANES
+    nfil, size, total = near_ref.shape
+    for step in range(blocks):
+        place = pl.multiple_of((me_ref[0] ^ step) * LANES, LANES)
+        line[:, pl.ds(place, LANES)] = taps_ref[8 * step : 8 * step + 8, :]
+    row = lax.broadcasted_iota(jnp.int32, (size, total), 0)
+    col = lax.broadcasted_iota(jnp.int32, (size, total), 1)
+    for index in range(nfil):
+        spread = jnp.broadcast_to(line[index : index + 1, :], (size, total))
+        rolled = pltpu.roll(spread, 0, 1, stride=1, stride_axis=0)
+        band = jnp.where(col >= row, rolled, 0.0)
+        near_ref[index] = band.astype(jnp.bfloat16)
+        reach = far_ref.shape[2] // size
+        for block in range(reach):
+            piece = band[:, (reach - 1 - block) * size : (reach - block) * size]
+            far_ref[index, :, block * size : (block + 1) * size] = piece.T.astype(jnp.bfloat16)
+
+
+def assemble(half, me, upper, arrived, first_ref, second_ref):
+    rows = arrived[0].shape[0] // 2
+    flip = jnp.where(upper, half - 1, 0)
+    slots = []
+    for step in range(2 * half):
+        slot = ((me ^ step) & (half - 1)) ^ flip
+        slots.append(slot)
+        if step < half:
+            where = pl.ds(pl.multiple_of(slot * rows, rows), rows)
+            first_ref[where, :] = arrived[step][0:rows, :]
+            second_ref[where, :] = arrived[step][rows : 2 * rows, :]
+        else:
+            where = pl.ds(pl.multiple_of((slot + half) * rows, rows), rows)
+            first_ref[where, :] = arrived[step][...]
+    return slots
+
+
+def lane_mask(width, nfil, index):
+    lane = lax.broadcasted_iota(jnp.int32, (1, width), 1)
+    return jnp.where(lane % nfil == index, 1.0, 0.0).astype(jnp.bfloat16)
+
+
+def conv_kernel(half, me_ref, *refs):
+    arrived = refs[: 2 * half]
+    near_ref, far_ref = refs[2 * half : 2 * half + 2]
+    outs = refs[2 * half + 2 : 3 * half + 2]
+    first_ref, second_ref, result_ref = refs[3 * half + 2 :]
+    nfil, size, total = near_ref.shape
+    width = first_ref.shape[1]
+    own = second_ref.shape[0]
+    rows = own // half
+    me = me_ref[0]
+    upper = me >= half
+    slots = assemble(half, me, upper, arrived, first_ref, second_ref)
+    masks = [lane_mask(width, nfil, index) for index in range(nfil)]
+    for top in range(0, own, size):
+        acc = jnp.zeros((size, width), jnp.float32)
+        for index in range(nfil):
+            acc += jnp.dot(
+                near_ref[index, :, 0 : total - top],
+                first_ref[top:total, :] * masks[index],
+                preferred_element_type=jnp.float32,
+            )
+        result_ref[0, top : top + size, :] = acc.astype(jnp.bfloat16)
+        acc = jnp.zeros((size, width), jnp.float32)
+        for index in range(nfil):
+            acc += jnp.dot(
+                far_ref[index, :, own - size - top : own],
+                second_ref[0 : top + size, :] * masks[index],
+                preferred_element_type=jnp.float32,
+            )
+        result_ref[1, top : top + size, :] = acc.astype(jnp.bfloat16)
+    for step in range(half):
+        where = pl.ds(pl.multiple_of(slots[step] * rows, rows), rows)
+        outs[step][0:rows, :] = result_ref[0, where, :]
+        outs[step][rows : 2 * rows, :] = result_ref[1, where, :]
+
+
+def lag_kernel(half, me_ref, *refs):
+    arrived = refs[: 2 * half]
+    out_ref = refs[2 * half]
+    first_ref, second_ref = refs[2 * half + 1 :]
+    total, width = first_ref.shape
+    own = second_ref.shape[0]
+    rows = own // half
+    nfil = NFILT
+    me = me_ref[0]
+    upper = me >= half
+    assemble(half, me, upper, arrived, first_ref, second_ref)
+    turn = exchange(rows, True, jnp.bfloat16)
+    share = width // 2
+    lanes = pl.ds(pl.multiple_of(jnp.where(upper, share, 0), LANES), share)
+    contract = (((1,), (1,)), ((), ()))
+    flipped = [exact_rows(turn, second_ref[b * rows : (b + 1) * rows, :]) for b in range(half)]
+    halves = [exact_rows(turn, second_ref[b * rows : (b + 1) * rows, lanes]) for b in range(half)]
+    for index in range(nfil):
+        mask = lane_mask(width, nfil, index)
+        half_mask = lane_mask(share, nfil, index)
+        inner = first_ref[0:own, :] * mask
+        outer = first_ref[own:total, lanes] * half_mask
+        acc = jnp.zeros((rows, total + rows), jnp.float32)
+        for block in range(half):
+            start = block * rows
+            near = lax.dot_general(
+                flipped[block], inner[start:own], contract, preferred_element_type=jnp.float32
+            )
+            far = lax.dot_general(
+                halves[block], outer, contract, preferred_element_type=jnp.float32
+            )
+            pieces = [near, far, jnp.zeros((rows, start + rows), jnp.float32)]
+            acc = acc + jnp.concatenate(pieces, axis=1)
+        rolled = pltpu.roll(acc, 0, 1, stride=1, stride_axis=0)
+        sums = jnp.sum(rolled, axis=0, keepdims=True)
+        sums = jnp.broadcast_to(sums, (8, total + rows))
+        lags = pltpu.roll(sums, total + 1, 1)
+        out_ref[index : index + 1, :] = lags[0:1, 0:total]
+    out_ref[nfil:8, :] = jnp.zeros((8 - nfil, total), jnp.float32)
+
+
+def final_kernel(half, slim, me_ref, q_ref, k_ref, v_ref, g_ref, *refs):
+    results = refs[:half]
+    out_ref, dq_ref, dk_ref, dv_ref = refs[half : half + 4]
+    (joined,) = refs[half + 4 :]
+    rows = q_ref.shape[0]
+    me = me_ref[0]
+    upper = me >= half
+    turn = exchange(rows, upper, jnp.bfloat16)
+    for step in range(half):
+        part = (me ^ step) & (half - 1)
+        lanes = pl.ds(pl.multiple_of(part * slim, LANES), slim)
+        joined[:, lanes] = results[step][...]
+    first = jnp.dot(turn, joined[0:rows, :], preferred_element_type=jnp.float32)
+    second = jnp.dot(turn, joined[rows : 2 * rows, :], preferred_element_type=jnp.float32)
+    mixed = jnp.where(upper, first, second)
+    grad = jnp.where(upper, second, first)
+    out_ref[...] = (q_ref[...].astype(jnp.float32) * mixed).astype(jnp.bfloat16)
+    dq_ref[...] = (g_ref[...].astype(jnp.float32) * mixed).astype(jnp.bfloat16)
+    dk_ref[...] = (v_ref[...].astype(jnp.float32) * grad).astype(jnp.bfloat16)
+    dv_ref[...] = (k_ref[...].astype(jnp.float32) * grad).astype(jnp.bfloat16)
+
+
+def swap(value, step, count):
+    return lax.ppermute(value, "ctx", [(i, i ^ step) for i in range(count)])
+
+
+def call(kernel, outs, scratch, flops, nbytes, *args):
+    return pl.pallas_call(
+        kernel,
+        out_shape=outs,
+        in_specs=[pl.BlockSpec(memory_space=pltpu.SMEM)]
+        + [pl.BlockSpec(memory_space=pltpu.VMEM)] * (len(args) - 1),
+        out_specs=jax.tree.map(lambda _: pl.BlockSpec(memory_space=pltpu.VMEM), outs),
+        scratch_shapes=scratch,
+        compiler_params=pltpu.CompilerParams(vmem_limit_bytes=48 * 2**20),
+        cost_estimate=pl.CostEstimate(flops=flops, bytes_accessed=nbytes, transcendentals=0),
+    )(*args)
+
+
+def halves_plan(count, chans, queries, keys, values, filters, cotangent):
+    rows, width = queries.shape
+    nfil = filters.shape[0]
+    half = count // 2
+    slim = width // half
+    total = count * rows
+    own = half * rows
+    size = min(256, own)
+    low = jnp.bfloat16
+    shape = jax.ShapeDtypeStruct
+    me = lax.axis_index("ctx")
+    where = me.astype(jnp.int32).reshape(1)
+
+    taps = jnp.pad(filters.astype(jnp.float32), ((0, 8 - nfil), (0, 0)))
+    step = 1
+    while step < count:
+        taps = jnp.concatenate([taps, swap(taps, step, count)], axis=0)
+        step *= 2
+
+    sent = call(
+        functools.partial(gate_kernel, half, slim),
+        [shape((2 * rows if k < half else rows, slim), low) for k in range(count)],
+        [pltpu.VMEM((2 * rows, width), low), pltpu.VMEM((rows, width), low)],
+        6 * rows * rows * width,
+        14 * rows * width,
+        where, queries, keys, values, cotangent,
+    )
+    arrived = [sent[0]] + [swap(sent[k], k, count) for k in range(1, count)]
+
+    near, far = call(
+        taps_kernel,
+        [shape((nfil, size, total), low), shape((nfil, size, own), low)],
+        [pltpu.VMEM((8, total), jnp.float32)],
+        nfil * size * total * 8,
+        nfil * size * total * 4,
+        where, taps,
+    )
+    results = call(
+        functools.partial(conv_kernel, half),
+        [shape((2 * rows, slim), low)] * half,
+        [
+            pltpu.VMEM((total, slim), low),
+            pltpu.VMEM((own, slim), low),
+            pltpu.VMEM((2, own, slim), low),
+        ],
+        2 * nfil * own * slim * (total + own),
+        4 * total * slim,
+        where, *arrived, near, far,
+    )
+    returned = [results[0]] + [swap(results[k], k, count) for k in range(1, half)]
+    lags = call(
+        functools.partial(lag_kernel, half),
+        shape((8, total), jnp.float32),
+        [pltpu.VMEM((total, slim), low), pltpu.VMEM((own, slim), low)],
+        2 * nfil * own * slim * total,
+        4 * total * slim,
+        where, *arrived,
+    )
+    step = 1
+    while step < chans:
+        lags = lags + lax.ppermute(lags, "chan", [(i, i ^ step) for i in range(chans)])
+        step *= 2
+    step = half
+    while step:
+        extent = lags.shape[1] // 2
+        low_part, high_part = lags[:, :extent], lags[:, extent:]
+        mine_high = (me & step) != 0
+        keep = jnp.where(mine_high, high_part, low_part)
+        send = jnp.where(mine_high, low_part, high_part)
+        lags = keep + swap(send, step, count)
+        step //= 2
+    scale = (total * (D // NFILT)) ** (-0.5)
+    filter_grad = lags[:nfil] * scale
+
+    outs = call(
+        functools.partial(final_kernel, half, slim),
+        [shape((rows, width), low)] * 4,
+        [pltpu.VMEM((2 * rows, width), low)],
+        4 * rows * rows * width,
+        20 * rows * width,
+        where, queries, keys, values, cotangent, *returned,
+    )
+    return (*outs, filter_grad)
 
 
 def toeplitz(padded, base, height, breadth):
@@ -33,7 +312,7 @@
     return lax.dynamic_update_slice_in_dim(lag_acc, current + sums, where, 1)
 
 
-def shards(queries, keys, values, filters, cotangent):
+def channel_plan(queries, keys, values, filters, cotangent):
     rows, width = queries.shape
     nfil = filters.shape[0]
     gated = (keys.astype(jnp.float32) * values.astype(jnp.float32)).astype(jnp.bfloat16)
@@ -52,31 +331,26 @@
     back_cols = chan_back.reshape(blocks, rows, slim, nfil)
     gated_pad = jnp.concatenate([jnp.zeros_like(gated_cols), gated_cols], axis=0)
     back_pad = jnp.concatenate([back_cols, jnp.zeros_like(back_cols)], axis=0)
-    bundle = 4
-
-    def turn(index, carry):
+
+    def turn(offset, carry):
         mixed_acc, grad_acc, lag_acc = carry
-        for member in range(bundle):
-            offset = index * bundle + member
-            tile = toeplitz(padded, offset * rows, rows, rows)
-            earlier = lax.dynamic_slice_in_dim(gated_pad, blocks - offset, blocks, 0)
-            later = lax.dynamic_slice_in_dim(back_pad, offset, blocks, 0)
-            mixed_acc = mixed_acc + jnp.einsum(
-                "fst,ntcf->nscf", tile, earlier, preferred_element_type=jnp.float32
-            )
-            grad_acc = grad_acc + jnp.einsum(
-                "fst,nscf->ntcf", tile, later, preferred_element_type=jnp.float32
-            )
-            product = jnp.einsum(
-                "nscf,ntcf->fst", back_cols, earlier, preferred_element_type=jnp.float32
-            )
-            lag_acc = add_lags(lag_acc, diagonal_sums(product), offset * rows - rows + 1)
+        tile = toeplitz(padded, offset * rows, rows, rows)
+        earlier = lax.dynamic_slice_in_dim(gated_pad, blocks - offset, blocks, 0)
+        later = lax.dynamic_slice_in_dim(back_pad, offset, blocks, 0)
+        mixed_acc = mixed_acc + jnp.einsum(
+            "fst,ntcf->nscf", tile, earlier, preferred_element_type=jnp.float32
+        )
+        grad_acc = grad_acc + jnp.einsum(
+            "fst,nscf->ntcf", tile, later, preferred_element_type=jnp.float32
+        )
+        product = jnp.einsum(
+            "nscf,ntcf->fst", back_cols, earlier, preferred_element_type=jnp.float32
+        )
+        lag_acc = add_lags(lag_acc, diagonal_sums(product), offset * rows - rows + 1)
         return (mixed_acc, grad_acc, lag_acc)
 
     blank = jnp.zeros((blocks, rows, slim, nfil), jnp.float32)
-    mixed_acc, grad_acc, lag_part = lax.fori_loop(
-        0, blocks // bundle, turn, (blank, blank, lag_start)
-    )
+    mixed_acc, grad_acc, lag_part = lax.fori_loop(0, blocks, turn, (blank, blank, lag_start))
     mixed_chan = mixed_acc.reshape(total, slim * nfil)
     grad_chan = grad_acc.reshape(total, slim * nfil)
     mixed, gated_grad = (
@@ -97,23 +371,20 @@
 
 
 def solution(mesh):
-    placed = (
-        P("ctx", "chan"),
-        P("ctx", "chan"),
-        P("ctx", "chan"),
-        P(None, "ctx"),
-        P("ctx", "chan"),
-    )
+    count, chans = mesh.shape["ctx"], mesh.shape["chan"]
+
+    def shards(queries, keys, values, filters, cotangent):
+        width = queries.shape[1]
+        quarter = width // max(count // 2, 1)
+        if count > 2 and quarter % (2 * LANES) == 0 and queries.shape[0] == LANES:
+            return halves_plan(count, chans, queries, keys, values, filters, cotangent)
+        return channel_plan(queries, keys, values, filters, cotangent)
+
+    wide = P("ctx", "chan")
     return jax.shard_map(
         shards,
         mesh=mesh,
-        in_specs=placed,
-        out_specs=(
-            P("ctx", "chan"),
-            P("ctx", "chan"),
-            P("ctx", "chan"),
-            P("ctx", "chan"),
-            P(None, "ctx"),
-        ),
+        in_specs=(wide, wide, wide, P(None, "ctx"), wide),
+        out_specs=(wide, wide, wide, wide, P(None, "ctx")),
         check_vma=False,
     )

time: 254 us -> 72.3 us (0.28)
  waiting for transfers between devices: 101 us -> 27.1 us
  local copies, waits for them, and re-layouts: 71.4 us -> 4.18 us
  blocking collectives: 28.3 us -> 0 us
  between operations: 14.2 us -> 0.74 us
  matrix products: 12.7 us -> 0 us
  starting transfers between devices: 18.3 us -> 28.9 us
  Pallas kernels: 0 us -> 10.4 us
  other arithmetic: 5.17 us -> 0.64 us
    unnamed x2 -> x0, waiting for transfers between devices: 68.2 us -> none
    all_to_all x4 -> x0, waiting for transfers between devices: 33.2 us -> none  [the longest x1 21 us: shards(): lax.all_to_all(mixed_chan, 'ctx', split_axis=0, concat_axis=1, tiled=True)]
    ppermute x0 -> x18, starting transfers between devices: none -> 28.9 us  [the longest x16 27.3 us: swap(): return lax.ppermute(value, 'ctx', [(i, i ^ step) for i in range(count)])]
    ppermute x0 -> x18, waiting for transfers between devices: none -> 27.1 us  [the longest x16 25.1 us: swap(): return lax.ppermute(value, 'ctx', [(i, i ^ step) for i in range(count)])]
    reshape x16 -> x0, local copies, waits for them, and re-layouts: 23 us -> none  [the longest x8 13.4 us: diagonal_sums(): return jnp.sum(flat.reshape(nfil, height, stride - 1), axis=1)]
    all_gather x1 -> x0, blocking collectives: 22.6 us -> none  [shards(): taps = lax.all_gather(filters, 'ctx', axis=1, tiled=True)]
    all_to_all x4 -> x0, starting transfers between devices: 18.3 us -> none  [the longest x1 7.41 us: shards(): lax.all_to_all(back, 'ctx', split_axis=1, concat_axis=0, tiled=True)]
    slice x17 -> x0, local copies, waits for them, and re-layouts: 13.4 us -> none  [the longest x8 6.85 us: toeplitz(): flat = tiled[:, height - 1:height - 1 + height * (span - 1)]]
  transfers between devices with their start and end apart: 5 -> 18, of which waited for: 3 -> 14; matrix products, arithmetic and copies ran while one was open for 4% -> 1% of each run, Pallas kernels for 0% -> 5%
where the time goes in v1:
time: 72.3 us; the launch traced here: 72 us
  starting transfers between devices  28.9 us (40%)
  waiting for transfers between devices  27.1 us (37%)
  Pallas kernels  10.4 us (14%)
  local copies, waits for them, and re-layouts  4.18 us (6%)
  between operations  0.74 us (1%)
    ppermute x16, starting transfers between devices, swap(): return lax.ppermute(value, 'ctx', [(i, i ^ step) for i in range(count)])  27.3 us
    ppermute x16, waiting for transfers between devices, swap(): return lax.ppermute(value, 'ctx', [(i, i ^ step) for i in range(count)])  25.1 us
    pallas_call x5, Pallas kernels, call(): pl.pallas_call(kernel, out_shape=outs, in_specs=[pl.BlockSpec(memory_spac...  10.4 us
    unnamed x18, local copies, waits for them, and re-layouts  4.18 us
    ppermute x2, waiting for transfers between devices, halves_plan(): lax.ppermute(lags, 'chan', [(i, i ^ step) for i in range(chans)])  2.03 us
    ppermute x2, starting transfers between devices, halves_plan(): lax.ppermute(lags, 'chan', [(i, i ^ step) for i in range(chans)])  1.57 us
  transfers between devices with their start and end apart: 18, of which 14 were waited for; matrix products, arithmetic and copies ran while one was open for 1% of the time, Pallas kernels for 5%

profile of v1, /device:TPU:0, one launch (start us, length us, event | category | flops | bytes accessed | tf_op | source)
XLA Modules:
  0.0 72.0 jit_solution(2080069698082272797)
XLA Ops:
  0.6 1.0 %copy-done = bf16[128,2048]{1,0:T(8,128)(2,1)S(1)} copy-done((bf16[128,2048]{1,0:T(8,128)(2,1)S(1)}, bf16[128,2048]{1,0:T(8,128)(2,1)}, u32[]{:S(2)}) %copy-start) | copy-done | bytes 524312
  1.7 1.0 %copy-done.2 = bf16[128,2048]{1,0:T(8,128)(2,1)S(1)} copy-done((bf16[128,2048]{1,0:T(8,128)(2,1)S(1)}, bf16[128,2048]{1,0:T(8,128)(2,1)}, u32[]{:S(2)}) %copy-start.2) | copy-done | bytes 524312
  2.7 1.0 %copy-done.4 = bf16[128,2048]{1,0:T(8,128)(2,1)S(1)} copy-done((bf16[128,2048]{1,0:T(8,128)(2,1)S(1)}, bf16[128,2048]{1,0:T(8,128)(2,1)}, u32[]{:S(2)}) %copy-start.4) | copy-done | bytes 524312
  3.8 1.0 %copy-done.6 = bf16[128,2048]{1,0:T(8,128)(2,1)S(1)} copy-done((bf16[128,2048]{1,0:T(8,128)(2,1)S(1)}, bf16[128,2048]{1,0:T(8,128)(2,1)}, u32[]{:S(2)}) %copy-start.6) | copy-done | bytes 524312
  4.8 0.9 %shard_map.92 = (bf16[256,512]{1,0:T(8,128)(2,1)S(1)}, bf16[256,512]{1,0:T(8,128)(2,1)S(1)}, bf16[256,512]{1,0:T(8,128)(2,1)S(1)}, bf16[256,512]{1,0:T(8,128)(2,...) custom-call(s32[1]{0:T(128)} %bitcast.me_ref, ...), custom_call_target="tpu_custom_call" | custom-call | flops 201326592 | bytes 3670016 | tf_op jit(solution)/shard_map/pallas_call | solution.py:192
  5.7 4.1 %collective-permute-start.3 = (bf16[128,512]{1,0:T(8,128)(2,1)S(1)}, bf16[128,512]{1,0:T(8,128)(2,1)S(1)}, u32[]{:S(2)}, u32[]{:S(2)}) collective-permute-start(bf16[128,512]{1,0:T(8,128)(2,1)S(1)} %get-tuple-element.27), channel_id=1, source_target_pairs={{0,4},{1,5},{2,6},{3,7},{4,0},{5,1},{6,2},{7,3},{8,12},{9,13},{10,... | collective-permute-start | bytes 393224 | tf_op jit(solution)/shard_map/ppermute | solution.py:188
  9.8 1.3 %collective-permute-start.4 = (bf16[128,512]{1,0:T(8,128)(2,1)S(1)}, bf16[128,512]{1,0:T(8,128)(2,1)S(1)}, u32[]{:S(2)}, u32[]{:S(2)}) collective-permute-start(bf16[128,512]{1,0:T(8,128)(2,1)S(1)} %get-tuple-element.28), channel_id=1, source_target_pairs={{0,5},{1,4},{2,7},{3,6},{4,1},{5,0},{6,3},{7,2},{8,13},{9,12},{10,... | collective-permute-start | bytes 393224 | tf_op jit(solution)/shard_map/ppermute | solution.py:188
  11.4 1.8 %collective-permute-start.1 = (bf16[256,512]{1,0:T(8,128)(2,1)S(1)}, bf16[256,512]{1,0:T(8,128)(2,1)S(1)}, u32[]{:S(2)}, u32[]{:S(2)}) collective-permute-start(bf16[256,512]{1,0:T(8,128)(2,1)S(1)} %get-tuple-element.25), channel_id=1, source_target_pairs={{0,2},{1,3},{2,0},{3,1},{4,6},{5,7},{6,4},{7,5},{8,10},{9,11},{10,... | collective-permute-start | bytes 786440 | tf_op jit(solution)/shard_map/ppermute | solution.py:188
  13.2 1.4 %collective-permute-start.2 = (bf16[256,512]{1,0:T(8,128)(2,1)S(1)}, bf16[256,512]{1,0:T(8,128)(2,1)S(1)}, u32[]{:S(2)}, u32[]{:S(2)}) collective-permute-start(bf16[256,512]{1,0:T(8,128)(2,1)S(1)} %get-tuple-element.26), channel_id=1, source_target_pairs={{0,3},{1,2},{2,1},{3,0},{4,7},{5,6},{6,5},{7,4},{8,11},{9,10},{10,... | collective-permute-start | bytes 786440 | tf_op jit(solution)/shard_map/ppermute | solution.py:188
  14.6 5.2 %collective-permute-done.3.refs_4_ = bf16[128,512]{1,0:T(8,128)(2,1)S(1)} collective-permute-done((bf16[128,512]{1,0:T(8,128)(2,1)S(1)}, bf16[128,512]{1,0:T(8,128)(2,1)S(1)}, u32[]{:S(2)}, u32[]{:S(2)}) %collective-permute-start.3) | collective-permute-done | bytes 131104 | tf_op jit(solution)/shard_map/ppermute | solution.py:188
  19.8 2.9 %collective-permute-start.5 = (bf16[128,512]{1,0:T(8,128)(2,1)S(1)}, bf16[128,512]{1,0:T(8,128)(2,1)S(1)}, u32[]{:S(2)}, u32[]{:S(2)}) collective-permute-start(bf16[128,512]{1,0:T(8,128)(2,1)S(1)} %get-tuple-element.29), channel_id=1, source_target_pairs={{0,6},{1,7},{2,4},{3,5},{4,2},{5,3},{6,0},{7,1},{8,14},{9,15},{10,... | collective-permute-start | bytes 393224 | tf_op jit(solution)/shard_map/ppermute | solution.py:188
  22.8 3.6 %collective-permute-start.6 = (bf16[128,512]{1,0:T(8,128)(2,1)S(1)}, bf16[128,512]{1,0:T(8,128)(2,1)S(1)}, u32[]{:S(2)}, u32[]{:S(2)}) collective-permute-start(bf16[128,512]{1,0:T(8,128)(2,1)S(1)} %get-tuple-element.30), channel_id=1, source_target_pairs={{0,7},{1,6},{2,5},{3,4},{4,3},{5,2},{6,1},{7,0},{8,15},{9,14},{10,... | collective-permute-start | bytes 393224 | tf_op jit(solution)/shard_map/ppermute | solution.py:188
  26.3 6.8 %collective-permute-done.5.refs_6_ = bf16[128,512]{1,0:T(8,128)(2,1)S(1)} collective-permute-done((bf16[128,512]{1,0:T(8,128)(2,1)S(1)}, bf16[128,512]{1,0:T(8,128)(2,1)S(1)}, u32[]{:S(2)}, u32[]{:S(2)}) %collective-permute-start.5) | collective-permute-done | bytes 131104 | tf_op jit(solution)/shard_map/ppermute | solution.py:188
  33.1 2.0 %collective-permute-done.6.refs_7_ = bf16[128,512]{1,0:T(8,128)(2,1)S(1)} collective-permute-done((bf16[128,512]{1,0:T(8,128)(2,1)S(1)}, bf16[128,512]{1,0:T(8,128)(2,1)S(1)}, u32[]{:S(2)}, u32[]{:S(2)}) %collective-permute-start.6) | collective-permute-done | bytes 131104 | tf_op jit(solution)/shard_map/ppermute | solution.py:188
  35.6 3.6 %shard_map.96 = f32[8,1024]{1,0:T(8,128)S(1)} custom-call(s32[1]{0:T(128)} %bitcast.me_ref, bf16[256,512]{1,0:T(8,128)(2,1)S(1)} %get-tuple-element.23.refs_0_, bf16[256,512]{1,0:T(8,128)(2,1)S(1)} %collective-permute-done.refs_1_, bf16[256,512]{1,0:T(8,128)(2,1)S(1)} %collective-permute-done.1.refs_2_, bf16[256,512]{1,0:T(8,128)(2,1)S(1)} %collective-permute-done.2.refs_3_, ...), custom_call_target="tpu_custom_call" | custom-call | flops 2147483648 | bytes 2097152 | tf_op jit(solution)/shard_map/pallas_call | solution.py:192
  39.8 0.6 collective-permute-done.13
  40.4 1.5 %collective-permute-start.14 = (f32[8,1024]{1,0:T(8,128)S(1)}, f32[8,1024]{1,0:T(8,128)S(1)}, u32[]{:S(2)}, u32[]{:S(2)}) collective-permute-start(f32[8,1024]{1,0:T(8,128)S(1)} %add.17), channel_id=1, source_target_pairs={{0,16},{8,24},{16,0},{24,8},{1,17},{9,25},{17,1},{25,9},{2,18},{10... | collective-permute-start | bytes 98312 | tf_op jit(solution)/shard_map/ppermute | solution.py:264
  41.9 1.0 %collective-permute-done.7 = f32[8,128]{1,0:T(8,128)S(1)} collective-permute-done((f32[8,128]{1,0:T(8,128)S(1)}, f32[8,128]{1,0:T(8,128)S(1)}, u32[]{:S(2)}, u32[]{:S(2)}) %collective-permute-start.7) | collective-permute-done | bytes 4128 | tf_op jit(solution)/shard_map/ppermute | solution.py:188
  42.9 1.4 %collective-permute-done.14 = f32[8,1024]{1,0:T(8,128)S(1)} collective-permute-done((f32[8,1024]{1,0:T(8,128)S(1)}, f32[8,1024]{1,0:T(8,128)S(1)}, u32[]{:S(2)}, u32[]{:S(2)}) %collective-permute-start.14) | collective-permute-done | bytes 32800 | tf_op jit(solution)/shard_map/ppermute | solution.py:264
  44.3 3.9 %collective-permute-start.15 = (f32[8,512]{1,0:T(8,128)S(1)}, f32[8,512]{1,0:T(8,128)S(1)}, u32[]{:S(2)}, u32[]{:S(2)}) collective-permute-start(f32[8,512]{1,0:T(8,128)S(1)} %slice_select_fusion), channel_id=1, source_target_pairs={{0,4},{1,5},{2,6},{3,7},{4,0},{5,1},{6,2},{7,3},{8,12},{9,13},{10,... | collective-permute-start | bytes 49160 | tf_op jit(solution)/shard_map/ppermute | solution.py:188
  48.2 1.5 %collective-permute-start.9 = (f32[32,128]{1,0:T(8,128)S(1)}, f32[32,128]{1,0:T(8,128)S(1)}, u32[]{:S(2)}, u32[]{:S(2)}) collective-permute-start(f32[32,128]{1,0:T(8,128)S(1)} %pad_maximum_fusion.1), channel_id=1, source_target_pairs={{0,4},{1,5},{2,6},{3,7},{4,0},{5,1},{6,2},{7,3},{8,12},{9,13},{10,... | collective-permute-start | bytes 49160 | tf_op jit(solution)/shard_map/ppermute | solution.py:188
  49.9 1.9 %collective-permute-start.16 = (f32[8,256]{1,0:T(8,128)S(1)}, f32[8,256]{1,0:T(8,128)S(1)}, u32[]{:S(2)}, u32[]{:S(2)}) collective-permute-start(f32[8,256]{1,0:T(8,128)S(1)} %slice_select_fusion.1), channel_id=1, source_target_pairs={{0,2},{1,3},{2,0},{3,1},{4,6},{5,7},{6,4},{7,5},{8,10},{9,11},{10,... | collective-permute-start | bytes 24584 | tf_op jit(solution)/shard_map/ppermute | solution.py:188
  51.8 1.0 %collective-permute-done.9 = f32[32,128]{1,0:T(8,128)S(1)} collective-permute-done((f32[32,128]{1,0:T(8,128)S(1)}, f32[32,128]{1,0:T(8,128)S(1)}, u32[]{:S(2)}, u32[]{:S(2)}) %collective-permute-start.9) | collective-permute-done | bytes 16416 | tf_op jit(solution)/shard_map/ppermute | solution.py:188
  52.8 0.7 shard_map.93
  53.6 0.6 collective-permute-start.17
  54.2 3.1 %shard_map.94 = (bf16[256,512]{1,0:T(8,128)(2,1)S(1)}, bf16[256,512]{1,0:T(8,128)(2,1)S(1)}, bf16[256,512]{1,0:T(8,128)(2,1)S(1)}, bf16[256,512]{1,0:T(8,128)(2,1)S(1)}) custom-call(s32[1]{0:T(128)} %bitcast.me_ref, bf16[256,512]{1,0:T(8,128)(2,1)S(1)} %get-tuple-element.23.refs_0_, bf16[256,512]{1,0:T(8,128)(2,1)S(1)} %collective-permute-done.refs_1_, ...), custom_call_target="tpu_custom_call" | custom-call | flops 3221225472 | bytes 2097152 | tf_op jit(solution)/shard_map/pallas_call | solution.py:192
  57.4 1.6 %collective-permute-start.10 = (bf16[256,512]{1,0:T(8,128)(2,1)S(1)}, bf16[256,512]{1,0:T(8,128)(2,1)S(1)}, u32[]{:S(2)}, u32[]{:S(2)}) collective-permute-start(bf16[256,512]{1,0:T(8,128)(2,1)S(1)} %get-tuple-element.34), channel_id=1, source_target_pairs={{0,1},{1,0},{2,3},{3,2},{4,5},{5,4},{6,7},{7,6},{8,9},{9,8},{10,11... | collective-permute-start | bytes 786440 | tf_op jit(solution)/shard_map/ppermute | solution.py:188
  58.9 1.9 %collective-permute-start.11 = (bf16[256,512]{1,0:T(8,128)(2,1)S(1)}, bf16[256,512]{1,0:T(8,128)(2,1)S(1)}, u32[]{:S(2)}, u32[]{:S(2)}) collective-permute-start(bf16[256,512]{1,0:T(8,128)(2,1)S(1)} %get-tuple-element.35), channel_id=1, source_target_pairs={{0,2},{1,3},{2,0},{3,1},{4,6},{5,7},{6,4},{7,5},{8,10},{9,11},{10,... | collective-permute-start | bytes 786440 | tf_op jit(solution)/shard_map/ppermute | solution.py:188
  60.9 0.6 slice_multiply_fusion
  61.5 5.1 %collective-permute-done.10.refs_1_ = bf16[256,512]{1,0:T(8,128)(2,1)S(1)} collective-permute-done((bf16[256,512]{1,0:T(8,128)(2,1)S(1)}, bf16[256,512]{1,0:T(8,128)(2,1)S(1)}, u32[]{:S(2)}, u32[]{:S(2)}) %collective-permute-start.10) | collective-permute-done | bytes 262176 | tf_op jit(solution)/shard_map/ppermute | solution.py:188
  66.9 2.9 %collective-permute-done.12.refs_3_ = bf16[256,512]{1,0:T(8,128)(2,1)S(1)} collective-permute-done((bf16[256,512]{1,0:T(8,128)(2,1)S(1)}, bf16[256,512]{1,0:T(8,128)(2,1)S(1)}, u32[]{:S(2)}, u32[]{:S(2)}) %collective-permute-start.12) | collective-permute-done | bytes 262176 | tf_op jit(solution)/shard_map/ppermute | solution.py:188
  69.9 2.2 %shard_map.95 = (bf16[128,2048]{1,0:T(8,128)(2,1)}, bf16[128,2048]{1,0:T(8,128)(2,1)}, bf16[128,2048]{1,0:T(8,128)(2,1)}, bf16[128,2048]{1,0:T(8,128)(2,1)}) custom-call(s32[1]{0:T(128)} %bitcast.me_ref, bf16[128,2048]{1,0:T(8,128)(2,1)S(1)} %copy-done.1, bf16[128,2048]{1,0:T(8,128)(2,1)S(1)} %copy-done.3, bf16[128,2048]{1,0:T(8,128)(2,1)S(1)} %copy-done.5, ...), custom_call_target="tpu_custom_call" | custom-call | flops 134217728 | bytes 5242880 | tf_op jit(solution)/shard_map/pallas_call | solution.py:192
  (40 shorter events, 2.2 us)
Async XLA Ops:
  0.6 1.0 %copy-start = (bf16[128,2048]{1,0:T(8,128)(2,1)S(1)}, bf16[128,2048]{1,0:T(8,128)(2,1)}, u32[]{:S(2)}) copy-start(bf16[128,2048]{1,0:T(8,128)(2,1)} %q_ref.3) | copy-start | bytes 1572868
  1.7 1.0 %copy-start.2 = (bf16[128,2048]{1,0:T(8,128)(2,1)S(1)}, bf16[128,2048]{1,0:T(8,128)(2,1)}, u32[]{:S(2)}) copy-start(bf16[128,2048]{1,0:T(8,128)(2,1)} %k_ref.3) | copy-start | bytes 1572868
  2.7 1.0 %copy-start.4 = (bf16[128,2048]{1,0:T(8,128)(2,1)S(1)}, bf16[128,2048]{1,0:T(8,128)(2,1)}, u32[]{:S(2)}) copy-start(bf16[128,2048]{1,0:T(8,128)(2,1)} %v_ref.3) | copy-start | bytes 1572868
  3.8 1.0 %copy-start.6 = (bf16[128,2048]{1,0:T(8,128)(2,1)S(1)}, bf16[128,2048]{1,0:T(8,128)(2,1)}, u32[]{:S(2)}) copy-start(bf16[128,2048]{1,0:T(8,128)(2,1)} %g_ref.3) | copy-start | bytes 1572868
  5.7 14.1 %collective-permute-start.3 = (bf16[128,512]{1,0:T(8,128)(2,1)S(1)}, bf16[128,512]{1,0:T(8,128)(2,1)S(1)}, u32[]{:S(2)}, u32[]{:S(2)}) collective-permute-start(bf16[128,512]{1,0:T(8,128)(2,1)S(1)} %get-tuple-element.27), channel_id=1, source_target_pairs={{0,4},{1,5},{2,6},{3,7},{4,0},{5,1},{6,2},{7,3},{8,12},{9,13},{10,... | collective-permute-start | bytes 393224 | tf_op jit(solution)/shard_map/ppermute | solution.py:188
  9.8 12.9 %collective-permute-start.4 = (bf16[128,512]{1,0:T(8,128)(2,1)S(1)}, bf16[128,512]{1,0:T(8,128)(2,1)S(1)}, u32[]{:S(2)}, u32[]{:S(2)}) collective-permute-start(bf16[128,512]{1,0:T(8,128)(2,1)S(1)} %get-tuple-element.28), channel_id=1, source_target_pairs={{0,5},{1,4},{2,7},{3,6},{4,1},{5,0},{6,3},{7,2},{8,13},{9,12},{10,... | collective-permute-start | bytes 393224 | tf_op jit(solution)/shard_map/ppermute | solution.py:188
  11.1 24.0 %collective-permute-start = (bf16[256,512]{1,0:T(8,128)(2,1)S(1)}, bf16[256,512]{1,0:T(8,128)(2,1)S(1)}, u32[]{:S(2)}, u32[]{:S(2)}) collective-permute-start(bf16[256,512]{1,0:T(8,128)(2,1)S(1)} %get-tuple-element.24), channel_id=1, source_target_pairs={{0,1},{1,0},{2,3},{3,2},{4,5},{5,4},{6,7},{7,6},{8,9},{9,8},{10,11... | collective-permute-start | bytes 786440 | tf_op jit(solution)/shard_map/ppermute | solution.py:188
  11.4 23.8 %collective-permute-start.1 = (bf16[256,512]{1,0:T(8,128)(2,1)S(1)}, bf16[256,512]{1,0:T(8,128)(2,1)S(1)}, u32[]{:S(2)}, u32[]{:S(2)}) collective-permute-start(bf16[256,512]{1,0:T(8,128)(2,1)S(1)} %get-tuple-element.25), channel_id=1, source_target_pairs={{0,2},{1,3},{2,0},{3,1},{4,6},{5,7},{6,4},{7,5},{8,10},{9,11},{10,... | collective-permute-start | bytes 786440 | tf_op jit(solution)/shard_map/ppermute | solution.py:188
  13.2 22.3 %collective-permute-start.2 = (bf16[256,512]{1,0:T(8,128)(2,1)S(1)}, bf16[256,512]{1,0:T(8,128)(2,1)S(1)}, u32[]{:S(2)}, u32[]{:S(2)}) collective-permute-start(bf16[256,512]{1,0:T(8,128)(2,1)S(1)} %get-tuple-element.26), channel_id=1, source_target_pairs={{0,3},{1,2},{2,1},{3,0},{4,7},{5,6},{6,5},{7,4},{8,11},{9,10},{10,... | collective-permute-start | bytes 786440 | tf_op jit(solution)/shard_map/ppermute | solution.py:188
  19.8 13.3 %collective-permute-start.5 = (bf16[128,512]{1,0:T(8,128)(2,1)S(1)}, bf16[128,512]{1,0:T(8,128)(2,1)S(1)}, u32[]{:S(2)}, u32[]{:S(2)}) collective-permute-start(bf16[128,512]{1,0:T(8,128)(2,1)S(1)} %get-tuple-element.29), channel_id=1, source_target_pairs={{0,6},{1,7},{2,4},{3,5},{4,2},{5,3},{6,0},{7,1},{8,14},{9,15},{10,... | collective-permute-start | bytes 393224 | tf_op jit(solution)/shard_map/ppermute | solution.py:188
  22.8 12.4 %collective-permute-start.6 = (bf16[128,512]{1,0:T(8,128)(2,1)S(1)}, bf16[128,512]{1,0:T(8,128)(2,1)S(1)}, u32[]{:S(2)}, u32[]{:S(2)}) collective-permute-start(bf16[128,512]{1,0:T(8,128)(2,1)S(1)} %get-tuple-element.30), channel_id=1, source_target_pairs={{0,7},{1,6},{2,5},{3,4},{4,3},{5,2},{6,1},{7,0},{8,15},{9,14},{10,... | collective-permute-start | bytes 393224 | tf_op jit(solution)/shard_map/ppermute | solution.py:188
  35.5 3.7 %copy-start.8 = (bf16[4,128]{1,0:T(4,128)(2,1)S(1)}, bf16[4,128]{1,0:T(4,128)(2,1)}, u32[]{:S(2)}) copy-start(bf16[4,128]{1,0:T(4,128)(2,1)} %param.8) | copy-start | bytes 3076
  39.1 1.3 %collective-permute-start.13 = (f32[8,1024]{1,0:T(8,128)S(1)}, f32[8,1024]{1,0:T(8,128)S(1)}, u32[]{:S(2)}, u32[]{:S(2)}) collective-permute-start(f32[8,1024]{1,0:T(8,128)S(1)} %shard_map.96), channel_id=1, source_target_pairs={{0,8},{8,0},{16,24},{24,16},{1,9},{9,1},{17,25},{25,17},{2,10},{10... | collective-permute-start | bytes 98312 | tf_op jit(solution)/shard_map/ppermute | solution.py:264
  39.2 3.7 %collective-permute-start.7 = (f32[8,128]{1,0:T(8,128)S(1)}, f32[8,128]{1,0:T(8,128)S(1)}, u32[]{:S(2)}, u32[]{:S(2)}) collective-permute-start(f32[8,128]{1,0:T(8,128)S(1)} %pad_convert_fusion), channel_id=1, source_target_pairs={{0,1},{1,0},{2,3},{3,2},{4,5},{5,4},{6,7},{7,6},{8,9},{9,8},{10,11... | collective-permute-start | bytes 12296 | tf_op jit(solution)/shard_map/ppermute | solution.py:188
  40.4 3.9 %collective-permute-start.14 = (f32[8,1024]{1,0:T(8,128)S(1)}, f32[8,1024]{1,0:T(8,128)S(1)}, u32[]{:S(2)}, u32[]{:S(2)}) collective-permute-start(f32[8,1024]{1,0:T(8,128)S(1)} %add.17), channel_id=1, source_target_pairs={{0,16},{8,24},{16,0},{24,8},{1,17},{9,25},{17,1},{25,9},{2,18},{10... | collective-permute-start | bytes 98312 | tf_op jit(solution)/shard_map/ppermute | solution.py:264
  42.9 5.3 %collective-permute-start.8 = (f32[16,128]{1,0:T(8,128)S(1)}, f32[16,128]{1,0:T(8,128)S(1)}, u32[]{:S(2)}, u32[]{:S(2)}) collective-permute-start(f32[16,128]{1,0:T(8,128)S(1)} %pad_maximum_fusion.2), channel_id=1, source_target_pairs={{0,2},{1,3},{2,0},{3,1},{4,6},{5,7},{6,4},{7,5},{8,10},{9,11},{10,... | collective-permute-start | bytes 24584 | tf_op jit(solution)/shard_map/ppermute | solution.py:188
  44.3 5.6 %collective-permute-start.15 = (f32[8,512]{1,0:T(8,128)S(1)}, f32[8,512]{1,0:T(8,128)S(1)}, u32[]{:S(2)}, u32[]{:S(2)}) collective-permute-start(f32[8,512]{1,0:T(8,128)S(1)} %slice_select_fusion), channel_id=1, source_target_pairs={{0,4},{1,5},{2,6},{3,7},{4,0},{5,1},{6,2},{7,3},{8,12},{9,13},{10,... | collective-permute-start | bytes 49160 | tf_op jit(solution)/shard_map/ppermute | solution.py:188
  48.2 4.6 %collective-permute-start.9 = (f32[32,128]{1,0:T(8,128)S(1)}, f32[32,128]{1,0:T(8,128)S(1)}, u32[]{:S(2)}, u32[]{:S(2)}) collective-permute-start(f32[32,128]{1,0:T(8,128)S(1)} %pad_maximum_fusion.1), channel_id=1, source_target_pairs={{0,4},{1,5},{2,6},{3,7},{4,0},{5,1},{6,2},{7,3},{8,12},{9,13},{10,... | collective-permute-start | bytes 49160 | tf_op jit(solution)/shard_map/ppermute | solution.py:188
  49.9 3.7 %collective-permute-start.16 = (f32[8,256]{1,0:T(8,128)S(1)}, f32[8,256]{1,0:T(8,128)S(1)}, u32[]{:S(2)}, u32[]{:S(2)}) collective-permute-start(f32[8,256]{1,0:T(8,128)S(1)} %slice_select_fusion.1), channel_id=1, source_target_pairs={{0,2},{1,3},{2,0},{3,1},{4,6},{5,7},{6,4},{7,5},{8,10},{9,11},{10,... | collective-permute-start | bytes 24584 | tf_op jit(solution)/shard_map/ppermute | solution.py:188
  53.6 7.3 %collective-permute-start.17 = (f32[8,128]{1,0:T(8,128)S(1)}, f32[8,128]{1,0:T(8,128)S(1)}, u32[]{:S(2)}, u32[]{:S(2)}) collective-permute-start(f32[8,128]{1,0:T(8,128)S(1)} %slice_select_fusion.2), channel_id=1, source_target_pairs={{0,1},{1,0},{2,3},{3,2},{4,5},{5,4},{6,7},{7,6},{8,9},{9,8},{10,11... | collective-permute-start | bytes 12296 | tf_op jit(solution)/shard_map/ppermute | solution.py:188
  54.2 15.6 %copy-start.1 = (bf16[128,2048]{1,0:T(8,128)(2,1)S(1)}, bf16[128,2048]{1,0:T(8,128)(2,1)}, u32[]{:S(2)}) copy-start(bf16[128,2048]{1,0:T(8,128)(2,1)} %q_ref.3) | copy-start | bytes 1572868
  54.2 15.6 %copy-start.3 = (bf16[128,2048]{1,0:T(8,128)(2,1)S(1)}, bf16[128,2048]{1,0:T(8,128)(2,1)}, u32[]{:S(2)}) copy-start(bf16[128,2048]{1,0:T(8,128)(2,1)} %k_ref.3) | copy-start | bytes 1572868
  54.2 15.6 %copy-start.5 = (bf16[128,2048]{1,0:T(8,128)(2,1)S(1)}, bf16[128,2048]{1,0:T(8,128)(2,1)}, u32[]{:S(2)}) copy-start(bf16[128,2048]{1,0:T(8,128)(2,1)} %v_ref.3) | copy-start | bytes 1572868
  54.2 15.6 %copy-start.7 = (bf16[128,2048]{1,0:T(8,128)(2,1)S(1)}, bf16[128,2048]{1,0:T(8,128)(2,1)}, u32[]{:S(2)}) copy-start(bf16[128,2048]{1,0:T(8,128)(2,1)} %g_ref.3) | copy-start | bytes 1572868
  57.4 9.2 %collective-permute-start.10 = (bf16[256,512]{1,0:T(8,128)(2,1)S(1)}, bf16[256,512]{1,0:T(8,128)(2,1)S(1)}, u32[]{:S(2)}, u32[]{:S(2)}) collective-permute-start(bf16[256,512]{1,0:T(8,128)(2,1)S(1)} %get-tuple-element.34), channel_id=1, source_target_pairs={{0,1},{1,0},{2,3},{3,2},{4,5},{5,4},{6,7},{7,6},{8,9},{9,8},{10,11... | collective-permute-start | bytes 786440 | tf_op jit(solution)/shard_map/ppermute | solution.py:188
  58.9 8.0 %collective-permute-start.11 = (bf16[256,512]{1,0:T(8,128)(2,1)S(1)}, bf16[256,512]{1,0:T(8,128)(2,1)S(1)}, u32[]{:S(2)}, u32[]{:S(2)}) collective-permute-start(bf16[256,512]{1,0:T(8,128)(2,1)S(1)} %get-tuple-element.35), channel_id=1, source_target_pairs={{0,2},{1,3},{2,0},{3,1},{4,6},{5,7},{6,4},{7,5},{8,10},{9,11},{10,... | collective-permute-start | bytes 786440 | tf_op jit(solution)/shard_map/ppermute | solution.py:188
  60.8 9.0 %collective-permute-start.12 = (bf16[256,512]{1,0:T(8,128)(2,1)S(1)}, bf16[256,512]{1,0:T(8,128)(2,1)S(1)}, u32[]{:S(2)}, u32[]{:S(2)}) collective-permute-start(bf16[256,512]{1,0:T(8,128)(2,1)S(1)} %get-tuple-element.36), channel_id=1, source_target_pairs={{0,3},{1,2},{2,1},{3,0},{4,7},{5,6},{6,5},{7,4},{8,11},{9,10},{10,... | collective-permute-start | bytes 786440 | tf_op jit(solution)/shard_map/ppermute | solution.py:188

commit v2 on v0

--- a/solution.py
+++ b/solution.py
@@ -1,10 +1,430 @@
+import functools
+
 import jax
 import jax.numpy as jnp
 from jax import lax
+from jax.experimental import pallas as pl
+from jax.experimental.pallas import tpu as pltpu
 from jax.sharding import PartitionSpec as P
 
 D = 8192
 NFILT = 4
+LANES = 128
+GRANT = 24 * 2**20
+
+
+def exchange(size, reverse, dtype):
+    row = lax.broadcasted_iota(jnp.int32, (size, size), 0)
+    col = lax.broadcasted_iota(jnp.int32, (size, size), 1)
+    target = jnp.where(reverse, size - 1 - row, row)
+    return jnp.where(col == target, 1.0, 0.0).astype(jnp.float32).astype(dtype)
+
+
+def exact_rows(matrix, values):
+    return jnp.dot(matrix, values, preferred_element_type=jnp.float32).astype(jnp.bfloat16)
+
+
+def gate_kernel(half, slim, me_ref, q_ref, k_ref, v_ref, g_ref, *refs):
+    outs, (pair_ref, held, sems) = refs[:-3], refs[-3:]
+    rows = q_ref.shape[0]
+    me = me_ref[0]
+    upper = me >= half
+    copies = []
+    for step in range(half):
+        part = (me ^ step) & (half - 1)
+        lanes = pl.ds(pl.multiple_of(part * slim, LANES), slim)
+        copies.append([])
+        for index, ref in enumerate((q_ref, k_ref, v_ref, g_ref)):
+            copy = pltpu.make_async_copy(
+                ref.at[:, lanes], held.at[step, index], sems.at[step, index]
+            )
+            copy.start()
+            copies[step].append(copy)
+    turn_other = exchange(rows, jnp.logical_not(upper), jnp.bfloat16)
+    for step in range(half):
+        for copy in copies[step]:
+            copy.wait()
+        q, k, v, g = [held[step, index].astype(jnp.float32) for index in range(4)]
+        gated = (k * v).astype(jnp.bfloat16)
+        back = (g * q).astype(jnp.bfloat16)
+        second = jnp.where(upper, back, gated)
+        pair_ref[step, 0] = jnp.where(upper, gated, back)
+        pair_ref[step, 1] = second
+        outs[step][...] = exact_rows(turn_other, second)
+
+
+def bundle_kernel(half, me_ref, mine_ref, other_ref, pair_ref, *outs):
+    rows = pair_ref.shape[2]
+    turn = exchange(rows, me_ref[0] >= half, jnp.bfloat16)
+    both = jnp.concatenate([mine_ref[...], other_ref[...]], axis=0).astype(jnp.bfloat16)
+    for step in range(half):
+        outs[step][0:rows, :] = exact_rows(turn, pair_ref[step, 0])
+        outs[step][rows : 2 * rows, :] = exact_rows(turn, pair_ref[step, 1])
+        outs[step][2 * rows :, :] = jnp.zeros((16, outs[step].shape[1]), jnp.bfloat16)
+        outs[step][2 * rows :, 0:LANES] = both
+
+
+def fill_bands(half, me, arrived, near_ref, far_ref, line):
+    nfil, size, total = near_ref.shape
+    for step in range(half):
+        both = arrived[step][arrived[step].shape[0] - 16 :, 0:LANES].astype(jnp.float32)
+        for index, source in enumerate((me ^ step, me ^ step ^ half)):
+            place = pl.multiple_of(source * LANES, LANES)
+            line[:, pl.ds(place, LANES)] = both[8 * index : 8 * index + 8, :]
+    row = lax.broadcasted_iota(jnp.int32, (size, total), 0)
+    col = lax.broadcasted_iota(jnp.int32, (size, total), 1)
+    reach = far_ref.shape[2] // size
+    for index in range(nfil):
+        spread = jnp.broadcast_to(line[index : index + 1, :], (size, total))
+        rolled = pltpu.roll(spread, 0, 1, stride=1, stride_axis=0)
+        band = jnp.where(col >= row, rolled, 0.0)
+        near_ref[index] = band.astype(jnp.bfloat16)
+        for block in range(reach):
+            piece = band[:, (reach - 1 - block) * size : (reach - block) * size]
+            far_ref[index, :, block * size : (block + 1) * size] = piece.T.astype(jnp.bfloat16)
+
+
+def slot_of(half, me, step):
+    return ((me ^ step) & (half - 1)) ^ jnp.where(me >= half, half - 1, 0)
+
+
+def rows_at(slot, rows):
+    return pl.ds(pl.multiple_of(slot * rows, rows), rows)
+
+
+def add_lags_of(first, flipped, mask, start, width, acc):
+    near = lax.dot_general(
+        flipped, first * mask, (((1,), (1,)), ((), ())), preferred_element_type=jnp.float32
+    )
+    rows, reach = near.shape
+    pieces = [near, jnp.zeros((rows, width - start - reach), jnp.float32)]
+    if start:
+        pieces = [jnp.zeros((rows, start), jnp.float32)] + pieces
+    return acc + jnp.concatenate(pieces, axis=1)
+
+
+def lag_sums(acc):
+    rows, width = acc.shape
+    rolled = pltpu.roll(acc, 0, 1, stride=1, stride_axis=0)
+    sums = jnp.sum(rolled, axis=0, keepdims=True)
+    sums = jnp.broadcast_to(sums, (8, width))
+    return pltpu.roll(sums, width - rows + 1, 1)[0:1, 0 : width - rows]
+
+
+def lane_mask(width, nfil, index):
+    lane = lax.broadcasted_iota(jnp.int32, (1, width), 1)
+    return jnp.where(lane % nfil == index, 1.0, 0.0).astype(jnp.bfloat16)
+
+
+def second_kernel(half, me_ref, *refs):
+    arrived = refs[:half]
+    outs = refs[half : 2 * half]
+    near_ref, far_ref, line, second_ref, result_ref = refs[2 * half :]
+    nfil, size, total = near_ref.shape
+    own, width = second_ref.shape
+    rows = own // half
+    me = me_ref[0]
+    fill_bands(half, me, arrived, near_ref, far_ref, line)
+    for step in range(half):
+        where = rows_at(slot_of(half, me, step), rows)
+        second_ref[where, :] = arrived[step][rows : 2 * rows, :]
+    masks = [lane_mask(width, nfil, index) for index in range(nfil)]
+    for top in range(0, own, size):
+        acc = jnp.zeros((size, width), jnp.float32)
+        for index in range(nfil):
+            acc += jnp.dot(
+                far_ref[index, :, own - size - top : own],
+                second_ref[0 : top + size, :] * masks[index],
+                preferred_element_type=jnp.float32,
+            )
+        result_ref[top : top + size, :] = acc.astype(jnp.bfloat16)
+    for step in range(half):
+        outs[step][...] = result_ref[rows_at(slot_of(half, me, step), rows), :]
+
+
+def inner_kernel(half, me_ref, *refs):
+    arrived = refs[:half]
+    near_ref, part_ref, flip_ref, lag_ref, first_ref = refs[half:]
+    nfil, size, total = near_ref.shape
+    own, width = first_ref.shape
+    rows = own // half
+    me = me_ref[0]
+    turn = exchange(rows, True, jnp.bfloat16)
+    for step in range(half):
+        where = rows_at(slot_of(half, me, step), rows)
+        first_ref[where, :] = arrived[step][0:rows, :]
+        flip_ref[where, :] = exact_rows(turn, arrived[step][rows : 2 * rows, :])
+    masks = [lane_mask(width, nfil, index) for index in range(nfil)]
+    for top in range(0, own, size):
+        acc = jnp.zeros((size, width), jnp.float32)
+        for index in range(nfil):
+            acc += jnp.dot(
+                near_ref[index, :, 0 : own - top],
+                first_ref[top:own, :] * masks[index],
+                preferred_element_type=jnp.float32,
+            )
+        part_ref[top : top + size, :] = acc
+    lag_ref[...] = jnp.zeros((8, total), jnp.float32)
+    for index in range(nfil):
+        acc = jnp.zeros((rows, own + rows), jnp.float32)
+        for start in range(0, own, rows):
+            acc = add_lags_of(
+                first_ref[start:own, :],
+                flip_ref[start : start + rows, :],
+                masks[index],
+                0,
+                own + rows,
+                acc,
+            )
+        lag_ref[index : index + 1, 0:own] = lag_sums(acc)
+
+
+def lag_kernel(half, me_ref, *refs):
+    arrived = refs[:half]
+    flip_ref, lag_ref, out_ref, first_ref = refs[half:]
+    nfil, total = NFILT, lag_ref.shape[1]
+    own, width = flip_ref.shape
+    rows = own // half
+    me = me_ref[0]
+    share = width // 2
+    lanes = pl.ds(pl.multiple_of(jnp.where(me >= half, share, 0), LANES), share)
+    for step in range(half):
+        where = rows_at(slot_of(half, me, step), rows)
+        first_ref[where, :] = arrived[step][:, lanes]
+    out_ref[...] = lag_ref[...]
+    for index in range(nfil):
+        mask = lane_mask(share, nfil, index)
+        acc = jnp.zeros((rows, total + rows), jnp.float32)
+        for start in range(0, own, rows):
+            acc = add_lags_of(
+                first_ref[...],
+                flip_ref[start : start + rows, lanes],
+                mask,
+                own - start,
+                total + rows,
+                acc,
+            )
+        out_ref[index : index + 1, :] += lag_sums(acc)
+
+
+def attach_kernel(half, me_ref, lag_ref, *refs):
+    outs, (held, sems) = refs[half : 2 * half], refs[2 * half :]
+    rows = outs[0].shape[0] - 16
+    nfil = NFILT
+    me = me_ref[0]
+    copies = []
+    for step in range(half):
+        pieces = []
+        for target in (me ^ step, me ^ step ^ half):
+            place = pl.multiple_of(target * LANES, LANES)
+            pieces.append(lag_ref[0:nfil, pl.ds(place, LANES)])
+        both = jnp.concatenate(pieces, axis=0)
+        high = both.astype(jnp.bfloat16).astype(jnp.float32)
+        rest = (both - high).astype(jnp.bfloat16).astype(jnp.float32)
+        held[step] = jnp.zeros(held.shape[1:], jnp.bfloat16)
+        held[step, :, 0:LANES] = jnp.concatenate([high, rest], axis=0).astype(jnp.bfloat16)
+        copy = pltpu.make_async_copy(held.at[step], outs[step].at[rows : rows + 16], sems.at[step])
+        copy.start()
+        copies.append(copy)
+    for copy in copies:
+        copy.wait()
+
+
+def outer_kernel(half, me_ref, *refs):
+    arrived = refs[:half]
+    near_ref, part_ref = refs[half : half + 2]
+    outs = refs[half + 2 : 2 * half + 2]
+    first_ref, result_ref = refs[2 * half + 2 :]
+    nfil, size, total = near_ref.shape
+    own, width = part_ref.shape
+    rows = own // half
+    me = me_ref[0]
+    for step in range(half):
+        first_ref[rows_at(slot_of(half, me, step), rows), :] = arrived[step][...]
+    for top in range(0, own, size):
+        acc = part_ref[top : top + size, :]
+        for index in range(nfil):
+            acc += jnp.dot(
+                near_ref[index, :, own - top : total - top],
+                first_ref[...] * lane_mask(width, nfil, index),
+                preferred_element_type=jnp.float32,
+            )
+        result_ref[top : top + size, :] = acc.astype(jnp.bfloat16)
+    for step in range(half):
+        outs[step][0:rows, :] = result_ref[rows_at(slot_of(half, me, step), rows), :]
+
+
+def final_kernel(half, slim, me_ref, q_ref, k_ref, v_ref, g_ref, *refs):
+    firsts, seconds = refs[:half], refs[half : 2 * half]
+    outs = refs[2 * half : 2 * half + 4]
+    held, sems = refs[2 * half + 4 :]
+    rows = q_ref.shape[0]
+    me = me_ref[0]
+    upper = me >= half
+    turn = exchange(rows, upper, jnp.bfloat16)
+    copies = []
+    for step in range(half):
+        part = (me ^ step) & (half - 1)
+        lanes = pl.ds(pl.multiple_of(part * slim, LANES), slim)
+        first = jnp.dot(turn, firsts[step][0:rows, :], preferred_element_type=jnp.float32)
+        second = jnp.dot(turn, seconds[step][...], preferred_element_type=jnp.float32)
+        mixed = jnp.where(upper, first, second)
+        grad = jnp.where(upper, second, first)
+        for index, (ref, value) in enumerate(
+            ((q_ref, mixed), (g_ref, mixed), (v_ref, grad), (k_ref, grad))
+        ):
+            held[step, index] = (ref[:, lanes].astype(jnp.float32) * value).astype(jnp.bfloat16)
+            copy = pltpu.make_async_copy(
+                held.at[step, index], outs[index].at[:, lanes], sems.at[step, index]
+            )
+            copy.start()
+            copies.append(copy)
+    for copy in copies:
+        copy.wait()
+
+
+def swap(value, step, count):
+    return lax.ppermute(value, "ctx", [(i, i ^ step) for i in range(count)])
+
+
+def after(value, *earlier):
+    return lax.optimization_barrier((value, *earlier))
+
+
+def call(kernel, outs, scratch, flops, nbytes, *args, far=0, far_out=False, alias=0):
+    near_spec, far_spec = pl.BlockSpec(memory_space=pltpu.VMEM), pl.BlockSpec(memory_space=pl.ANY)
+    near = len(args) - 1 - far - alias
+    return pl.pallas_call(
+        kernel,
+        out_shape=outs,
+        in_specs=[pl.BlockSpec(memory_space=pltpu.SMEM)]
+        + [far_spec] * far
+        + [near_spec] * near
+        + [far_spec] * alias,
+        out_specs=[far_spec if far_out else near_spec] * len(outs),
+        scratch_shapes=scratch,
+        input_output_aliases={len(args) - alias + k: k for k in range(alias)},
+        compiler_params=pltpu.CompilerParams(vmem_limit_bytes=GRANT),
+        cost_estimate=pl.CostEstimate(flops=flops, bytes_accessed=nbytes, transcendentals=0),
+    )(*args)
+
+
+def halves_plan(count, chans, queries, keys, values, filters, cotangent):
+    rows, width = queries.shape
+    nfil = filters.shape[0]
+    half = count // 2
+    slim = width // half
+    total = count * rows
+    own = half * rows
+    size = min(256, own)
+    low = jnp.bfloat16
+    shape = jax.ShapeDtypeStruct
+    me = lax.axis_index("ctx")
+    where = me.astype(jnp.int32).reshape(1)
+
+    taps = jnp.pad(filters.astype(jnp.float32), ((0, 8 - nfil), (0, 0)))
+    other_taps = swap(taps, half, count)
+    branches = [
+        pltpu.with_memory_space_constraint(x, pltpu.HBM)
+        for x in (queries, keys, values, cotangent)
+    ]
+    *sent, pair = call(
+        functools.partial(gate_kernel, half, slim),
+        [shape((rows, slim), low)] * half + [shape((half, 2, rows, slim), low)],
+        [pltpu.VMEM((half, 4, rows, slim), low), pltpu.SemaphoreType.DMA((half, 4))],
+        2 * rows * rows * width,
+        14 * rows * width,
+        where, *branches, far=4,
+    )
+    inner = call(
+        functools.partial(bundle_kernel, half),
+        [shape((2 * rows + 16, slim), low)] * half,
+        [],
+        4 * rows * rows * width,
+        8 * rows * width,
+        where, taps, other_taps, pair,
+    )
+    inner = [inner[0]] + [swap(inner[k], k, count) for k in range(1, half)]
+    outer = list(sent)
+    for k in range(half):
+        if k >= half - 2:
+            outer[k], inner[k - 1] = after(outer[k], inner[k - 1])
+        outer[k] = swap(outer[k], half + k, count)
+
+    *second, near = call(
+        functools.partial(second_kernel, half),
+        [shape((rows, slim), low)] * half + [shape((nfil, size, total), low)],
+        [
+            pltpu.VMEM((nfil, size, own), low),
+            pltpu.VMEM((8, total), jnp.float32),
+            pltpu.VMEM((own, slim), low),
+            pltpu.VMEM((own, slim), low),
+        ],
+        2 * nfil * own * slim * own,
+        8 * own * slim,
+        where, *inner,
+    )
+    second = [second[0]] + [swap(second[k], k, count) for k in range(1, half)]
+    part, flipped, lags = call(
+        functools.partial(inner_kernel, half),
+        [
+            shape((own, slim), jnp.float32),
+            shape((own, slim), low),
+            shape((8, total), jnp.float32),
+        ],
+        [pltpu.VMEM((own, slim), low)],
+        4 * nfil * own * slim * own,
+        8 * own * slim,
+        where, *inner, near,
+    )
+    (lags,) = call(
+        functools.partial(lag_kernel, half),
+        [shape((8, total), jnp.float32)],
+        [pltpu.VMEM((own, slim // 2), low)],
+        nfil * own * slim * own,
+        2 * own * slim,
+        where, *outer, flipped, lags,
+    )
+    outer[0], lags = after(outer[0], lags)
+    across = lambda value, move, turn: lax.ppermute(
+        value,
+        ("chan", "ctx"),
+        [(c * count + i, (c ^ move) * count + (i ^ turn)) for c in range(chans) for i in range(count)],
+    )
+    first = call(
+        functools.partial(outer_kernel, half),
+        [shape((rows + 16, slim), low)] * half,
+        [pltpu.VMEM((own, slim), low)] * 2,
+        2 * nfil * own * slim * own,
+        4 * own * slim,
+        where, *outer, near, part,
+    )
+    lags = lags + across(lags, 1, 0)
+    first = call(
+        functools.partial(attach_kernel, half),
+        [shape((rows + 16, slim), low)] * half,
+        [pltpu.VMEM((half, 16, slim), low), pltpu.SemaphoreType.DMA((half,))],
+        0,
+        32 * slim * half,
+        where, lags, *first, alias=half, far_out=True,
+    )
+    first = [first[0]] + [swap(first[k], k, count) for k in range(1, half)]
+    sums = sum(value[rows:, 0:LANES].astype(jnp.float32) for value in first)
+    sums = sums[: 2 * nfil] + sums[2 * nfil :]
+    mine, other = sums[:nfil], sums[nfil:]
+    scale = (total * (D // NFILT)) ** (-0.5)
+    arrived = [across(other, 0, half), across(mine, 2, 0), across(other, 2, half)]
+    filter_grad = (mine + sum(arrived)) * scale
+
+    outs = call(
+        functools.partial(final_kernel, half, slim),
+        [shape((rows, width), low)] * 4,
+        [pltpu.VMEM((half, 4, rows, slim), low), pltpu.SemaphoreType.DMA((half, 4))],
+        4 * rows * rows * width,
+        20 * rows * width,
+        where, queries, keys, values, cotangent, *first, *second, far_out=True,
+    )
+    return (*outs, filter_grad)
 
 
 def toeplitz(padded, base, height, breadth):
@@ -33,7 +453,7 @@
     return lax.dynamic_update_slice_in_dim(lag_acc, current + sums, where, 1)
 
 
-def shards(queries, keys, values, filters, cotangent):
+def channel_plan(queries, keys, values, filters, cotangent):
     rows, width = queries.shape
     nfil = filters.shape[0]
     gated = (keys.astype(jnp.float32) * values.astype(jnp.float32)).astype(jnp.bfloat16)
@@ -52,31 +472,26 @@
     back_cols = chan_back.reshape(blocks, rows, slim, nfil)
     gated_pad = jnp.concatenate([jnp.zeros_like(gated_cols), gated_cols], axis=0)
     back_pad = jnp.concatenate([back_cols, jnp.zeros_like(back_cols)], axis=0)
-    bundle = 4
-
-    def turn(index, carry):
+
+    def turn(offset, carry):
         mixed_acc, grad_acc, lag_acc = carry
-        for member in range(bundle):
-            offset = index * bundle + member
-            tile = toeplitz(padded, offset * rows, rows, rows)
-            earlier = lax.dynamic_slice_in_dim(gated_pad, blocks - offset, blocks, 0)
-            later = lax.dynamic_slice_in_dim(back_pad, offset, blocks, 0)
-            mixed_acc = mixed_acc + jnp.einsum(
-                "fst,ntcf->nscf", tile, earlier, preferred_element_type=jnp.float32
-            )
-            grad_acc = grad_acc + jnp.einsum(
-                "fst,nscf->ntcf", tile, later, preferred_element_type=jnp.float32
-            )
-            product = jnp.einsum(
-                "nscf,ntcf->fst", back_cols, earlier, preferred_element_type=jnp.float32
-            )
-            lag_acc = add_lags(lag_acc, diagonal_sums(product), offset * rows - rows + 1)
+        tile = toeplitz(padded, offset * rows, rows, rows)
+        earlier = lax.dynamic_slice_in_dim(gated_pad, blocks - offset, blocks, 0)
+        later = lax.dynamic_slice_in_dim(back_pad, offset, blocks, 0)
+        mixed_acc = mixed_acc + jnp.einsum(
+            "fst,ntcf->nscf", tile, earlier, preferred_element_type=jnp.float32
+        )
+        grad_acc = grad_acc + jnp.einsum(
+            "fst,nscf->ntcf", tile, later, preferred_element_type=jnp.float32
+        )
+        product = jnp.einsum(
+            "nscf,ntcf->fst", back_cols, earlier, preferred_element_type=jnp.float32
+        )
+        lag_acc = add_lags(lag_acc, diagonal_sums(product), offset * rows - rows + 1)
         return (mixed_acc, grad_acc, lag_acc)
 
     blank = jnp.zeros((blocks, rows, slim, nfil), jnp.float32)
-    mixed_acc, grad_acc, lag_part = lax.fori_loop(
-        0, blocks // bundle, turn, (blank, blank, lag_start)
-    )
+    mixed_acc, grad_acc, lag_part = lax.fori_loop(0, blocks, turn, (blank, blank, lag_start))
     mixed_chan = mixed_acc.reshape(total, slim * nfil)
     grad_chan = grad_acc.reshape(total, slim * nfil)
     mixed, gated_grad = (
@@ -97,23 +512,20 @@
 
 
 def solution(mesh):
-    placed = (
-        P("ctx", "chan"),
-        P("ctx", "chan"),
-        P("ctx", "chan"),
-        P(None, "ctx"),
-        P("ctx", "chan"),
-    )
+    count, chans = mesh.shape["ctx"], mesh.shape["chan"]
+
+    def shards(queries, keys, values, filters, cotangent):
+        width = queries.shape[1]
+        quarter = width // max(count // 2, 1)
+        if count == 8 and chans == 4 and quarter % (2 * LANES) == 0 and queries.shape[0] == LANES:
+            return halves_plan(count, chans, queries, keys, values, filters, cotangent)
+        return channel_plan(queries, keys, values, filters, cotangent)
+
+    wide = P("ctx", "chan")
     return jax.shard_map(
         shards,
         mesh=mesh,
-        in_specs=placed,
-        out_specs=(
-            P("ctx", "chan"),
-            P("ctx", "chan"),
-            P("ctx", "chan"),
-            P("ctx", "chan"),
-            P(None, "ctx"),
-        ),
+        in_specs=(wide, wide, wide, P(None, "ctx"), wide),
+        out_specs=(wide, wide, wide, wide, P(None, "ctx")),
         check_vma=False,
     )

time: 254 us -> 60.1 us (0.24)
  waiting for transfers between devices: 101 us -> 14.2 us
  local copies, waits for them, and re-layouts: 71.4 us -> 0.03 us
  blocking collectives: 28.3 us -> 0 us
  starting transfers between devices: 18.3 us -> 31.8 us
  between operations: 14.2 us -> 0.8 us
  matrix products: 12.7 us -> 0 us
  Pallas kernels: 0 us -> 11.9 us
  other arithmetic: 5.17 us -> 1.29 us
    unnamed x2 -> x0, waiting for transfers between devices: 68.2 us -> none
    all_to_all x4 -> x0, waiting for transfers between devices: 33.2 us -> none  [the longest x1 21 us: shards(): lax.all_to_all(mixed_chan, 'ctx', split_axis=0, concat_axis=1, tiled=True)]
    ppermute x0 -> x18, starting transfers between devices: none -> 31.8 us  [the longest x14 27 us: swap(): return lax.ppermute(value, 'ctx', [(i, i ^ step) for i in range(count)])]
    reshape x16 -> x0, local copies, waits for them, and re-layouts: 23 us -> none  [the longest x8 13.4 us: diagonal_sums(): return jnp.sum(flat.reshape(nfil, height, stride - 1), axis=1)]
    all_gather x1 -> x0, blocking collectives: 22.6 us -> none  [shards(): taps = lax.all_gather(filters, 'ctx', axis=1, tiled=True)]
    all_to_all x4 -> x0, starting transfers between devices: 18.3 us -> none  [the longest x1 7.41 us: shards(): lax.all_to_all(back, 'ctx', split_axis=1, concat_axis=0, tiled=True)]
    ppermute x0 -> x18, waiting for transfers between devices: none -> 14.2 us  [the longest x14 12.6 us: swap(): return lax.ppermute(value, 'ctx', [(i, i ^ step) for i in range(count)])]
    slice x17 -> x1, local copies, waits for them, and re-layouts: 13.4 us -> 0.01 us  [halves_plan(): mine, other = (sums[:nfil], sums[nfil:])]
  transfers between devices with their start and end apart: 5 -> 18, of which waited for: 3 -> 8; matrix products, arithmetic and copies ran while one was open for 4% -> 0% of each run, Pallas kernels for 0% -> 16%
where the time goes in v2:
time: 60.1 us; the launch traced here: 60 us
  starting transfers between devices  31.8 us (53%)
  waiting for transfers between devices  14.2 us (24%)
  Pallas kernels  11.9 us (20%)
  other arithmetic  1.29 us (2%)
  between operations  0.8 us (1%)
    ppermute x14, starting transfers between devices, swap(): return lax.ppermute(value, 'ctx', [(i, i ^ step) for i in range(count)])  27 us
    ppermute x14, waiting for transfers between devices, swap(): return lax.ppermute(value, 'ctx', [(i, i ^ step) for i in range(count)])  12.6 us
    pallas_call x8, Pallas kernels, call(): pl.pallas_call(kernel, out_shape=outs, in_specs=[pl.BlockSpec(memory_spac...  11.9 us
    ppermute x4, starting transfers between devices, halves_plan(): lax.ppermute(value, ('chan', 'ctx'), [(c * count + i, (c ^ move) * count...  4.77 us
    ppermute x4, waiting for transfers between devices, halves_plan(): lax.ppermute(value, ('chan', 'ctx'), [(c * count + i, (c ^ move) * count...  1.58 us
  transfers between devices with their start and end apart: 18, of which 8 were waited for; matrix products, arithmetic and copies ran while one was open for 0% of the time, Pallas kernels for 16%

profile of v2, /device:TPU:0, one launch (start us, length us, event | category | flops | bytes accessed | tf_op | source)
XLA Modules:
  0.0 60.0 jit_solution(16880055309354797923)
XLA Ops:
  0.6 0.7 %pad_convert_fusion.mine_ref = f32[8,128]{1,0:T(8,128)S(1)} fusion(bf16[4,128]{1,0:T(4,128)(2,1)} %param.8), kind=kLoop, calls=%fused_computation.3 | loop fusion | flops 1024 | bytes 5120 | tf_op jit(solution)/shard_map/jit(_pad)/pad | solution.py:325
  1.3 4.0 %collective-permute-start.2 = (f32[8,128]{1,0:T(8,128)S(1)}, f32[8,128]{1,0:T(8,128)S(1)}, u32[]{:S(2)}, u32[]{:S(2)}) collective-permute-start(f32[8,128]{1,0:T(8,128)S(1)} %pad_convert_fusion.mine_ref), channel_id=1, source_target_pairs={{0,4},{1,5},{2,6},{3,7},{4,0},{5,1},{6,2},{7,3},{8,12},{9,13},{10,... | collective-permute-start | bytes 12296 | tf_op jit(solution)/shard_map/ppermute | solution.py:287
  5.4 2.2 %shard_map.92 = (bf16[128,512]{1,0:T(8,128)(2,1)S(1)}, bf16[128,512]{1,0:T(8,128)(2,1)S(1)}, bf16[128,512]{1,0:T(8,128)(2,1)S(1)}, bf16[128,512]{1,0:T(8,128)(2,1)S(1)}, bf16[4,2,128,512]{3,2,1,0:T(8,128)(2,1)S(1)}) custom-call(s32[1]{0:T(128)} %bitcast.me_ref, bf16[128,2048]{1,0:T(8,128)(2,1)} %q_ref.3, bf16[128,2048]{1,0:T(8,128)(2,1)} %k_ref.3, ...), custom_call_target="tpu_custom_call" | custom-call | flops 67108864 | bytes 3670016 | tf_op jit(solution)/shard_map/pallas_call | solution.py:297
  7.6 0.4 shard_map.93
  8.0 1.6 %collective-permute-start.3 = (bf16[272,512]{1,0:T(8,128)(2,1)S(1)}, bf16[272,512]{1,0:T(8,128)(2,1)S(1)}, u32[]{:S(2)}, u32[]{:S(2)}) collective-permute-start(bf16[272,512]{1,0:T(8,128)(2,1)S(1)} %get-tuple-element.44), channel_id=1, source_target_pairs={{0,1},{1,0},{2,3},{3,2},{4,5},{5,4},{6,7},{7,6},{8,9},{9,8},{10,11... | collective-permute-start | bytes 835592 | tf_op jit(solution)/shard_map/ppermute | solution.py:287
  9.6 1.6 %collective-permute-start.5 = (bf16[272,512]{1,0:T(8,128)(2,1)S(1)}, bf16[272,512]{1,0:T(8,128)(2,1)S(1)}, u32[]{:S(2)}, u32[]{:S(2)}) collective-permute-start(bf16[272,512]{1,0:T(8,128)(2,1)S(1)} %get-tuple-element.47), channel_id=1, source_target_pairs={{0,2},{1,3},{2,0},{3,1},{4,6},{5,7},{6,4},{7,5},{8,10},{9,11},{10,... | collective-permute-start | bytes 835592 | tf_op jit(solution)/shard_map/ppermute | solution.py:287
  11.5 2.3 %collective-permute-start = (bf16[128,512]{1,0:T(8,128)(2,1)S(1)}, bf16[128,512]{1,0:T(8,128)(2,1)S(1)}, u32[]{:S(2)}, u32[]{:S(2)}) collective-permute-start(bf16[128,512]{1,0:T(8,128)(2,1)S(1)} %get-tuple-element.40), channel_id=1, source_target_pairs={{0,4},{1,5},{2,6},{3,7},{4,0},{5,1},{6,2},{7,3},{8,12},{9,13},{10,... | collective-permute-start | bytes 393224 | tf_op jit(solution)/shard_map/ppermute | solution.py:287
  13.8 1.6 %collective-permute-start.1 = (bf16[128,512]{1,0:T(8,128)(2,1)S(1)}, bf16[128,512]{1,0:T(8,128)(2,1)S(1)}, u32[]{:S(2)}, u32[]{:S(2)}) collective-permute-start(bf16[128,512]{1,0:T(8,128)(2,1)S(1)} %get-tuple-element.41), channel_id=1, source_target_pairs={{0,5},{1,4},{2,7},{3,6},{4,1},{5,0},{6,3},{7,2},{8,13},{9,12},{10,... | collective-permute-start | bytes 393224 | tf_op jit(solution)/shard_map/ppermute | solution.py:287
  15.4 0.7 %collective-permute-done.3.refs_1_ = bf16[272,512]{1,0:T(8,128)(2,1)S(1)} collective-permute-done((bf16[272,512]{1,0:T(8,128)(2,1)S(1)}, bf16[272,512]{1,0:T(8,128)(2,1)S(1)}, u32[]{:S(2)}, u32[]{:S(2)}) %collective-permute-start.3) | collective-permute-done | bytes 278560 | tf_op jit(solution)/shard_map/ppermute | solution.py:287
  16.2 2.6 %collective-permute-start.4 = (bf16[128,512]{1,0:T(8,128)(2,1)S(1)}, bf16[128,512]{1,0:T(8,128)(2,1)S(1)}, u32[]{:S(2)}, u32[]{:S(2)}) collective-permute-start(bf16[128,512]{1,0:T(8,128)(2,1)S(1)} %get-tuple-element.45), channel_id=1, source_target_pairs={{0,6},{1,7},{2,4},{3,5},{4,2},{5,3},{6,0},{7,1},{8,14},{9,15},{10,... | collective-permute-start | bytes 393224 | tf_op jit(solution)/shard_map/ppermute | solution.py:287
  18.7 6.1 %collective-permute-done.5.refs_2_ = bf16[272,512]{1,0:T(8,128)(2,1)S(1)} collective-permute-done((bf16[272,512]{1,0:T(8,128)(2,1)S(1)}, bf16[272,512]{1,0:T(8,128)(2,1)S(1)}, u32[]{:S(2)}, u32[]{:S(2)}) %collective-permute-start.5) | collective-permute-done | bytes 278560 | tf_op jit(solution)/shard_map/ppermute | solution.py:287
  24.8 3.2 %collective-permute-start.6 = (bf16[128,512]{1,0:T(8,128)(2,1)S(1)}, bf16[128,512]{1,0:T(8,128)(2,1)S(1)}, u32[]{:S(2)}, u32[]{:S(2)}) collective-permute-start(bf16[128,512]{1,0:T(8,128)(2,1)S(1)} %get-tuple-element.48), channel_id=1, source_target_pairs={{0,7},{1,6},{2,5},{3,4},{4,3},{5,2},{6,1},{7,0},{8,15},{9,14},{10,... | collective-permute-start | bytes 393224 | tf_op jit(solution)/shard_map/ppermute | solution.py:287
  28.0 2.6 %collective-permute-done.7.refs_3_ = bf16[272,512]{1,0:T(8,128)(2,1)S(1)} collective-permute-done((bf16[272,512]{1,0:T(8,128)(2,1)S(1)}, bf16[272,512]{1,0:T(8,128)(2,1)S(1)}, u32[]{:S(2)}, u32[]{:S(2)}) %collective-permute-start.7) | collective-permute-done | bytes 278560 | tf_op jit(solution)/shard_map/ppermute | solution.py:287
  30.6 1.4 %shard_map.94 = (bf16[128,512]{1,0:T(8,128)(2,1)S(1)}, bf16[128,512]{1,0:T(8,128)(2,1)S(1)}, bf16[128,512]{1,0:T(8,128)(2,1)S(1)}, bf16[128,512]{1,0:T(8,128)(2,1)S(1)}, bf16[4,256,1024]{2,1,0:T(8,128)(2,1)S(1)}) custom-call(s32[1]{0:T(128)} %bitcast.me_ref, bf16[272,512]{1,0:T(8,128)(2,1)S(1)} %get-tuple-element.49.refs_0_, ...), custom_call_target="tpu_custom_call" | custom-call | flops 1073741824 | bytes 2097152 | tf_op jit(solution)/shard_map/pallas_call | solution.py:297
  32.0 2.9 %shard_map.95 = (f32[512,512]{1,0:T(8,128)S(1)}, bf16[512,512]{1,0:T(8,128)(2,1)S(1)}, f32[8,1024]{1,0:T(8,128)S(1)}) custom-call(s32[1]{0:T(128)} %bitcast.me_ref, bf16[272,512]{1,0:T(8,128)(2,1)S(1)} %get-tuple-element.49.refs_0_, bf16[272,512]{1,0:T(8,128)(2,1)S(1)} %collective-permute-done.3.refs_1_, ...), custom_call_target="tpu_custom_call" | custom-call | flops 2147483648 | bytes 2097152 | tf_op jit(solution)/shard_map/pallas_call | solution.py:297
  34.9 0.6 %collective-permute-done.6.refs_3_ = bf16[128,512]{1,0:T(8,128)(2,1)S(1)} collective-permute-done((bf16[128,512]{1,0:T(8,128)(2,1)S(1)}, bf16[128,512]{1,0:T(8,128)(2,1)S(1)}, u32[]{:S(2)}, u32[]{:S(2)}) %collective-permute-start.6) | collective-permute-done | bytes 131104 | tf_op jit(solution)/shard_map/ppermute | solution.py:287
  35.5 1.7 %shard_map.96 = f32[8,1024]{1,0:T(8,128)S(1)} custom-call(s32[1]{0:T(128)} %bitcast.me_ref, bf16[128,512]{1,0:T(8,128)(2,1)S(1)} %collective-permute-done.refs_0_, bf16[128,512]{1,0:T(8,128)(2,1)S(1)} %collective-permute-done.1.refs_1_, bf16[128,512]{1,0:T(8,128)(2,1)S(1)} %collective-permute-done.4.refs_2_, ...), custom_call_target="tpu_custom_call" | custom-call | flops 536870912 | bytes 524288 | tf_op jit(solution)/shard_map/pallas_call | solution.py:297
  37.4 1.4 %shard_map.97 = (bf16[144,512]{1,0:T(8,128)(2,1)S(1)}, bf16[144,512]{1,0:T(8,128)(2,1)S(1)}, bf16[144,512]{1,0:T(8,128)(2,1)S(1)}, bf16[144,512]{1,0:T(8,128)(2,1)S(1)}) custom-call(s32[1]{0:T(128)} %bitcast.me_ref, bf16[128,512]{1,0:T(8,128)(2,1)S(1)} %collective-permute-done.refs_0_, bf16[128,512]{1,0:T(8,128)(2,1)S(1)} %collective-permute-done.1.refs_1_, ...), custom_call_target="tpu_custom_call" | custom-call | flops 1073741824 | bytes 1048576 | tf_op jit(solution)/shard_map/pallas_call | solution.py:297
  39.0 1.6 %collective-permute-start.9 = (bf16[144,512]{1,0:T(8,128)(2,1)S(1)}, bf16[144,512]{1,0:T(8,128)(2,1)S(1)}, u32[]{:S(2)}, u32[]{:S(2)}) collective-permute-start(bf16[144,512]{1,0:T(8,128)(2,1)S(1)} %get-tuple-element.64), channel_id=1, source_target_pairs={{0,1},{1,0},{2,3},{3,2},{4,5},{5,4},{6,7},{7,6},{8,9},{9,8},{10,11... | collective-permute-start | bytes 442376 | tf_op jit(solution)/shard_map/ppermute | solution.py:287
  40.6 2.0 %collective-permute-start.10 = (bf16[144,512]{1,0:T(8,128)(2,1)S(1)}, bf16[144,512]{1,0:T(8,128)(2,1)S(1)}, u32[]{:S(2)}, u32[]{:S(2)}) collective-permute-start(bf16[144,512]{1,0:T(8,128)(2,1)S(1)} %get-tuple-element.65), channel_id=1, source_target_pairs={{0,2},{1,3},{2,0},{3,1},{4,6},{5,7},{6,4},{7,5},{8,10},{9,11},{10,... | collective-permute-start | bytes 442376 | tf_op jit(solution)/shard_map/ppermute | solution.py:287
  42.6 0.4 collective-permute-start.11
  43.0 1.1 %collective-permute-start.12 = (bf16[128,512]{1,0:T(8,128)(2,1)S(1)}, bf16[128,512]{1,0:T(8,128)(2,1)S(1)}, u32[]{:S(2)}, u32[]{:S(2)}) collective-permute-start(bf16[128,512]{1,0:T(8,128)(2,1)S(1)} %get-tuple-element.68), channel_id=1, source_target_pairs={{0,1},{1,0},{2,3},{3,2},{4,5},{5,4},{6,7},{7,6},{8,9},{9,8},{10,11... | collective-permute-start | bytes 393224 | tf_op jit(solution)/shard_map/ppermute | solution.py:287
  44.1 2.0 %collective-permute-start.13 = (bf16[128,512]{1,0:T(8,128)(2,1)S(1)}, bf16[128,512]{1,0:T(8,128)(2,1)S(1)}, u32[]{:S(2)}, u32[]{:S(2)}) collective-permute-start(bf16[128,512]{1,0:T(8,128)(2,1)S(1)} %get-tuple-element.69), channel_id=1, source_target_pairs={{0,2},{1,3},{2,0},{3,1},{4,6},{5,7},{6,4},{7,5},{8,10},{9,11},{10,... | collective-permute-start | bytes 393224 | tf_op jit(solution)/shard_map/ppermute | solution.py:287
  46.1 2.6 %collective-permute-start.14 = (bf16[128,512]{1,0:T(8,128)(2,1)S(1)}, bf16[128,512]{1,0:T(8,128)(2,1)S(1)}, u32[]{:S(2)}, u32[]{:S(2)}) collective-permute-start(bf16[128,512]{1,0:T(8,128)(2,1)S(1)} %get-tuple-element.70), channel_id=1, source_target_pairs={{0,3},{1,2},{2,1},{3,0},{4,7},{5,6},{6,5},{7,4},{8,11},{9,10},{10,... | collective-permute-start | bytes 393224 | tf_op jit(solution)/shard_map/ppermute | solution.py:287
  48.7 2.1 %collective-permute-done.11.refs_3_ = bf16[144,512]{1,0:T(8,128)(2,1)S(1)} collective-permute-done((bf16[144,512]{1,0:T(8,128)(2,1)S(1)}, bf16[144,512]{1,0:T(8,128)(2,1)S(1)}, u32[]{:S(2)}, u32[]{:S(2)}) %collective-permute-start.11) | collective-permute-done | bytes 147488 | tf_op jit(solution)/shard_map/ppermute | solution.py:287
  50.8 4.1 %collective-permute-start.17 = (f32[4,128]{1,0:T(4,128)S(1)}, f32[4,128]{1,0:T(4,128)S(1)}, u32[]{:S(2)}, u32[]{:S(2)}) collective-permute-start(f32[4,128]{1,0:T(4,128)S(1)} %get-tuple-element.76), channel_id=1, source_target_pairs={{0,20},{1,21},{2,22},{3,23},{4,16},{5,17},{6,18},{7,19},{8,28},{9,... | collective-permute-start | bytes 6152 | tf_op jit(solution)/shard_map/ppermute | solution.py:389
  54.9 0.6 %collective-permute-start.16 = (f32[4,128]{1,0:T(4,128)S(1)}, f32[4,128]{1,0:T(4,128)S(1)}, u32[]{:S(2)}, u32[]{:S(2)}) collective-permute-start(f32[4,128]{1,0:T(4,128)S(1)} %get-tuple-element.75), channel_id=1, source_target_pairs={{0,16},{1,17},{2,18},{3,19},{4,20},{5,21},{6,22},{7,23},{8,24},{9,... | collective-permute-start | bytes 6152 | tf_op jit(solution)/shard_map/ppermute | solution.py:389
  55.5 0.5 collective-permute-done.14.refs_7_
  56.0 1.8 %shard_map.99 = (bf16[128,2048]{1,0:T(8,128)(2,1)}, bf16[128,2048]{1,0:T(8,128)(2,1)}, bf16[128,2048]{1,0:T(8,128)(2,1)}, bf16[128,2048]{1,0:T(8,128)(2,1)}) custom-call(s32[1]{0:T(128)} %bitcast.me_ref, bf16[128,2048]{1,0:T(8,128)(2,1)S(1)} %copy-done, bf16[128,2048]{1,0:T(8,128)(2,1)S(1)} %copy-done.1, bf16[128,2048]{1,0:T(8,128)(2,1)S(1)} %copy-done.2, ...), custom_call_target="tpu_custom_call" | custom-call | flops 134217728 | bytes 5242880 | tf_op jit(solution)/shard_map/pallas_call | solution.py:297
  57.8 0.7 %collective-permute-done.16 = f32[4,128]{1,0:T(4,128)S(1)} collective-permute-done((f32[4,128]{1,0:T(4,128)S(1)}, f32[4,128]{1,0:T(4,128)S(1)}, u32[]{:S(2)}, u32[]{:S(2)}) %collective-permute-start.16) | collective-permute-done | bytes 2080 | tf_op jit(solution)/shard_map/ppermute | solution.py:389
  58.5 0.9 %collective-permute-done.15 = f32[4,128]{1,0:T(4,128)S(1)} collective-permute-done((f32[4,128]{1,0:T(4,128)S(1)}, f32[4,128]{1,0:T(4,128)S(1)}, u32[]{:S(2)}, u32[]{:S(2)}) %collective-permute-start.15) | collective-permute-done | bytes 2080 | tf_op jit(solution)/shard_map/ppermute | solution.py:389
  59.4 0.6 add_multiply_fusion
  (26 shorter events, 0.7 us)
Async XLA Ops:
  1.3 6.2 %collective-permute-start.2 = (f32[8,128]{1,0:T(8,128)S(1)}, f32[8,128]{1,0:T(8,128)S(1)}, u32[]{:S(2)}, u32[]{:S(2)}) collective-permute-start(f32[8,128]{1,0:T(8,128)S(1)} %pad_convert_fusion.mine_ref), channel_id=1, source_target_pairs={{0,4},{1,5},{2,6},{3,7},{4,0},{5,1},{6,2},{7,3},{8,12},{9,13},{10,... | collective-permute-start | bytes 12296 | tf_op jit(solution)/shard_map/ppermute | solution.py:287
  8.0 8.2 %collective-permute-start.3 = (bf16[272,512]{1,0:T(8,128)(2,1)S(1)}, bf16[272,512]{1,0:T(8,128)(2,1)S(1)}, u32[]{:S(2)}, u32[]{:S(2)}) collective-permute-start(bf16[272,512]{1,0:T(8,128)(2,1)S(1)} %get-tuple-element.44), channel_id=1, source_target_pairs={{0,1},{1,0},{2,3},{3,2},{4,5},{5,4},{6,7},{7,6},{8,9},{9,8},{10,11... | collective-permute-start | bytes 835592 | tf_op jit(solution)/shard_map/ppermute | solution.py:287
  9.6 15.2 %collective-permute-start.5 = (bf16[272,512]{1,0:T(8,128)(2,1)S(1)}, bf16[272,512]{1,0:T(8,128)(2,1)S(1)}, u32[]{:S(2)}, u32[]{:S(2)}) collective-permute-start(bf16[272,512]{1,0:T(8,128)(2,1)S(1)} %get-tuple-element.47), channel_id=1, source_target_pairs={{0,2},{1,3},{2,0},{3,1},{4,6},{5,7},{6,4},{7,5},{8,10},{9,11},{10,... | collective-permute-start | bytes 835592 | tf_op jit(solution)/shard_map/ppermute | solution.py:287
  11.2 19.5 %collective-permute-start.7 = (bf16[272,512]{1,0:T(8,128)(2,1)S(1)}, bf16[272,512]{1,0:T(8,128)(2,1)S(1)}, u32[]{:S(2)}, u32[]{:S(2)}) collective-permute-start(bf16[272,512]{1,0:T(8,128)(2,1)S(1)} %get-tuple-element.52), channel_id=1, source_target_pairs={{0,3},{1,2},{2,1},{3,0},{4,7},{5,6},{6,5},{7,4},{8,11},{9,10},{10,... | collective-permute-start | bytes 835592 | tf_op jit(solution)/shard_map/ppermute | solution.py:287
  11.5 23.3 %collective-permute-start = (bf16[128,512]{1,0:T(8,128)(2,1)S(1)}, bf16[128,512]{1,0:T(8,128)(2,1)S(1)}, u32[]{:S(2)}, u32[]{:S(2)}) collective-permute-start(bf16[128,512]{1,0:T(8,128)(2,1)S(1)} %get-tuple-element.40), channel_id=1, source_target_pairs={{0,4},{1,5},{2,6},{3,7},{4,0},{5,1},{6,2},{7,3},{8,12},{9,13},{10,... | collective-permute-start | bytes 393224 | tf_op jit(solution)/shard_map/ppermute | solution.py:287
  13.8 21.1 %collective-permute-start.1 = (bf16[128,512]{1,0:T(8,128)(2,1)S(1)}, bf16[128,512]{1,0:T(8,128)(2,1)S(1)}, u32[]{:S(2)}, u32[]{:S(2)}) collective-permute-start(bf16[128,512]{1,0:T(8,128)(2,1)S(1)} %get-tuple-element.41), channel_id=1, source_target_pairs={{0,5},{1,4},{2,7},{3,6},{4,1},{5,0},{6,3},{7,2},{8,13},{9,12},{10,... | collective-permute-start | bytes 393224 | tf_op jit(solution)/shard_map/ppermute | solution.py:287
  16.2 18.7 %collective-permute-start.4 = (bf16[128,512]{1,0:T(8,128)(2,1)S(1)}, bf16[128,512]{1,0:T(8,128)(2,1)S(1)}, u32[]{:S(2)}, u32[]{:S(2)}) collective-permute-start(bf16[128,512]{1,0:T(8,128)(2,1)S(1)} %get-tuple-element.45), channel_id=1, source_target_pairs={{0,6},{1,7},{2,4},{3,5},{4,2},{5,3},{6,0},{7,1},{8,14},{9,15},{10,... | collective-permute-start | bytes 393224 | tf_op jit(solution)/shard_map/ppermute | solution.py:287
  24.8 10.7 %collective-permute-start.6 = (bf16[128,512]{1,0:T(8,128)(2,1)S(1)}, bf16[128,512]{1,0:T(8,128)(2,1)S(1)}, u32[]{:S(2)}, u32[]{:S(2)}) collective-permute-start(bf16[128,512]{1,0:T(8,128)(2,1)S(1)} %get-tuple-element.48), channel_id=1, source_target_pairs={{0,7},{1,6},{2,5},{3,4},{4,3},{5,2},{6,1},{7,0},{8,15},{9,14},{10,... | collective-permute-start | bytes 393224 | tf_op jit(solution)/shard_map/ppermute | solution.py:287
  37.3 1.5 %collective-permute-start.8 = (f32[8,1024]{1,0:T(8,128)S(1)}, f32[8,1024]{1,0:T(8,128)S(1)}, u32[]{:S(2)}, u32[]{:S(2)}) collective-permute-start(f32[8,1024]{1,0:T(8,128)S(1)} %shard_map.96), channel_id=1, source_target_pairs={{0,8},{1,9},{2,10},{3,11},{4,12},{5,13},{6,14},{7,15},{8,0},{9,1},... | collective-permute-start | bytes 98312 | tf_op jit(solution)/shard_map/ppermute | solution.py:389
  37.3 18.7 %copy-start = (bf16[128,2048]{1,0:T(8,128)(2,1)S(1)}, bf16[128,2048]{1,0:T(8,128)(2,1)}, u32[]{:S(2)}) copy-start(bf16[128,2048]{1,0:T(8,128)(2,1)} %q_ref.3) | copy-start | bytes 1572868
  37.3 18.7 %copy-start.1 = (bf16[128,2048]{1,0:T(8,128)(2,1)S(1)}, bf16[128,2048]{1,0:T(8,128)(2,1)}, u32[]{:S(2)}) copy-start(bf16[128,2048]{1,0:T(8,128)(2,1)} %k_ref.3) | copy-start | bytes 1572868
  37.4 18.7 %copy-start.2 = (bf16[128,2048]{1,0:T(8,128)(2,1)S(1)}, bf16[128,2048]{1,0:T(8,128)(2,1)}, u32[]{:S(2)}) copy-start(bf16[128,2048]{1,0:T(8,128)(2,1)} %v_ref.3) | copy-start | bytes 1572868
  37.4 18.7 %copy-start.3 = (bf16[128,2048]{1,0:T(8,128)(2,1)S(1)}, bf16[128,2048]{1,0:T(8,128)(2,1)}, u32[]{:S(2)}) copy-start(bf16[128,2048]{1,0:T(8,128)(2,1)} %g_ref.3) | copy-start | bytes 1572868
  39.0 7.1 %collective-permute-start.9 = (bf16[144,512]{1,0:T(8,128)(2,1)S(1)}, bf16[144,512]{1,0:T(8,128)(2,1)S(1)}, u32[]{:S(2)}, u32[]{:S(2)}) collective-permute-start(bf16[144,512]{1,0:T(8,128)(2,1)S(1)} %get-tuple-element.64), channel_id=1, source_target_pairs={{0,1},{1,0},{2,3},{3,2},{4,5},{5,4},{6,7},{7,6},{8,9},{9,8},{10,11... | collective-permute-start | bytes 442376 | tf_op jit(solution)/shard_map/ppermute | solution.py:287
  40.6 8.1 %collective-permute-start.10 = (bf16[144,512]{1,0:T(8,128)(2,1)S(1)}, bf16[144,512]{1,0:T(8,128)(2,1)S(1)}, u32[]{:S(2)}, u32[]{:S(2)}) collective-permute-start(bf16[144,512]{1,0:T(8,128)(2,1)S(1)} %get-tuple-element.65), channel_id=1, source_target_pairs={{0,2},{1,3},{2,0},{3,1},{4,6},{5,7},{6,4},{7,5},{8,10},{9,11},{10,... | collective-permute-start | bytes 442376 | tf_op jit(solution)/shard_map/ppermute | solution.py:287
  42.6 8.2 %collective-permute-start.11 = (bf16[144,512]{1,0:T(8,128)(2,1)S(1)}, bf16[144,512]{1,0:T(8,128)(2,1)S(1)}, u32[]{:S(2)}, u32[]{:S(2)}) collective-permute-start(bf16[144,512]{1,0:T(8,128)(2,1)S(1)} %get-tuple-element.66), channel_id=1, source_target_pairs={{0,3},{1,2},{2,1},{3,0},{4,7},{5,6},{6,5},{7,4},{8,11},{9,10},{10,... | collective-permute-start | bytes 442376 | tf_op jit(solution)/shard_map/ppermute | solution.py:287
  43.0 11.9 %collective-permute-start.12 = (bf16[128,512]{1,0:T(8,128)(2,1)S(1)}, bf16[128,512]{1,0:T(8,128)(2,1)S(1)}, u32[]{:S(2)}, u32[]{:S(2)}) collective-permute-start(bf16[128,512]{1,0:T(8,128)(2,1)S(1)} %get-tuple-element.68), channel_id=1, source_target_pairs={{0,1},{1,0},{2,3},{3,2},{4,5},{5,4},{6,7},{7,6},{8,9},{9,8},{10,11... | collective-permute-start | bytes 393224 | tf_op jit(solution)/shard_map/ppermute | solution.py:287
  44.1 11.5 %collective-permute-start.13 = (bf16[128,512]{1,0:T(8,128)(2,1)S(1)}, bf16[128,512]{1,0:T(8,128)(2,1)S(1)}, u32[]{:S(2)}, u32[]{:S(2)}) collective-permute-start(bf16[128,512]{1,0:T(8,128)(2,1)S(1)} %get-tuple-element.69), channel_id=1, source_target_pairs={{0,2},{1,3},{2,0},{3,1},{4,6},{5,7},{6,4},{7,5},{8,10},{9,11},{10,... | collective-permute-start | bytes 393224 | tf_op jit(solution)/shard_map/ppermute | solution.py:287
  46.1 9.9 %collective-permute-start.14 = (bf16[128,512]{1,0:T(8,128)(2,1)S(1)}, bf16[128,512]{1,0:T(8,128)(2,1)S(1)}, u32[]{:S(2)}, u32[]{:S(2)}) collective-permute-start(bf16[128,512]{1,0:T(8,128)(2,1)S(1)} %get-tuple-element.70), channel_id=1, source_target_pairs={{0,3},{1,2},{2,1},{3,0},{4,7},{5,6},{6,5},{7,4},{8,11},{9,10},{10,... | collective-permute-start | bytes 393224 | tf_op jit(solution)/shard_map/ppermute | solution.py:287
  50.8 7.7 %collective-permute-start.17 = (f32[4,128]{1,0:T(4,128)S(1)}, f32[4,128]{1,0:T(4,128)S(1)}, u32[]{:S(2)}, u32[]{:S(2)}) collective-permute-start(f32[4,128]{1,0:T(4,128)S(1)} %get-tuple-element.76), channel_id=1, source_target_pairs={{0,20},{1,21},{2,22},{3,23},{4,16},{5,17},{6,18},{7,19},{8,28},{9,... | collective-permute-start | bytes 6152 | tf_op jit(solution)/shard_map/ppermute | solution.py:389
  54.9 4.5 %collective-permute-start.15 = (f32[4,128]{1,0:T(4,128)S(1)}, f32[4,128]{1,0:T(4,128)S(1)}, u32[]{:S(2)}, u32[]{:S(2)}) collective-permute-start(f32[4,128]{1,0:T(4,128)S(1)} %get-tuple-element.76), channel_id=1, source_target_pairs={{0,4},{1,5},{2,6},{3,7},{4,0},{5,1},{6,2},{7,3},{8,12},{9,13},{10,... | collective-permute-start | bytes 6152 | tf_op jit(solution)/shard_map/ppermute | solution.py:389
  54.9 3.6 %collective-permute-start.16 = (f32[4,128]{1,0:T(4,128)S(1)}, f32[4,128]{1,0:T(4,128)S(1)}, u32[]{:S(2)}, u32[]{:S(2)}) collective-permute-start(f32[4,128]{1,0:T(4,128)S(1)} %get-tuple-element.75), channel_id=1, source_target_pairs={{0,16},{1,17},{2,18},{3,19},{4,20},{5,21},{6,22},{7,23},{8,24},{9,... | collective-permute-start | bytes 6152 | tf_op jit(solution)/shard_map/ppermute | solution.py:389

commit v3 on v2

--- a/solution.py
+++ b/solution.py
@@ -56,7 +56,9 @@
 def bundle_kernel(half, me_ref, mine_ref, other_ref, pair_ref, *outs):
     rows = pair_ref.shape[2]
     turn = exchange(rows, me_ref[0] >= half, jnp.bfloat16)
-    both = jnp.concatenate([mine_ref[...], other_ref[...]], axis=0).astype(jnp.bfloat16)
+    mine, other = mine_ref[...].astype(jnp.float32), other_ref[...].astype(jnp.float32)
+    gap = jnp.zeros((8 - mine.shape[0], LANES), jnp.float32)
+    both = jnp.concatenate([mine, gap, other, gap], axis=0).astype(jnp.bfloat16)
     for step in range(half):
         outs[step][0:rows, :] = exact_rows(turn, pair_ref[step, 0])
         outs[step][rows : 2 * rows, :] = exact_rows(turn, pair_ref[step, 1])
@@ -92,23 +94,64 @@
     return pl.ds(pl.multiple_of(slot * rows, rows), rows)
 
 
-def add_lags_of(first, flipped, mask, start, width, acc):
-    near = lax.dot_general(
-        flipped, first * mask, (((1,), (1,)), ((), ())), preferred_element_type=jnp.float32
-    )
-    rows, reach = near.shape
-    pieces = [near, jnp.zeros((rows, width - start - reach), jnp.float32)]
+def products(left, right):
+    contract = (((1,), (1,)), ((), ()))
+    return lax.dot_general(left, right, contract, preferred_element_type=jnp.float32)
+
+
+def placed(values, start, width):
+    rows, reach = values.shape
+    pieces = [values, jnp.zeros((rows, width - start - reach), jnp.float32)]
     if start:
         pieces = [jnp.zeros((rows, start), jnp.float32)] + pieces
-    return acc + jnp.concatenate(pieces, axis=1)
-
-
-def lag_sums(acc):
-    rows, width = acc.shape
+    return jnp.concatenate(pieces, axis=1)
+
+
+def diagonal_rows(acc):
     rolled = pltpu.roll(acc, 0, 1, stride=1, stride_axis=0)
-    sums = jnp.sum(rolled, axis=0, keepdims=True)
-    sums = jnp.broadcast_to(sums, (8, width))
-    return pltpu.roll(sums, width - rows + 1, 1)[0:1, 0 : width - rows]
+    return jnp.broadcast_to(jnp.sum(rolled, axis=0, keepdims=True), (8, acc.shape[1]))
+
+
+def pair_base(half, me, pair, rows):
+    slot = slot_of(half, me, 2 * pair)
+    return pl.multiple_of((slot // 2) * 2 * rows, 2 * rows)
+
+
+def stack_pair(half, me, pair, arrived, target, rows):
+    for index in range(2):
+        place = (slot_of(half, me, 2 * pair + index) % 2) * rows
+        target[pl.ds(pl.multiple_of(place, rows), rows), :] = arrived[index][...]
+
+
+def outer_lags(half, me, base, pair_ref, flip_ref, lag_ref):
+    own, width = flip_ref.shape
+    rows = own // half
+    reach = pair_ref.shape[0]
+    share = width // 2
+    window = own + reach
+    lanes = pl.ds(pl.multiple_of(jnp.where(me >= half, share, 0), LANES), share)
+    for index in range(NFILT):
+        right = pair_ref[:, lanes] * lane_mask(share, NFILT, index)
+        acc = jnp.zeros((rows, window), jnp.float32)
+        for start in range(0, own, rows):
+            left = flip_ref[start : start + rows, lanes]
+            acc = acc + placed(products(left, right), own - rows - start, window)
+        sums = pltpu.roll(diagonal_rows(acc), 1, 1)
+        lag_ref[index : index + 1, pl.ds(base, window)] += sums[0:1, :]
+
+
+def outer_rows(half, top, base, near_ref, pair_ref):
+    nfil, size, total = near_ref.shape
+    reach, width = pair_ref.shape
+    acc = jnp.zeros((size, width), jnp.float32)
+    for index in range(nfil):
+        start = pl.multiple_of(total // 2 - top + base, reach)
+        acc += jnp.dot(
+            near_ref[index, :, pl.ds(start, reach)],
+            pair_ref[...] * lane_mask(width, nfil, index),
+            preferred_element_type=jnp.float32,
+        )
+    return acc
 
 
 def lane_mask(width, nfil, index):
@@ -116,18 +159,24 @@
     return jnp.where(lane % nfil == index, 1.0, 0.0).astype(jnp.bfloat16)
 
 
-def second_kernel(half, me_ref, *refs):
-    arrived = refs[:half]
-    outs = refs[half : 2 * half]
-    near_ref, far_ref, line, second_ref, result_ref = refs[2 * half :]
+def inner_kernel(half, me_ref, *refs):
+    arrived, across = refs[:half], refs[half : half + 2]
+    outs = refs[half + 2 : 2 * half + 2]
+    near_ref, part_ref, flip_ref, lag_ref = refs[2 * half + 2 : 2 * half + 6]
+    far_ref, line, first_ref, second_ref, pair_ref, result_ref = refs[2 * half + 6 :]
     nfil, size, total = near_ref.shape
     own, width = second_ref.shape
     rows = own // half
     me = me_ref[0]
+    turn = exchange(rows, True, jnp.bfloat16)
     fill_bands(half, me, arrived, near_ref, far_ref, line)
     for step in range(half):
         where = rows_at(slot_of(half, me, step), rows)
+        first_ref[where, :] = arrived[step][0:rows, :]
         second_ref[where, :] = arrived[step][rows : 2 * rows, :]
+        flip_ref[where, :] = exact_rows(turn, arrived[step][rows : 2 * rows, :])
+    stack_pair(half, me, 0, across, pair_ref, rows)
+    base = pair_base(half, me, 0, rows)
     masks = [lane_mask(width, nfil, index) for index in range(nfil)]
     for top in range(0, own, size):
         acc = jnp.zeros((size, width), jnp.float32)
@@ -140,23 +189,8 @@
         result_ref[top : top + size, :] = acc.astype(jnp.bfloat16)
     for step in range(half):
         outs[step][...] = result_ref[rows_at(slot_of(half, me, step), rows), :]
-
-
-def inner_kernel(half, me_ref, *refs):
-    arrived = refs[:half]
-    near_ref, part_ref, flip_ref, lag_ref, first_ref = refs[half:]
-    nfil, size, total = near_ref.shape
-    own, width = first_ref.shape
-    rows = own // half
-    me = me_ref[0]
-    turn = exchange(rows, True, jnp.bfloat16)
-    for step in range(half):
-        where = rows_at(slot_of(half, me, step), rows)
-        first_ref[where, :] = arrived[step][0:rows, :]
-        flip_ref[where, :] = exact_rows(turn, arrived[step][rows : 2 * rows, :])
-    masks = [lane_mask(width, nfil, index) for index in range(nfil)]
     for top in range(0, own, size):
-        acc = jnp.zeros((size, width), jnp.float32)
+        acc = outer_rows(half, top, base, near_ref, pair_ref)
         for index in range(nfil):
             acc += jnp.dot(
                 near_ref[index, :, 0 : own - top],
@@ -168,43 +202,23 @@
     for index in range(nfil):
         acc = jnp.zeros((rows, own + rows), jnp.float32)
         for start in range(0, own, rows):
-            acc = add_lags_of(
-                first_ref[start:own, :],
-                flip_ref[start : start + rows, :],
-                masks[index],
-                0,
-                own + rows,
-                acc,
+            right = first_ref[start:own, :] * masks[index]
+            acc = acc + placed(
+                products(flip_ref[start : start + rows, :], right), 0, own + rows
             )
-        lag_ref[index : index + 1, 0:own] = lag_sums(acc)
+        sums = pltpu.roll(diagonal_rows(acc), own + 1, 1)
+        lag_ref[index : index + 1, 0:own] = sums[0:1, 0:own]
+    outer_lags(half, me, base, pair_ref, flip_ref, lag_ref)
 
 
 def lag_kernel(half, me_ref, *refs):
-    arrived = refs[:half]
-    flip_ref, lag_ref, out_ref, first_ref = refs[half:]
-    nfil, total = NFILT, lag_ref.shape[1]
-    own, width = flip_ref.shape
-    rows = own // half
+    across = refs[:2]
+    flip_ref, lag_ref, out_ref, pair_ref = refs[2:]
+    rows = flip_ref.shape[0] // half
     me = me_ref[0]
-    share = width // 2
-    lanes = pl.ds(pl.multiple_of(jnp.where(me >= half, share, 0), LANES), share)
-    for step in range(half):
-        where = rows_at(slot_of(half, me, step), rows)
-        first_ref[where, :] = arrived[step][:, lanes]
+    stack_pair(half, me, 1, across, pair_ref, rows)
     out_ref[...] = lag_ref[...]
-    for index in range(nfil):
-        mask = lane_mask(share, nfil, index)
-        acc = jnp.zeros((rows, total + rows), jnp.float32)
-        for start in range(0, own, rows):
-            acc = add_lags_of(
-                first_ref[...],
-                flip_ref[start : start + rows, lanes],
-                mask,
-                own - start,
-                total + rows,
-                acc,
-            )
-        out_ref[index : index + 1, :] += lag_sums(acc)
+    outer_lags(half, me, pair_base(half, me, 1, rows), pair_ref, flip_ref, out_ref)
 
 
 def attach_kernel(half, me_ref, lag_ref, *refs):
@@ -231,24 +245,18 @@
 
 
 def outer_kernel(half, me_ref, *refs):
-    arrived = refs[:half]
-    near_ref, part_ref = refs[half : half + 2]
-    outs = refs[half + 2 : 2 * half + 2]
-    first_ref, result_ref = refs[2 * half + 2 :]
+    across = refs[:2]
+    near_ref, part_ref = refs[2:4]
+    outs = refs[4 : half + 4]
+    pair_ref, result_ref = refs[half + 4 :]
     nfil, size, total = near_ref.shape
     own, width = part_ref.shape
     rows = own // half
     me = me_ref[0]
-    for step in range(half):
-        first_ref[rows_at(slot_of(half, me, step), rows), :] = arrived[step][...]
+    stack_pair(half, me, 1, across, pair_ref, rows)
+    base = pair_base(half, me, 1, rows)
     for top in range(0, own, size):
-        acc = part_ref[top : top + size, :]
-        for index in range(nfil):
-            acc += jnp.dot(
-                near_ref[index, :, own - top : total - top],
-                first_ref[...] * lane_mask(width, nfil, index),
-                preferred_element_type=jnp.float32,
-            )
+        acc = part_ref[top : top + size, :] + outer_rows(half, top, base, near_ref, pair_ref)
         result_ref[top : top + size, :] = acc.astype(jnp.bfloat16)
     for step in range(half):
         outs[step][0:rows, :] = result_ref[rows_at(slot_of(half, me, step), rows), :]
@@ -322,8 +330,7 @@
     me = lax.axis_index("ctx")
     where = me.astype(jnp.int32).reshape(1)
 
-    taps = jnp.pad(filters.astype(jnp.float32), ((0, 8 - nfil), (0, 0)))
-    other_taps = swap(taps, half, count)
+    other_taps = swap(filters, half, count)
     branches = [
         pltpu.with_memory_space_constraint(x, pltpu.HBM)
         for x in (queries, keys, values, cotangent)
@@ -342,62 +349,60 @@
         [],
         4 * rows * rows * width,
         8 * rows * width,
-        where, taps, other_taps, pair,
+        where, filters, other_taps, pair,
     )
     inner = [inner[0]] + [swap(inner[k], k, count) for k in range(1, half)]
     outer = list(sent)
-    for k in range(half):
-        if k >= half - 2:
-            outer[k], inner[k - 1] = after(outer[k], inner[k - 1])
-        outer[k] = swap(outer[k], half + k, count)
-
-    *second, near = call(
-        functools.partial(second_kernel, half),
-        [shape((rows, slim), low)] * half + [shape((nfil, size, total), low)],
+    outer[0] = swap(outer[0], half, count)
+    outer[1] = swap(outer[1], half + 1, count)
+    outer[2], inner[1] = after(outer[2], inner[1])
+    outer[2] = swap(outer[2], half + 2, count)
+    outer[3], inner[2] = after(outer[3], inner[2])
+    outer[3] = swap(outer[3], half + 3, count)
+
+    *second, near, part, flipped, lags = call(
+        functools.partial(inner_kernel, half),
+        [shape((rows, slim), low)] * half
+        + [
+            shape((nfil, size, total), low),
+            shape((own, slim), jnp.float32),
+            shape((own, slim), low),
+            shape((8, total), jnp.float32),
+        ],
         [
             pltpu.VMEM((nfil, size, own), low),
             pltpu.VMEM((8, total), jnp.float32),
             pltpu.VMEM((own, slim), low),
             pltpu.VMEM((own, slim), low),
+            pltpu.VMEM((2 * rows, slim), low),
+            pltpu.VMEM((own, slim), low),
         ],
-        2 * nfil * own * slim * own,
+        8 * nfil * own * slim * own,
         8 * own * slim,
-        where, *inner,
+        where, *inner, *outer[:2],
     )
     second = [second[0]] + [swap(second[k], k, count) for k in range(1, half)]
-    part, flipped, lags = call(
-        functools.partial(inner_kernel, half),
-        [
-            shape((own, slim), jnp.float32),
-            shape((own, slim), low),
-            shape((8, total), jnp.float32),
-        ],
-        [pltpu.VMEM((own, slim), low)],
-        4 * nfil * own * slim * own,
-        8 * own * slim,
-        where, *inner, near,
-    )
-    (lags,) = call(
-        functools.partial(lag_kernel, half),
-        [shape((8, total), jnp.float32)],
-        [pltpu.VMEM((own, slim // 2), low)],
-        nfil * own * slim * own,
-        2 * own * slim,
-        where, *outer, flipped, lags,
-    )
-    outer[0], lags = after(outer[0], lags)
     across = lambda value, move, turn: lax.ppermute(
         value,
         ("chan", "ctx"),
         [(c * count + i, (c ^ move) * count + (i ^ turn)) for c in range(chans) for i in range(count)],
     )
+    (lags,) = call(
+        functools.partial(lag_kernel, half),
+        [shape((8, total), jnp.float32)],
+        [pltpu.VMEM((2 * rows, slim), low)],
+        nfil * own * slim * own // 2,
+        own * slim,
+        where, *outer[2:], flipped, lags,
+    )
+    outer[2], lags = after(outer[2], lags)
     first = call(
         functools.partial(outer_kernel, half),
         [shape((rows + 16, slim), low)] * half,
-        [pltpu.VMEM((own, slim), low)] * 2,
-        2 * nfil * own * slim * own,
+        [pltpu.VMEM((2 * rows, slim), low), pltpu.VMEM((own, slim), low)],
+        nfil * own * slim * own,
         4 * own * slim,
-        where, *outer, near, part,
+        where, *outer[2:], near, part,
     )
     lags = lags + across(lags, 1, 0)
     first = call(

time: 60.1 us -> 58.8 us (0.978)
  waiting for transfers between devices: 14.2 us -> 12.6 us
  starting transfers between devices: 31.8 us -> 32.9 us
  other arithmetic: 1.29 us -> 0.6 us
    ppermute x14, waiting for transfers between devices: 12.6 us -> 10.8 us  [swap(): return lax.ppermute(value, 'ctx', [(i, i ^ step) for i in range(count)])]
    ppermute x14, starting transfers between devices: 27 us -> 28.4 us  [swap(): return lax.ppermute(value, 'ctx', [(i, i ^ step) for i in range(count)])]
    pad x1 -> x0, other arithmetic: 0.68 us -> none  [halves_plan(): taps = jnp.pad(filters.astype(jnp.float32), ((0, 8 - nfil), (0, 0)))]
    pallas_call x8 -> x7, Pallas kernels: 11.9 us -> 11.7 us  [call(): pl.pallas_call(kernel, out_shape=outs, in_specs=[pl.BlockSpec(memory_spac...]
  transfers between devices with their start and end apart: 18 -> 18, of which waited for: 8 -> 9; matrix products, arithmetic and copies ran while one was open for 0% -> 0% of each run, Pallas kernels for 16% -> 17%
where the time goes in v3:
time: 58.8 us; the launch traced here: 58.6 us
  starting transfers between devices  32.9 us (56%)
  waiting for transfers between devices  12.6 us (21%)
  Pallas kernels  11.7 us (20%)
  between operations  0.79 us (1%)
  other arithmetic  0.6 us (1%)
    ppermute x14, starting transfers between devices, swap(): return lax.ppermute(value, 'ctx', [(i, i ^ step) for i in range(count)])  28.4 us
    pallas_call x7, Pallas kernels, call(): pl.pallas_call(kernel, out_shape=outs, in_specs=[pl.BlockSpec(memory_spac...  11.7 us
    ppermute x14, waiting for transfers between devices, swap(): return lax.ppermute(value, 'ctx', [(i, i ^ step) for i in range(count)])  10.8 us
    ppermute x4, starting transfers between devices, halves_plan(): lax.ppermute(value, ('chan', 'ctx'), [(c * count + i, (c ^ move) * count...  4.52 us
    ppermute x4, waiting for transfers between devices, halves_plan(): lax.ppermute(value, ('chan', 'ctx'), [(c * count + i, (c ^ move) * count...  1.8 us
  transfers between devices with their start and end apart: 18, of which 9 were waited for; matrix products, arithmetic and copies ran while one was open for 0% of the time, Pallas kernels for 17%

profile of v3, /device:TPU:0, one launch (start us, length us, event | category | flops | bytes accessed | tf_op | source)
XLA Modules:
  0.0 58.6 jit_solution(5912787194699679348)
XLA Ops:
  0.6 4.1 %collective-permute-start = (bf16[4,128]{1,0:T(4,128)(2,1)}, bf16[4,128]{1,0:T(4,128)(2,1)S(1)}, u32[]{:S(2)}, u32[]{:S(2)}) collective-permute-start(bf16[4,128]{1,0:T(4,128)(2,1)} %mine_ref.1), channel_id=1, source_target_pairs={{0,4},{1,5},{2,6},{3,7},{4,0},{5,1},{6,2},{7,3},{8,12},{9,13},{10,... | collective-permute-start | bytes 3080 | tf_op jit(solution)/shard_map/ppermute | solution.py:295
  4.7 2.2 %shard_map.92 = (bf16[128,512]{1,0:T(8,128)(2,1)S(1)}, bf16[128,512]{1,0:T(8,128)(2,1)S(1)}, bf16[128,512]{1,0:T(8,128)(2,1)S(1)}, bf16[128,512]{1,0:T(8,128)(2,1)S(1)}, bf16[4,2,128,512]{3,2,1,0:T(8,128)(2,1)S(1)}) custom-call(s32[1]{0:T(128)} %bitcast.me_ref, bf16[128,2048]{1,0:T(8,128)(2,1)} %q_ref.3, bf16[128,2048]{1,0:T(8,128)(2,1)} %k_ref.3, ...), custom_call_target="tpu_custom_call" | custom-call | flops 67108864 | bytes 3670016 | tf_op jit(solution)/shard_map/pallas_call | solution.py:305
  7.0 0.4 shard_map.93
  7.4 1.6 %collective-permute-start.1 = (bf16[272,512]{1,0:T(8,128)(2,1)S(1)}, bf16[272,512]{1,0:T(8,128)(2,1)S(1)}, u32[]{:S(2)}, u32[]{:S(2)}) collective-permute-start(bf16[272,512]{1,0:T(8,128)(2,1)S(1)} %get-tuple-element.42), channel_id=1, source_target_pairs={{0,1},{1,0},{2,3},{3,2},{4,5},{5,4},{6,7},{7,6},{8,9},{9,8},{10,11... | collective-permute-start | bytes 835592 | tf_op jit(solution)/shard_map/ppermute | solution.py:295
  9.0 1.6 %collective-permute-start.3 = (bf16[272,512]{1,0:T(8,128)(2,1)S(1)}, bf16[272,512]{1,0:T(8,128)(2,1)S(1)}, u32[]{:S(2)}, u32[]{:S(2)}) collective-permute-start(bf16[272,512]{1,0:T(8,128)(2,1)S(1)} %get-tuple-element.45), channel_id=1, source_target_pairs={{0,2},{1,3},{2,0},{3,1},{4,6},{5,7},{6,4},{7,5},{8,10},{9,11},{10,... | collective-permute-start | bytes 835592 | tf_op jit(solution)/shard_map/ppermute | solution.py:295
  10.6 0.4 collective-permute-start.5
  10.9 2.5 %collective-permute-start.6 = (bf16[128,512]{1,0:T(8,128)(2,1)S(1)}, bf16[128,512]{1,0:T(8,128)(2,1)S(1)}, u32[]{:S(2)}, u32[]{:S(2)}) collective-permute-start(bf16[128,512]{1,0:T(8,128)(2,1)S(1)} %get-tuple-element.51), channel_id=1, source_target_pairs={{0,4},{1,5},{2,6},{3,7},{4,0},{5,1},{6,2},{7,3},{8,12},{9,13},{10,... | collective-permute-start | bytes 393224 | tf_op jit(solution)/shard_map/ppermute | solution.py:295
  13.4 1.4 %collective-permute-start.7 = (bf16[128,512]{1,0:T(8,128)(2,1)S(1)}, bf16[128,512]{1,0:T(8,128)(2,1)S(1)}, u32[]{:S(2)}, u32[]{:S(2)}) collective-permute-start(bf16[128,512]{1,0:T(8,128)(2,1)S(1)} %get-tuple-element.52), channel_id=1, source_target_pairs={{0,5},{1,4},{2,7},{3,6},{4,1},{5,0},{6,3},{7,2},{8,13},{9,12},{10,... | collective-permute-start | bytes 393224 | tf_op jit(solution)/shard_map/ppermute | solution.py:295
  14.8 0.8 %collective-permute-done.1.refs_1_ = bf16[272,512]{1,0:T(8,128)(2,1)S(1)} collective-permute-done((bf16[272,512]{1,0:T(8,128)(2,1)S(1)}, bf16[272,512]{1,0:T(8,128)(2,1)S(1)}, u32[]{:S(2)}, u32[]{:S(2)}) %collective-permute-start.1) | collective-permute-done | bytes 278560 | tf_op jit(solution)/shard_map/ppermute | solution.py:295
  15.6 2.9 %collective-permute-start.2 = (bf16[128,512]{1,0:T(8,128)(2,1)S(1)}, bf16[128,512]{1,0:T(8,128)(2,1)S(1)}, u32[]{:S(2)}, u32[]{:S(2)}) collective-permute-start(bf16[128,512]{1,0:T(8,128)(2,1)S(1)} %get-tuple-element.43), channel_id=1, source_target_pairs={{0,6},{1,7},{2,4},{3,5},{4,2},{5,3},{6,0},{7,1},{8,14},{9,15},{10,... | collective-permute-start | bytes 393224 | tf_op jit(solution)/shard_map/ppermute | solution.py:295
  18.5 5.7 %collective-permute-done.3.refs_2_ = bf16[272,512]{1,0:T(8,128)(2,1)S(1)} collective-permute-done((bf16[272,512]{1,0:T(8,128)(2,1)S(1)}, bf16[272,512]{1,0:T(8,128)(2,1)S(1)}, u32[]{:S(2)}, u32[]{:S(2)}) %collective-permute-start.3) | collective-permute-done | bytes 278560 | tf_op jit(solution)/shard_map/ppermute | solution.py:295
  24.2 3.4 %collective-permute-start.4 = (bf16[128,512]{1,0:T(8,128)(2,1)S(1)}, bf16[128,512]{1,0:T(8,128)(2,1)S(1)}, u32[]{:S(2)}, u32[]{:S(2)}) collective-permute-start(bf16[128,512]{1,0:T(8,128)(2,1)S(1)} %get-tuple-element.46), channel_id=1, source_target_pairs={{0,7},{1,6},{2,5},{3,4},{4,3},{5,2},{6,1},{7,0},{8,15},{9,14},{10,... | collective-permute-start | bytes 393224 | tf_op jit(solution)/shard_map/ppermute | solution.py:295
  27.6 1.7 %collective-permute-done.7.refs_5_ = bf16[128,512]{1,0:T(8,128)(2,1)S(1)} collective-permute-done((bf16[128,512]{1,0:T(8,128)(2,1)S(1)}, bf16[128,512]{1,0:T(8,128)(2,1)S(1)}, u32[]{:S(2)}, u32[]{:S(2)}) %collective-permute-start.7) | collective-permute-done | bytes 131104 | tf_op jit(solution)/shard_map/ppermute | solution.py:295
  29.3 0.5 collective-permute-done.5.refs_3_
  29.9 5.4 %shard_map.94 = (bf16[128,512]{1,0:T(8,128)(2,1)S(1)}, bf16[128,512]{1,0:T(8,128)(2,1)S(1)}, bf16[128,512]{1,0:T(8,128)(2,1)S(1)}, bf16[128,512]{1,0:T(8,128)(2,...) custom-call(s32[1]{0:T(128)} %bitcast.me_ref, ...), custom_call_target="tpu_custom_call" | custom-call | flops 4294967296 | bytes 2097152 | tf_op jit(solution)/shard_map/pallas_call | solution.py:305
  35.2 1.0 %shard_map.95 = f32[8,1024]{1,0:T(8,128)S(1)} custom-call(s32[1]{0:T(128)} %bitcast.me_ref, bf16[128,512]{1,0:T(8,128)(2,1)S(1)} %collective-permute-done.2.refs_0_, bf16[128,512]{1,0:T(8,128)(2,1)S(1)} %collective-permute-done.4.refs_1_, bf16[512,512]{1,0:T(8,128)(2,1)S(1)} %get-tuple-element.53.refs_2_, f32[8,1024]{1,0:T(8,128)S(1)} %get-tuple-element.54.refs_3_), custom_call_target="tpu_custom_call" | custom-call | flops 268435456 | bytes 262144 | tf_op jit(solution)/shard_map/pallas_call | solution.py:305
  36.4 0.8 %shard_map.96 = (bf16[144,512]{1,0:T(8,128)(2,1)S(1)}, bf16[144,512]{1,0:T(8,128)(2,1)S(1)}, bf16[144,512]{1,0:T(8,128)(2,1)S(1)}, bf16[144,512]{1,0:T(8,128)(2,1)S(1)}) custom-call(s32[1]{0:T(128)} %bitcast.me_ref, bf16[128,512]{1,0:T(8,128)(2,1)S(1)} %collective-permute-done.2.refs_0_, bf16[128,512]{1,0:T(8,128)(2,1)S(1)} %collective-permute-done.4.refs_1_, ...), custom_call_target="tpu_custom_call" | custom-call | flops 536870912 | bytes 1048576 | tf_op jit(solution)/shard_map/pallas_call | solution.py:305
  37.2 0.3 collective-permute-done.8
  37.7 1.6 %collective-permute-start.9 = (bf16[144,512]{1,0:T(8,128)(2,1)S(1)}, bf16[144,512]{1,0:T(8,128)(2,1)S(1)}, u32[]{:S(2)}, u32[]{:S(2)}) collective-permute-start(bf16[144,512]{1,0:T(8,128)(2,1)S(1)} %get-tuple-element.64), channel_id=1, source_target_pairs={{0,1},{1,0},{2,3},{3,2},{4,5},{5,4},{6,7},{7,6},{8,9},{9,8},{10,11... | collective-permute-start | bytes 442376 | tf_op jit(solution)/shard_map/ppermute | solution.py:295
  39.3 2.8 %collective-permute-start.10 = (bf16[144,512]{1,0:T(8,128)(2,1)S(1)}, bf16[144,512]{1,0:T(8,128)(2,1)S(1)}, u32[]{:S(2)}, u32[]{:S(2)}) collective-permute-start(bf16[144,512]{1,0:T(8,128)(2,1)S(1)} %get-tuple-element.65), channel_id=1, source_target_pairs={{0,2},{1,3},{2,0},{3,1},{4,6},{5,7},{6,4},{7,5},{8,10},{9,11},{10,... | collective-permute-start | bytes 442376 | tf_op jit(solution)/shard_map/ppermute | solution.py:295
  42.1 1.5 %collective-permute-start.12 = (bf16[128,512]{1,0:T(8,128)(2,1)S(1)}, bf16[128,512]{1,0:T(8,128)(2,1)S(1)}, u32[]{:S(2)}, u32[]{:S(2)}) collective-permute-start(bf16[128,512]{1,0:T(8,128)(2,1)S(1)} %get-tuple-element.68), channel_id=1, source_target_pairs={{0,1},{1,0},{2,3},{3,2},{4,5},{5,4},{6,7},{7,6},{8,9},{9,8},{10,11... | collective-permute-start | bytes 393224 | tf_op jit(solution)/shard_map/ppermute | solution.py:295
  43.6 2.0 %collective-permute-start.13 = (bf16[128,512]{1,0:T(8,128)(2,1)S(1)}, bf16[128,512]{1,0:T(8,128)(2,1)S(1)}, u32[]{:S(2)}, u32[]{:S(2)}) collective-permute-start(bf16[128,512]{1,0:T(8,128)(2,1)S(1)} %get-tuple-element.69), channel_id=1, source_target_pairs={{0,2},{1,3},{2,0},{3,1},{4,6},{5,7},{6,4},{7,5},{8,10},{9,11},{10,... | collective-permute-start | bytes 393224 | tf_op jit(solution)/shard_map/ppermute | solution.py:295
  45.6 2.6 %collective-permute-start.14 = (bf16[128,512]{1,0:T(8,128)(2,1)S(1)}, bf16[128,512]{1,0:T(8,128)(2,1)S(1)}, u32[]{:S(2)}, u32[]{:S(2)}) collective-permute-start(bf16[128,512]{1,0:T(8,128)(2,1)S(1)} %get-tuple-element.70), channel_id=1, source_target_pairs={{0,3},{1,2},{2,1},{3,0},{4,7},{5,6},{6,5},{7,4},{8,11},{9,10},{10,... | collective-permute-start | bytes 393224 | tf_op jit(solution)/shard_map/ppermute | solution.py:295
  48.3 1.6 %collective-permute-done.11.refs_3_ = bf16[144,512]{1,0:T(8,128)(2,1)S(1)} collective-permute-done((bf16[144,512]{1,0:T(8,128)(2,1)S(1)}, bf16[144,512]{1,0:T(8,128)(2,1)S(1)}, u32[]{:S(2)}, u32[]{:S(2)}) %collective-permute-start.11) | collective-permute-done | bytes 147488 | tf_op jit(solution)/shard_map/ppermute | solution.py:295
  49.8 3.7 %collective-permute-start.17 = (f32[4,128]{1,0:T(4,128)S(1)}, f32[4,128]{1,0:T(4,128)S(1)}, u32[]{:S(2)}, u32[]{:S(2)}) collective-permute-start(f32[4,128]{1,0:T(4,128)S(1)} %get-tuple-element.76), channel_id=1, source_target_pairs={{0,20},{1,21},{2,22},{3,23},{4,16},{5,17},{6,18},{7,19},{8,28},{9,... | collective-permute-start | bytes 6152 | tf_op jit(solution)/shard_map/ppermute | solution.py:385
  53.5 0.2 collective-permute-start.15
  53.8 0.5 collective-permute-start.16
  54.3 0.5 collective-permute-done.14.refs_7_
  54.8 1.8 %shard_map.98 = (bf16[128,2048]{1,0:T(8,128)(2,1)}, bf16[128,2048]{1,0:T(8,128)(2,1)}, bf16[128,2048]{1,0:T(8,128)(2,1)}, bf16[128,2048]{1,0:T(8,128)(2,1)}) custom-call(s32[1]{0:T(128)} %bitcast.me_ref, bf16[128,2048]{1,0:T(8,128)(2,1)S(1)} %copy-done, bf16[128,2048]{1,0:T(8,128)(2,1)S(1)} %copy-done.1, bf16[128,2048]{1,0:T(8,128)(2,1)S(1)} %copy-done.2, ...), custom_call_target="tpu_custom_call" | custom-call | flops 134217728 | bytes 5242880 | tf_op jit(solution)/shard_map/pallas_call | solution.py:305
  56.6 0.8 %collective-permute-done.16 = f32[4,128]{1,0:T(4,128)S(1)} collective-permute-done((f32[4,128]{1,0:T(4,128)S(1)}, f32[4,128]{1,0:T(4,128)S(1)}, u32[]{:S(2)}, u32[]{:S(2)}) %collective-permute-start.16) | collective-permute-done | bytes 2080 | tf_op jit(solution)/shard_map/ppermute | solution.py:385
  57.4 0.7 %collective-permute-done.15 = f32[4,128]{1,0:T(4,128)S(1)} collective-permute-done((f32[4,128]{1,0:T(4,128)S(1)}, f32[4,128]{1,0:T(4,128)S(1)}, u32[]{:S(2)}, u32[]{:S(2)}) %collective-permute-start.15) | collective-permute-done | bytes 2080 | tf_op jit(solution)/shard_map/ppermute | solution.py:385
  58.0 0.6 add_multiply_fusion
  (26 shorter events, 0.3 us)
Async XLA Ops:
  0.6 6.3 %copy-start.4 = (bf16[4,128]{1,0:T(4,128)(2,1)S(1)}, bf16[4,128]{1,0:T(4,128)(2,1)}, u32[]{:S(2)}) copy-start(bf16[4,128]{1,0:T(4,128)(2,1)} %mine_ref.1) | copy-start | bytes 3076
  0.6 6.3 %collective-permute-start = (bf16[4,128]{1,0:T(4,128)(2,1)}, bf16[4,128]{1,0:T(4,128)(2,1)S(1)}, u32[]{:S(2)}, u32[]{:S(2)}) collective-permute-start(bf16[4,128]{1,0:T(4,128)(2,1)} %mine_ref.1), channel_id=1, source_target_pairs={{0,4},{1,5},{2,6},{3,7},{4,0},{5,1},{6,2},{7,3},{8,12},{9,13},{10,... | collective-permute-start | bytes 3080 | tf_op jit(solution)/shard_map/ppermute | solution.py:295
  7.4 8.2 %collective-permute-start.1 = (bf16[272,512]{1,0:T(8,128)(2,1)S(1)}, bf16[272,512]{1,0:T(8,128)(2,1)S(1)}, u32[]{:S(2)}, u32[]{:S(2)}) collective-permute-start(bf16[272,512]{1,0:T(8,128)(2,1)S(1)} %get-tuple-element.42), channel_id=1, source_target_pairs={{0,1},{1,0},{2,3},{3,2},{4,5},{5,4},{6,7},{7,6},{8,9},{9,8},{10,11... | collective-permute-start | bytes 835592 | tf_op jit(solution)/shard_map/ppermute | solution.py:295
  9.0 15.2 %collective-permute-start.3 = (bf16[272,512]{1,0:T(8,128)(2,1)S(1)}, bf16[272,512]{1,0:T(8,128)(2,1)S(1)}, u32[]{:S(2)}, u32[]{:S(2)}) collective-permute-start(bf16[272,512]{1,0:T(8,128)(2,1)S(1)} %get-tuple-element.45), channel_id=1, source_target_pairs={{0,2},{1,3},{2,0},{3,1},{4,6},{5,7},{6,4},{7,5},{8,10},{9,11},{10,... | collective-permute-start | bytes 835592 | tf_op jit(solution)/shard_map/ppermute | solution.py:295
  10.6 19.3 %collective-permute-start.5 = (bf16[272,512]{1,0:T(8,128)(2,1)S(1)}, bf16[272,512]{1,0:T(8,128)(2,1)S(1)}, u32[]{:S(2)}, u32[]{:S(2)}) collective-permute-start(bf16[272,512]{1,0:T(8,128)(2,1)S(1)} %get-tuple-element.50), channel_id=1, source_target_pairs={{0,3},{1,2},{2,1},{3,0},{4,7},{5,6},{6,5},{7,4},{8,11},{9,10},{10,... | collective-permute-start | bytes 835592 | tf_op jit(solution)/shard_map/ppermute | solution.py:295
  10.9 16.7 %collective-permute-start.6 = (bf16[128,512]{1,0:T(8,128)(2,1)S(1)}, bf16[128,512]{1,0:T(8,128)(2,1)S(1)}, u32[]{:S(2)}, u32[]{:S(2)}) collective-permute-start(bf16[128,512]{1,0:T(8,128)(2,1)S(1)} %get-tuple-element.51), channel_id=1, source_target_pairs={{0,4},{1,5},{2,6},{3,7},{4,0},{5,1},{6,2},{7,3},{8,12},{9,13},{10,... | collective-permute-start | bytes 393224 | tf_op jit(solution)/shard_map/ppermute | solution.py:295
  13.4 15.9 %collective-permute-start.7 = (bf16[128,512]{1,0:T(8,128)(2,1)S(1)}, bf16[128,512]{1,0:T(8,128)(2,1)S(1)}, u32[]{:S(2)}, u32[]{:S(2)}) collective-permute-start(bf16[128,512]{1,0:T(8,128)(2,1)S(1)} %get-tuple-element.52), channel_id=1, source_target_pairs={{0,5},{1,4},{2,7},{3,6},{4,1},{5,0},{6,3},{7,2},{8,13},{9,12},{10,... | collective-permute-start | bytes 393224 | tf_op jit(solution)/shard_map/ppermute | solution.py:295
  15.6 19.6 %collective-permute-start.2 = (bf16[128,512]{1,0:T(8,128)(2,1)S(1)}, bf16[128,512]{1,0:T(8,128)(2,1)S(1)}, u32[]{:S(2)}, u32[]{:S(2)}) collective-permute-start(bf16[128,512]{1,0:T(8,128)(2,1)S(1)} %get-tuple-element.43), channel_id=1, source_target_pairs={{0,6},{1,7},{2,4},{3,5},{4,2},{5,3},{6,0},{7,1},{8,14},{9,15},{10,... | collective-permute-start | bytes 393224 | tf_op jit(solution)/shard_map/ppermute | solution.py:295
  24.2 11.0 %collective-permute-start.4 = (bf16[128,512]{1,0:T(8,128)(2,1)S(1)}, bf16[128,512]{1,0:T(8,128)(2,1)S(1)}, u32[]{:S(2)}, u32[]{:S(2)}) collective-permute-start(bf16[128,512]{1,0:T(8,128)(2,1)S(1)} %get-tuple-element.46), channel_id=1, source_target_pairs={{0,7},{1,6},{2,5},{3,4},{4,3},{5,2},{6,1},{7,0},{8,15},{9,14},{10,... | collective-permute-start | bytes 393224 | tf_op jit(solution)/shard_map/ppermute | solution.py:295
  36.3 1.3 %collective-permute-start.8 = (f32[8,1024]{1,0:T(8,128)S(1)}, f32[8,1024]{1,0:T(8,128)S(1)}, u32[]{:S(2)}, u32[]{:S(2)}) collective-permute-start(f32[8,1024]{1,0:T(8,128)S(1)} %shard_map.95), channel_id=1, source_target_pairs={{0,8},{1,9},{2,10},{3,11},{4,12},{5,13},{6,14},{7,15},{8,0},{9,1},... | collective-permute-start | bytes 98312 | tf_op jit(solution)/shard_map/ppermute | solution.py:385
  36.4 18.4 %copy-start = (bf16[128,2048]{1,0:T(8,128)(2,1)S(1)}, bf16[128,2048]{1,0:T(8,128)(2,1)}, u32[]{:S(2)}) copy-start(bf16[128,2048]{1,0:T(8,128)(2,1)} %q_ref.3) | copy-start | bytes 1572868
  36.4 18.4 %copy-start.1 = (bf16[128,2048]{1,0:T(8,128)(2,1)S(1)}, bf16[128,2048]{1,0:T(8,128)(2,1)}, u32[]{:S(2)}) copy-start(bf16[128,2048]{1,0:T(8,128)(2,1)} %k_ref.3) | copy-start | bytes 1572868
  36.4 18.4 %copy-start.2 = (bf16[128,2048]{1,0:T(8,128)(2,1)S(1)}, bf16[128,2048]{1,0:T(8,128)(2,1)}, u32[]{:S(2)}) copy-start(bf16[128,2048]{1,0:T(8,128)(2,1)} %v_ref.3) | copy-start | bytes 1572868
  36.4 18.4 %copy-start.3 = (bf16[128,2048]{1,0:T(8,128)(2,1)S(1)}, bf16[128,2048]{1,0:T(8,128)(2,1)}, u32[]{:S(2)}) copy-start(bf16[128,2048]{1,0:T(8,128)(2,1)} %g_ref.3) | copy-start | bytes 1572868
  37.7 7.9 %collective-permute-start.9 = (bf16[144,512]{1,0:T(8,128)(2,1)S(1)}, bf16[144,512]{1,0:T(8,128)(2,1)S(1)}, u32[]{:S(2)}, u32[]{:S(2)}) collective-permute-start(bf16[144,512]{1,0:T(8,128)(2,1)S(1)} %get-tuple-element.64), channel_id=1, source_target_pairs={{0,1},{1,0},{2,3},{3,2},{4,5},{5,4},{6,7},{7,6},{8,9},{9,8},{10,11... | collective-permute-start | bytes 442376 | tf_op jit(solution)/shard_map/ppermute | solution.py:295
  39.3 8.9 %collective-permute-start.10 = (bf16[144,512]{1,0:T(8,128)(2,1)S(1)}, bf16[144,512]{1,0:T(8,128)(2,1)S(1)}, u32[]{:S(2)}, u32[]{:S(2)}) collective-permute-start(bf16[144,512]{1,0:T(8,128)(2,1)S(1)} %get-tuple-element.65), channel_id=1, source_target_pairs={{0,2},{1,3},{2,0},{3,1},{4,6},{5,7},{6,4},{7,5},{8,10},{9,11},{10,... | collective-permute-start | bytes 442376 | tf_op jit(solution)/shard_map/ppermute | solution.py:295
  42.1 7.7 %collective-permute-start.11 = (bf16[144,512]{1,0:T(8,128)(2,1)S(1)}, bf16[144,512]{1,0:T(8,128)(2,1)S(1)}, u32[]{:S(2)}, u32[]{:S(2)}) collective-permute-start(bf16[144,512]{1,0:T(8,128)(2,1)S(1)} %get-tuple-element.66), channel_id=1, source_target_pairs={{0,3},{1,2},{2,1},{3,0},{4,7},{5,6},{6,5},{7,4},{8,11},{9,10},{10,... | collective-permute-start | bytes 442376 | tf_op jit(solution)/shard_map/ppermute | solution.py:295
  42.1 11.7 %collective-permute-start.12 = (bf16[128,512]{1,0:T(8,128)(2,1)S(1)}, bf16[128,512]{1,0:T(8,128)(2,1)S(1)}, u32[]{:S(2)}, u32[]{:S(2)}) collective-permute-start(bf16[128,512]{1,0:T(8,128)(2,1)S(1)} %get-tuple-element.68), channel_id=1, source_target_pairs={{0,1},{1,0},{2,3},{3,2},{4,5},{5,4},{6,7},{7,6},{8,9},{9,8},{10,11... | collective-permute-start | bytes 393224 | tf_op jit(solution)/shard_map/ppermute | solution.py:295
  43.6 10.7 %collective-permute-start.13 = (bf16[128,512]{1,0:T(8,128)(2,1)S(1)}, bf16[128,512]{1,0:T(8,128)(2,1)S(1)}, u32[]{:S(2)}, u32[]{:S(2)}) collective-permute-start(bf16[128,512]{1,0:T(8,128)(2,1)S(1)} %get-tuple-element.69), channel_id=1, source_target_pairs={{0,2},{1,3},{2,0},{3,1},{4,6},{5,7},{6,4},{7,5},{8,10},{9,11},{10,... | collective-permute-start | bytes 393224 | tf_op jit(solution)/shard_map/ppermute | solution.py:295
  45.6 9.2 %collective-permute-start.14 = (bf16[128,512]{1,0:T(8,128)(2,1)S(1)}, bf16[128,512]{1,0:T(8,128)(2,1)S(1)}, u32[]{:S(2)}, u32[]{:S(2)}) collective-permute-start(bf16[128,512]{1,0:T(8,128)(2,1)S(1)} %get-tuple-element.70), channel_id=1, source_target_pairs={{0,3},{1,2},{2,1},{3,0},{4,7},{5,6},{6,5},{7,4},{8,11},{9,10},{10,... | collective-permute-start | bytes 393224 | tf_op jit(solution)/shard_map/ppermute | solution.py:295
  49.8 7.5 %collective-permute-start.17 = (f32[4,128]{1,0:T(4,128)S(1)}, f32[4,128]{1,0:T(4,128)S(1)}, u32[]{:S(2)}, u32[]{:S(2)}) collective-permute-start(f32[4,128]{1,0:T(4,128)S(1)} %get-tuple-element.76), channel_id=1, source_target_pairs={{0,20},{1,21},{2,22},{3,23},{4,16},{5,17},{6,18},{7,19},{8,28},{9,... | collective-permute-start | bytes 6152 | tf_op jit(solution)/shard_map/ppermute | solution.py:385
  53.5 4.5 %collective-permute-start.15 = (f32[4,128]{1,0:T(4,128)S(1)}, f32[4,128]{1,0:T(4,128)S(1)}, u32[]{:S(2)}, u32[]{:S(2)}) collective-permute-start(f32[4,128]{1,0:T(4,128)S(1)} %get-tuple-element.76), channel_id=1, source_target_pairs={{0,4},{1,5},{2,6},{3,7},{4,0},{5,1},{6,2},{7,3},{8,12},{9,13},{10,... | collective-permute-start | bytes 6152 | tf_op jit(solution)/shard_map/ppermute | solution.py:385
  53.8 3.6 %collective-permute-start.16 = (f32[4,128]{1,0:T(4,128)S(1)}, f32[4,128]{1,0:T(4,128)S(1)}, u32[]{:S(2)}, u32[]{:S(2)}) collective-permute-start(f32[4,128]{1,0:T(4,128)S(1)} %get-tuple-element.75), channel_id=1, source_target_pairs={{0,16},{1,17},{2,18},{3,19},{4,20},{5,21},{6,22},{7,23},{8,24},{9,... | collective-permute-start | bytes 6152 | tf_op jit(solution)/shard_map/ppermute | solution.py:385

commit v4 on v3

--- a/solution.py
+++ b/solution.py
@@ -30,21 +30,23 @@
     me = me_ref[0]
     upper = me >= half
     copies = []
-    for step in range(half):
-        part = (me ^ step) & (half - 1)
-        lanes = pl.ds(pl.multiple_of(part * slim, LANES), slim)
+    for chunk in range(half // 2):
+        base = (((me & (half - 1)) // 2) ^ chunk) * 2 * slim
+        lanes = pl.ds(pl.multiple_of(base, LANES), 2 * slim)
         copies.append([])
         for index, ref in enumerate((q_ref, k_ref, v_ref, g_ref)):
             copy = pltpu.make_async_copy(
-                ref.at[:, lanes], held.at[step, index], sems.at[step, index]
+                ref.at[:, lanes], held.at[chunk, index], sems.at[chunk, index]
             )
             copy.start()
-            copies[step].append(copy)
+            copies[chunk].append(copy)
     turn_other = exchange(rows, jnp.logical_not(upper), jnp.bfloat16)
     for step in range(half):
-        for copy in copies[step]:
-            copy.wait()
-        q, k, v, g = [held[step, index].astype(jnp.float32) for index in range(4)]
+        if step % 2 == 0:
+            for copy in copies[step // 2]:
+                copy.wait()
+        lanes = pl.ds(pl.multiple_of(((me ^ step) & 1) * slim, LANES), slim)
+        q, k, v, g = [held[step // 2, index, :, lanes].astype(jnp.float32) for index in range(4)]
         gated = (k * v).astype(jnp.bfloat16)
         back = (g * q).astype(jnp.bfloat16)
         second = jnp.where(upper, back, gated)
@@ -99,12 +101,17 @@
     return lax.dot_general(left, right, contract, preferred_element_type=jnp.float32)
 
 
-def placed(values, start, width):
-    rows, reach = values.shape
-    pieces = [values, jnp.zeros((rows, width - start - reach), jnp.float32)]
-    if start:
-        pieces = [jnp.zeros((rows, start), jnp.float32)] + pieces
-    return jnp.concatenate(pieces, axis=1)
+def add_columns(columns, values, start):
+    first = start // LANES
+    for index in range(values.shape[1] // LANES):
+        piece = values[:, index * LANES : (index + 1) * LANES]
+        have = columns[first + index]
+        columns[first + index] = piece if have is None else have + piece
+
+
+def joined_columns(columns, rows):
+    blank = jnp.zeros((rows, LANES), jnp.float32)
+    return jnp.concatenate([blank if c is None else c for c in columns], axis=1)
 
 
 def diagonal_rows(acc):
@@ -132,11 +139,11 @@
     lanes = pl.ds(pl.multiple_of(jnp.where(me >= half, share, 0), LANES), share)
     for index in range(NFILT):
         right = pair_ref[:, lanes] * lane_mask(share, NFILT, index)
-        acc = jnp.zeros((rows, window), jnp.float32)
+        columns = [None] * (window // LANES)
+        every = products(flip_ref[:, lanes], right)
         for start in range(0, own, rows):
-            left = flip_ref[start : start + rows, lanes]
-            acc = acc + placed(products(left, right), own - rows - start, window)
-        sums = pltpu.roll(diagonal_rows(acc), 1, 1)
+            add_columns(columns, every[start : start + rows, :], own - rows - start)
+        sums = pltpu.roll(diagonal_rows(joined_columns(columns, rows)), 1, 1)
         lag_ref[index : index + 1, pl.ds(base, window)] += sums[0:1, :]
 
 
@@ -200,13 +207,11 @@
         part_ref[top : top + size, :] = acc
     lag_ref[...] = jnp.zeros((8, total), jnp.float32)
     for index in range(nfil):
-        acc = jnp.zeros((rows, own + rows), jnp.float32)
+        columns = [None] * ((own + rows) // LANES)
+        every = products(flip_ref[...], first_ref[...] * masks[index])
         for start in range(0, own, rows):
-            right = first_ref[start:own, :] * masks[index]
-            acc = acc + placed(
-                products(flip_ref[start : start + rows, :], right), 0, own + rows
-            )
-        sums = pltpu.roll(diagonal_rows(acc), own + 1, 1)
+            add_columns(columns, every[start : start + rows, start:own], 0)
+        sums = pltpu.roll(diagonal_rows(joined_columns(columns, rows)), own + 1, 1)
         lag_ref[index : index + 1, 0:own] = sums[0:1, 0:own]
     outer_lags(half, me, base, pair_ref, flip_ref, lag_ref)
 
@@ -338,7 +343,7 @@
     *sent, pair = call(
         functools.partial(gate_kernel, half, slim),
         [shape((rows, slim), low)] * half + [shape((half, 2, rows, slim), low)],
-        [pltpu.VMEM((half, 4, rows, slim), low), pltpu.SemaphoreType.DMA((half, 4))],
+        [pltpu.VMEM((half // 2, 4, rows, 2 * slim), low), pltpu.SemaphoreType.DMA((half // 2, 4))],
         2 * rows * rows * width,
         14 * rows * width,
         where, *branches, far=4,

time: 58.8 us -> 58.2 us (0.990)
  Pallas kernels: 11.7 us -> 10.3 us
    pallas_call x7, Pallas kernels: 11.7 us -> 10.3 us  [call(): pl.pallas_call(kernel, out_shape=outs, in_specs=[pl.BlockSpec(memory_spac...]
  transfers between devices with their start and end apart: 18 -> 18, of which waited for: 9 -> 10; matrix products, arithmetic and copies ran while one was open for 0% -> 0% of each run, Pallas kernels for 17% -> 16%
where the time goes in v4:
time: 58.2 us; the launch traced here: 58.1 us
  starting transfers between devices  33.2 us (57%)
  waiting for transfers between devices  13.1 us (23%)
  Pallas kernels  10.3 us (18%)
  between operations  0.79 us (1%)
  other arithmetic  0.6 us (1%)
    ppermute x14, starting transfers between devices, swap(): return lax.ppermute(value, 'ctx', [(i, i ^ step) for i in range(count)])  28.4 us
    ppermute x14, waiting for transfers between devices, swap(): return lax.ppermute(value, 'ctx', [(i, i ^ step) for i in range(count)])  10.9 us
    pallas_call x7, Pallas kernels, call(): pl.pallas_call(kernel, out_shape=outs, in_specs=[pl.BlockSpec(memory_spac...  10.3 us
    ppermute x4, starting transfers between devices, halves_plan(): lax.ppermute(value, ('chan', 'ctx'), [(c * count + i, (c ^ move) * count...  4.79 us
    ppermute x4, waiting for transfers between devices, halves_plan(): lax.ppermute(value, ('chan', 'ctx'), [(c * count + i, (c ^ move) * count...  2.28 us
  transfers between devices with their start and end apart: 18, of which 10 were waited for; matrix products, arithmetic and copies ran while one was open for 0% of the time, Pallas kernels for 16%

profile of v4, /device:TPU:0, one launch (start us, length us, event | category | flops | bytes accessed | tf_op | source)
XLA Modules:
  0.0 58.1 jit_solution(4863811514969786308)
XLA Ops:
  0.6 4.1 %collective-permute-start = (bf16[4,128]{1,0:T(4,128)(2,1)}, bf16[4,128]{1,0:T(4,128)(2,1)S(1)}, u32[]{:S(2)}, u32[]{:S(2)}) collective-permute-start(bf16[4,128]{1,0:T(4,128)(2,1)} %mine_ref.1), channel_id=1, source_target_pairs={{0,4},{1,5},{2,6},{3,7},{4,0},{5,1},{6,2},{7,3},{8,12},{9,13},{10,... | collective-permute-start | bytes 3080 | tf_op jit(solution)/shard_map/ppermute | solution.py:300
  4.7 1.9 %shard_map.92 = (bf16[128,512]{1,0:T(8,128)(2,1)S(1)}, bf16[128,512]{1,0:T(8,128)(2,1)S(1)}, bf16[128,512]{1,0:T(8,128)(2,1)S(1)}, bf16[128,512]{1,0:T(8,128)(2,1)S(1)}, bf16[4,2,128,512]{3,2,1,0:T(8,128)(2,1)S(1)}) custom-call(s32[1]{0:T(128)} %bitcast.me_ref, bf16[128,2048]{1,0:T(8,128)(2,1)} %q_ref.3, bf16[128,2048]{1,0:T(8,128)(2,1)} %k_ref.3, ...), custom_call_target="tpu_custom_call" | custom-call | flops 67108864 | bytes 3670016 | tf_op jit(solution)/shard_map/pallas_call | solution.py:310
  6.7 0.4 shard_map.93
  7.1 1.7 %collective-permute-start.1 = (bf16[272,512]{1,0:T(8,128)(2,1)S(1)}, bf16[272,512]{1,0:T(8,128)(2,1)S(1)}, u32[]{:S(2)}, u32[]{:S(2)}) collective-permute-start(bf16[272,512]{1,0:T(8,128)(2,1)S(1)} %get-tuple-element.42), channel_id=1, source_target_pairs={{0,1},{1,0},{2,3},{3,2},{4,5},{5,4},{6,7},{7,6},{8,9},{9,8},{10,11... | collective-permute-start | bytes 835592 | tf_op jit(solution)/shard_map/ppermute | solution.py:300
  8.8 1.6 %collective-permute-start.3 = (bf16[272,512]{1,0:T(8,128)(2,1)S(1)}, bf16[272,512]{1,0:T(8,128)(2,1)S(1)}, u32[]{:S(2)}, u32[]{:S(2)}) collective-permute-start(bf16[272,512]{1,0:T(8,128)(2,1)S(1)} %get-tuple-element.45), channel_id=1, source_target_pairs={{0,2},{1,3},{2,0},{3,1},{4,6},{5,7},{6,4},{7,5},{8,10},{9,11},{10,... | collective-permute-start | bytes 835592 | tf_op jit(solution)/shard_map/ppermute | solution.py:300
  10.4 0.2 collective-permute-start.5
  10.7 2.7 %collective-permute-start.6 = (bf16[128,512]{1,0:T(8,128)(2,1)S(1)}, bf16[128,512]{1,0:T(8,128)(2,1)S(1)}, u32[]{:S(2)}, u32[]{:S(2)}) collective-permute-start(bf16[128,512]{1,0:T(8,128)(2,1)S(1)} %get-tuple-element.51), channel_id=1, source_target_pairs={{0,4},{1,5},{2,6},{3,7},{4,0},{5,1},{6,2},{7,3},{8,12},{9,13},{10,... | collective-permute-start | bytes 393224 | tf_op jit(solution)/shard_map/ppermute | solution.py:300
  13.4 1.3 %collective-permute-start.7 = (bf16[128,512]{1,0:T(8,128)(2,1)S(1)}, bf16[128,512]{1,0:T(8,128)(2,1)S(1)}, u32[]{:S(2)}, u32[]{:S(2)}) collective-permute-start(bf16[128,512]{1,0:T(8,128)(2,1)S(1)} %get-tuple-element.52), channel_id=1, source_target_pairs={{0,5},{1,4},{2,7},{3,6},{4,1},{5,0},{6,3},{7,2},{8,13},{9,12},{10,... | collective-permute-start | bytes 393224 | tf_op jit(solution)/shard_map/ppermute | solution.py:300
  14.7 0.6 %collective-permute-done.1.refs_1_ = bf16[272,512]{1,0:T(8,128)(2,1)S(1)} collective-permute-done((bf16[272,512]{1,0:T(8,128)(2,1)S(1)}, bf16[272,512]{1,0:T(8,128)(2,1)S(1)}, u32[]{:S(2)}, u32[]{:S(2)}) %collective-permute-start.1) | collective-permute-done | bytes 278560 | tf_op jit(solution)/shard_map/ppermute | solution.py:300
  15.3 3.3 %collective-permute-start.2 = (bf16[128,512]{1,0:T(8,128)(2,1)S(1)}, bf16[128,512]{1,0:T(8,128)(2,1)S(1)}, u32[]{:S(2)}, u32[]{:S(2)}) collective-permute-start(bf16[128,512]{1,0:T(8,128)(2,1)S(1)} %get-tuple-element.43), channel_id=1, source_target_pairs={{0,6},{1,7},{2,4},{3,5},{4,2},{5,3},{6,0},{7,1},{8,14},{9,15},{10,... | collective-permute-start | bytes 393224 | tf_op jit(solution)/shard_map/ppermute | solution.py:300
  18.6 5.4 %collective-permute-done.3.refs_2_ = bf16[272,512]{1,0:T(8,128)(2,1)S(1)} collective-permute-done((bf16[272,512]{1,0:T(8,128)(2,1)S(1)}, bf16[272,512]{1,0:T(8,128)(2,1)S(1)}, u32[]{:S(2)}, u32[]{:S(2)}) %collective-permute-start.3) | collective-permute-done | bytes 278560 | tf_op jit(solution)/shard_map/ppermute | solution.py:300
  24.1 3.5 %collective-permute-start.4 = (bf16[128,512]{1,0:T(8,128)(2,1)S(1)}, bf16[128,512]{1,0:T(8,128)(2,1)S(1)}, u32[]{:S(2)}, u32[]{:S(2)}) collective-permute-start(bf16[128,512]{1,0:T(8,128)(2,1)S(1)} %get-tuple-element.46), channel_id=1, source_target_pairs={{0,7},{1,6},{2,5},{3,4},{4,3},{5,2},{6,1},{7,0},{8,15},{9,14},{10,... | collective-permute-start | bytes 393224 | tf_op jit(solution)/shard_map/ppermute | solution.py:300
  27.6 1.6 %collective-permute-done.7.refs_5_ = bf16[128,512]{1,0:T(8,128)(2,1)S(1)} collective-permute-done((bf16[128,512]{1,0:T(8,128)(2,1)S(1)}, bf16[128,512]{1,0:T(8,128)(2,1)S(1)}, u32[]{:S(2)}, u32[]{:S(2)}) %collective-permute-start.7) | collective-permute-done | bytes 131104 | tf_op jit(solution)/shard_map/ppermute | solution.py:300
  29.2 0.1 collective-permute-done.5.refs_3_
  29.3 4.5 %shard_map.94 = (bf16[128,512]{1,0:T(8,128)(2,1)S(1)}, bf16[128,512]{1,0:T(8,128)(2,1)S(1)}, bf16[128,512]{1,0:T(8,128)(2,1)S(1)}, bf16[128,512]{1,0:T(8,128)(2,...) custom-call(s32[1]{0:T(128)} %bitcast.me_ref, ...), custom_call_target="tpu_custom_call" | custom-call | flops 4294967296 | bytes 2097152 | tf_op jit(solution)/shard_map/pallas_call | solution.py:310
  33.9 1.2 %collective-permute-done.4.refs_1_ = bf16[128,512]{1,0:T(8,128)(2,1)S(1)} collective-permute-done((bf16[128,512]{1,0:T(8,128)(2,1)S(1)}, bf16[128,512]{1,0:T(8,128)(2,1)S(1)}, u32[]{:S(2)}, u32[]{:S(2)}) %collective-permute-start.4) | collective-permute-done | bytes 131104 | tf_op jit(solution)/shard_map/ppermute | solution.py:300
  35.1 0.8 %shard_map.95 = f32[8,1024]{1,0:T(8,128)S(1)} custom-call(s32[1]{0:T(128)} %bitcast.me_ref, bf16[128,512]{1,0:T(8,128)(2,1)S(1)} %collective-permute-done.2.refs_0_, bf16[128,512]{1,0:T(8,128)(2,1)S(1)} %collective-permute-done.4.refs_1_, bf16[512,512]{1,0:T(8,128)(2,1)S(1)} %get-tuple-element.53.refs_2_, f32[8,1024]{1,0:T(8,128)S(1)} %get-tuple-element.54.refs_3_), custom_call_target="tpu_custom_call" | custom-call | flops 268435456 | bytes 262144 | tf_op jit(solution)/shard_map/pallas_call | solution.py:310
  36.0 0.8 %shard_map.96 = (bf16[144,512]{1,0:T(8,128)(2,1)S(1)}, bf16[144,512]{1,0:T(8,128)(2,1)S(1)}, bf16[144,512]{1,0:T(8,128)(2,1)S(1)}, bf16[144,512]{1,0:T(8,128)(2,1)S(1)}) custom-call(s32[1]{0:T(128)} %bitcast.me_ref, bf16[128,512]{1,0:T(8,128)(2,1)S(1)} %collective-permute-done.2.refs_0_, bf16[128,512]{1,0:T(8,128)(2,1)S(1)} %collective-permute-done.4.refs_1_, ...), custom_call_target="tpu_custom_call" | custom-call | flops 536870912 | bytes 1048576 | tf_op jit(solution)/shard_map/pallas_call | solution.py:310
  36.8 0.3 collective-permute-done.8
  37.1 0.2 shard_map.97
  37.3 1.6 %collective-permute-start.9 = (bf16[144,512]{1,0:T(8,128)(2,1)S(1)}, bf16[144,512]{1,0:T(8,128)(2,1)S(1)}, u32[]{:S(2)}, u32[]{:S(2)}) collective-permute-start(bf16[144,512]{1,0:T(8,128)(2,1)S(1)} %get-tuple-element.64), channel_id=1, source_target_pairs={{0,1},{1,0},{2,3},{3,2},{4,5},{5,4},{6,7},{7,6},{8,9},{9,8},{10,11... | collective-permute-start | bytes 442376 | tf_op jit(solution)/shard_map/ppermute | solution.py:300
  38.9 2.1 %collective-permute-start.10 = (bf16[144,512]{1,0:T(8,128)(2,1)S(1)}, bf16[144,512]{1,0:T(8,128)(2,1)S(1)}, u32[]{:S(2)}, u32[]{:S(2)}) collective-permute-start(bf16[144,512]{1,0:T(8,128)(2,1)S(1)} %get-tuple-element.65), channel_id=1, source_target_pairs={{0,2},{1,3},{2,0},{3,1},{4,6},{5,7},{6,4},{7,5},{8,10},{9,11},{10,... | collective-permute-start | bytes 442376 | tf_op jit(solution)/shard_map/ppermute | solution.py:300
  41.0 1.4 %collective-permute-start.12 = (bf16[128,512]{1,0:T(8,128)(2,1)S(1)}, bf16[128,512]{1,0:T(8,128)(2,1)S(1)}, u32[]{:S(2)}, u32[]{:S(2)}) collective-permute-start(bf16[128,512]{1,0:T(8,128)(2,1)S(1)} %get-tuple-element.68), channel_id=1, source_target_pairs={{0,1},{1,0},{2,3},{3,2},{4,5},{5,4},{6,7},{7,6},{8,9},{9,8},{10,11... | collective-permute-start | bytes 393224 | tf_op jit(solution)/shard_map/ppermute | solution.py:300
  42.5 2.0 %collective-permute-start.13 = (bf16[128,512]{1,0:T(8,128)(2,1)S(1)}, bf16[128,512]{1,0:T(8,128)(2,1)S(1)}, u32[]{:S(2)}, u32[]{:S(2)}) collective-permute-start(bf16[128,512]{1,0:T(8,128)(2,1)S(1)} %get-tuple-element.69), channel_id=1, source_target_pairs={{0,2},{1,3},{2,0},{3,1},{4,6},{5,7},{6,4},{7,5},{8,10},{9,11},{10,... | collective-permute-start | bytes 393224 | tf_op jit(solution)/shard_map/ppermute | solution.py:300
  44.5 2.6 %collective-permute-start.14 = (bf16[128,512]{1,0:T(8,128)(2,1)S(1)}, bf16[128,512]{1,0:T(8,128)(2,1)S(1)}, u32[]{:S(2)}, u32[]{:S(2)}) collective-permute-start(bf16[128,512]{1,0:T(8,128)(2,1)S(1)} %get-tuple-element.70), channel_id=1, source_target_pairs={{0,3},{1,2},{2,1},{3,0},{4,7},{5,6},{6,5},{7,4},{8,11},{9,10},{10,... | collective-permute-start | bytes 393224 | tf_op jit(solution)/shard_map/ppermute | solution.py:300
  47.1 1.8 %collective-permute-done.11.refs_3_ = bf16[144,512]{1,0:T(8,128)(2,1)S(1)} collective-permute-done((bf16[144,512]{1,0:T(8,128)(2,1)S(1)}, bf16[144,512]{1,0:T(8,128)(2,1)S(1)}, u32[]{:S(2)}, u32[]{:S(2)}) %collective-permute-start.11) | collective-permute-done | bytes 147488 | tf_op jit(solution)/shard_map/ppermute | solution.py:300
  48.9 4.1 %collective-permute-start.17 = (f32[4,128]{1,0:T(4,128)S(1)}, f32[4,128]{1,0:T(4,128)S(1)}, u32[]{:S(2)}, u32[]{:S(2)}) collective-permute-start(f32[4,128]{1,0:T(4,128)S(1)} %get-tuple-element.76), channel_id=1, source_target_pairs={{0,20},{1,21},{2,22},{3,23},{4,16},{5,17},{6,18},{7,19},{8,28},{9,... | collective-permute-start | bytes 6152 | tf_op jit(solution)/shard_map/ppermute | solution.py:390
  53.0 0.6 %collective-permute-start.16 = (f32[4,128]{1,0:T(4,128)S(1)}, f32[4,128]{1,0:T(4,128)S(1)}, u32[]{:S(2)}, u32[]{:S(2)}) collective-permute-start(f32[4,128]{1,0:T(4,128)S(1)} %get-tuple-element.75), channel_id=1, source_target_pairs={{0,16},{1,17},{2,18},{3,19},{4,20},{5,21},{6,22},{7,23},{8,24},{9,... | collective-permute-start | bytes 6152 | tf_op jit(solution)/shard_map/ppermute | solution.py:390
  53.8 1.8 %shard_map.98 = (bf16[128,2048]{1,0:T(8,128)(2,1)}, bf16[128,2048]{1,0:T(8,128)(2,1)}, bf16[128,2048]{1,0:T(8,128)(2,1)}, bf16[128,2048]{1,0:T(8,128)(2,1)}) custom-call(s32[1]{0:T(128)} %bitcast.me_ref, bf16[128,2048]{1,0:T(8,128)(2,1)S(1)} %copy-done, bf16[128,2048]{1,0:T(8,128)(2,1)S(1)} %copy-done.1, bf16[128,2048]{1,0:T(8,128)(2,1)S(1)} %copy-done.2, ...), custom_call_target="tpu_custom_call" | custom-call | flops 134217728 | bytes 5242880 | tf_op jit(solution)/shard_map/pallas_call | solution.py:310
  55.6 1.0 %collective-permute-done.16 = f32[4,128]{1,0:T(4,128)S(1)} collective-permute-done((f32[4,128]{1,0:T(4,128)S(1)}, f32[4,128]{1,0:T(4,128)S(1)}, u32[]{:S(2)}, u32[]{:S(2)}) %collective-permute-start.16) | collective-permute-done | bytes 2080 | tf_op jit(solution)/shard_map/ppermute | solution.py:390
  56.6 0.9 %collective-permute-done.15 = f32[4,128]{1,0:T(4,128)S(1)} collective-permute-done((f32[4,128]{1,0:T(4,128)S(1)}, f32[4,128]{1,0:T(4,128)S(1)}, u32[]{:S(2)}, u32[]{:S(2)}) %collective-permute-start.15) | collective-permute-done | bytes 2080 | tf_op jit(solution)/shard_map/ppermute | solution.py:390
  57.5 0.6 %add_multiply_fusion = f32[4,128]{1,0:T(4,128)} fusion(f32[4,128]{1,0:T(4,128)S(1)} %collective-permute-done.17, f32[4,128]{1,0:T(4,128)S(1)} %collective-permute-done.15, f32[4,128]{1,0:T(4,128)S(1)} %collective-permute-done.16, f32[8,128]{1,0:T(8,128)S(1)} %slice_add_fusion), kind=kLoop, calls=%fused_computation.2 | loop fusion | flops 2048 | bytes 10240 | tf_op jit(solution)/shard_map/mul | solution.py:427
  (26 shorter events, 0.3 us)
Async XLA Ops:
  0.6 6.1 %copy-start.4 = (bf16[4,128]{1,0:T(4,128)(2,1)S(1)}, bf16[4,128]{1,0:T(4,128)(2,1)}, u32[]{:S(2)}) copy-start(bf16[4,128]{1,0:T(4,128)(2,1)} %mine_ref.1) | copy-start | bytes 3076
  0.6 6.0 %collective-permute-start = (bf16[4,128]{1,0:T(4,128)(2,1)}, bf16[4,128]{1,0:T(4,128)(2,1)S(1)}, u32[]{:S(2)}, u32[]{:S(2)}) collective-permute-start(bf16[4,128]{1,0:T(4,128)(2,1)} %mine_ref.1), channel_id=1, source_target_pairs={{0,4},{1,5},{2,6},{3,7},{4,0},{5,1},{6,2},{7,3},{8,12},{9,13},{10,... | collective-permute-start | bytes 3080 | tf_op jit(solution)/shard_map/ppermute | solution.py:300
  7.1 8.2 %collective-permute-start.1 = (bf16[272,512]{1,0:T(8,128)(2,1)S(1)}, bf16[272,512]{1,0:T(8,128)(2,1)S(1)}, u32[]{:S(2)}, u32[]{:S(2)}) collective-permute-start(bf16[272,512]{1,0:T(8,128)(2,1)S(1)} %get-tuple-element.42), channel_id=1, source_target_pairs={{0,1},{1,0},{2,3},{3,2},{4,5},{5,4},{6,7},{7,6},{8,9},{9,8},{10,11... | collective-permute-start | bytes 835592 | tf_op jit(solution)/shard_map/ppermute | solution.py:300
  8.8 15.2 %collective-permute-start.3 = (bf16[272,512]{1,0:T(8,128)(2,1)S(1)}, bf16[272,512]{1,0:T(8,128)(2,1)S(1)}, u32[]{:S(2)}, u32[]{:S(2)}) collective-permute-start(bf16[272,512]{1,0:T(8,128)(2,1)S(1)} %get-tuple-element.45), channel_id=1, source_target_pairs={{0,2},{1,3},{2,0},{3,1},{4,6},{5,7},{6,4},{7,5},{8,10},{9,11},{10,... | collective-permute-start | bytes 835592 | tf_op jit(solution)/shard_map/ppermute | solution.py:300
  10.4 18.9 %collective-permute-start.5 = (bf16[272,512]{1,0:T(8,128)(2,1)S(1)}, bf16[272,512]{1,0:T(8,128)(2,1)S(1)}, u32[]{:S(2)}, u32[]{:S(2)}) collective-permute-start(bf16[272,512]{1,0:T(8,128)(2,1)S(1)} %get-tuple-element.50), channel_id=1, source_target_pairs={{0,3},{1,2},{2,1},{3,0},{4,7},{5,6},{6,5},{7,4},{8,11},{9,10},{10,... | collective-permute-start | bytes 835592 | tf_op jit(solution)/shard_map/ppermute | solution.py:300
  10.7 16.9 %collective-permute-start.6 = (bf16[128,512]{1,0:T(8,128)(2,1)S(1)}, bf16[128,512]{1,0:T(8,128)(2,1)S(1)}, u32[]{:S(2)}, u32[]{:S(2)}) collective-permute-start(bf16[128,512]{1,0:T(8,128)(2,1)S(1)} %get-tuple-element.51), channel_id=1, source_target_pairs={{0,4},{1,5},{2,6},{3,7},{4,0},{5,1},{6,2},{7,3},{8,12},{9,13},{10,... | collective-permute-start | bytes 393224 | tf_op jit(solution)/shard_map/ppermute | solution.py:300
  13.4 15.8 %collective-permute-start.7 = (bf16[128,512]{1,0:T(8,128)(2,1)S(1)}, bf16[128,512]{1,0:T(8,128)(2,1)S(1)}, u32[]{:S(2)}, u32[]{:S(2)}) collective-permute-start(bf16[128,512]{1,0:T(8,128)(2,1)S(1)} %get-tuple-element.52), channel_id=1, source_target_pairs={{0,5},{1,4},{2,7},{3,6},{4,1},{5,0},{6,3},{7,2},{8,13},{9,12},{10,... | collective-permute-start | bytes 393224 | tf_op jit(solution)/shard_map/ppermute | solution.py:300
  15.3 18.5 %collective-permute-start.2 = (bf16[128,512]{1,0:T(8,128)(2,1)S(1)}, bf16[128,512]{1,0:T(8,128)(2,1)S(1)}, u32[]{:S(2)}, u32[]{:S(2)}) collective-permute-start(bf16[128,512]{1,0:T(8,128)(2,1)S(1)} %get-tuple-element.43), channel_id=1, source_target_pairs={{0,6},{1,7},{2,4},{3,5},{4,2},{5,3},{6,0},{7,1},{8,14},{9,15},{10,... | collective-permute-start | bytes 393224 | tf_op jit(solution)/shard_map/ppermute | solution.py:300
  24.1 11.0 %collective-permute-start.4 = (bf16[128,512]{1,0:T(8,128)(2,1)S(1)}, bf16[128,512]{1,0:T(8,128)(2,1)S(1)}, u32[]{:S(2)}, u32[]{:S(2)}) collective-permute-start(bf16[128,512]{1,0:T(8,128)(2,1)S(1)} %get-tuple-element.46), channel_id=1, source_target_pairs={{0,7},{1,6},{2,5},{3,4},{4,3},{5,2},{6,1},{7,0},{8,15},{9,14},{10,... | collective-permute-start | bytes 393224 | tf_op jit(solution)/shard_map/ppermute | solution.py:300
  35.8 1.3 %collective-permute-start.8 = (f32[8,1024]{1,0:T(8,128)S(1)}, f32[8,1024]{1,0:T(8,128)S(1)}, u32[]{:S(2)}, u32[]{:S(2)}) collective-permute-start(f32[8,1024]{1,0:T(8,128)S(1)} %shard_map.95), channel_id=1, source_target_pairs={{0,8},{1,9},{2,10},{3,11},{4,12},{5,13},{6,14},{7,15},{8,0},{9,1},... | collective-permute-start | bytes 98312 | tf_op jit(solution)/shard_map/ppermute | solution.py:390
  35.9 17.8 %copy-start = (bf16[128,2048]{1,0:T(8,128)(2,1)S(1)}, bf16[128,2048]{1,0:T(8,128)(2,1)}, u32[]{:S(2)}) copy-start(bf16[128,2048]{1,0:T(8,128)(2,1)} %q_ref.3) | copy-start | bytes 1572868
  35.9 17.8 %copy-start.1 = (bf16[128,2048]{1,0:T(8,128)(2,1)S(1)}, bf16[128,2048]{1,0:T(8,128)(2,1)}, u32[]{:S(2)}) copy-start(bf16[128,2048]{1,0:T(8,128)(2,1)} %k_ref.3) | copy-start | bytes 1572868
  36.0 17.8 %copy-start.2 = (bf16[128,2048]{1,0:T(8,128)(2,1)S(1)}, bf16[128,2048]{1,0:T(8,128)(2,1)}, u32[]{:S(2)}) copy-start(bf16[128,2048]{1,0:T(8,128)(2,1)} %v_ref.3) | copy-start | bytes 1572868
  36.0 17.8 %copy-start.3 = (bf16[128,2048]{1,0:T(8,128)(2,1)S(1)}, bf16[128,2048]{1,0:T(8,128)(2,1)}, u32[]{:S(2)}) copy-start(bf16[128,2048]{1,0:T(8,128)(2,1)} %g_ref.3) | copy-start | bytes 1572868
  37.3 7.2 %collective-permute-start.9 = (bf16[144,512]{1,0:T(8,128)(2,1)S(1)}, bf16[144,512]{1,0:T(8,128)(2,1)S(1)}, u32[]{:S(2)}, u32[]{:S(2)}) collective-permute-start(bf16[144,512]{1,0:T(8,128)(2,1)S(1)} %get-tuple-element.64), channel_id=1, source_target_pairs={{0,1},{1,0},{2,3},{3,2},{4,5},{5,4},{6,7},{7,6},{8,9},{9,8},{10,11... | collective-permute-start | bytes 442376 | tf_op jit(solution)/shard_map/ppermute | solution.py:300
  38.9 8.3 %collective-permute-start.10 = (bf16[144,512]{1,0:T(8,128)(2,1)S(1)}, bf16[144,512]{1,0:T(8,128)(2,1)S(1)}, u32[]{:S(2)}, u32[]{:S(2)}) collective-permute-start(bf16[144,512]{1,0:T(8,128)(2,1)S(1)} %get-tuple-element.65), channel_id=1, source_target_pairs={{0,2},{1,3},{2,0},{3,1},{4,6},{5,7},{6,4},{7,5},{8,10},{9,11},{10,... | collective-permute-start | bytes 442376 | tf_op jit(solution)/shard_map/ppermute | solution.py:300
  41.0 7.9 %collective-permute-start.11 = (bf16[144,512]{1,0:T(8,128)(2,1)S(1)}, bf16[144,512]{1,0:T(8,128)(2,1)S(1)}, u32[]{:S(2)}, u32[]{:S(2)}) collective-permute-start(bf16[144,512]{1,0:T(8,128)(2,1)S(1)} %get-tuple-element.66), channel_id=1, source_target_pairs={{0,3},{1,2},{2,1},{3,0},{4,7},{5,6},{6,5},{7,4},{8,11},{9,10},{10,... | collective-permute-start | bytes 442376 | tf_op jit(solution)/shard_map/ppermute | solution.py:300
  41.0 12.0 %collective-permute-start.12 = (bf16[128,512]{1,0:T(8,128)(2,1)S(1)}, bf16[128,512]{1,0:T(8,128)(2,1)S(1)}, u32[]{:S(2)}, u32[]{:S(2)}) collective-permute-start(bf16[128,512]{1,0:T(8,128)(2,1)S(1)} %get-tuple-element.68), channel_id=1, source_target_pairs={{0,1},{1,0},{2,3},{3,2},{4,5},{5,4},{6,7},{7,6},{8,9},{9,8},{10,11... | collective-permute-start | bytes 393224 | tf_op jit(solution)/shard_map/ppermute | solution.py:300
  42.5 11.2 %collective-permute-start.13 = (bf16[128,512]{1,0:T(8,128)(2,1)S(1)}, bf16[128,512]{1,0:T(8,128)(2,1)S(1)}, u32[]{:S(2)}, u32[]{:S(2)}) collective-permute-start(bf16[128,512]{1,0:T(8,128)(2,1)S(1)} %get-tuple-element.69), channel_id=1, source_target_pairs={{0,2},{1,3},{2,0},{3,1},{4,6},{5,7},{6,4},{7,5},{8,10},{9,11},{10,... | collective-permute-start | bytes 393224 | tf_op jit(solution)/shard_map/ppermute | solution.py:300
  44.5 9.3 %collective-permute-start.14 = (bf16[128,512]{1,0:T(8,128)(2,1)S(1)}, bf16[128,512]{1,0:T(8,128)(2,1)S(1)}, u32[]{:S(2)}, u32[]{:S(2)}) collective-permute-start(bf16[128,512]{1,0:T(8,128)(2,1)S(1)} %get-tuple-element.70), channel_id=1, source_target_pairs={{0,3},{1,2},{2,1},{3,0},{4,7},{5,6},{6,5},{7,4},{8,11},{9,10},{10,... | collective-permute-start | bytes 393224 | tf_op jit(solution)/shard_map/ppermute | solution.py:300
  48.9 7.7 %collective-permute-start.17 = (f32[4,128]{1,0:T(4,128)S(1)}, f32[4,128]{1,0:T(4,128)S(1)}, u32[]{:S(2)}, u32[]{:S(2)}) collective-permute-start(f32[4,128]{1,0:T(4,128)S(1)} %get-tuple-element.76), channel_id=1, source_target_pairs={{0,20},{1,21},{2,22},{3,23},{4,16},{5,17},{6,18},{7,19},{8,28},{9,... | collective-permute-start | bytes 6152 | tf_op jit(solution)/shard_map/ppermute | solution.py:390
  53.0 4.5 %collective-permute-start.15 = (f32[4,128]{1,0:T(4,128)S(1)}, f32[4,128]{1,0:T(4,128)S(1)}, u32[]{:S(2)}, u32[]{:S(2)}) collective-permute-start(f32[4,128]{1,0:T(4,128)S(1)} %get-tuple-element.76), channel_id=1, source_target_pairs={{0,4},{1,5},{2,6},{3,7},{4,0},{5,1},{6,2},{7,3},{8,12},{9,13},{10,... | collective-permute-start | bytes 6152 | tf_op jit(solution)/shard_map/ppermute | solution.py:390
  53.0 3.6 %collective-permute-start.16 = (f32[4,128]{1,0:T(4,128)S(1)}, f32[4,128]{1,0:T(4,128)S(1)}, u32[]{:S(2)}, u32[]{:S(2)}) collective-permute-start(f32[4,128]{1,0:T(4,128)S(1)} %get-tuple-element.75), channel_id=1, source_target_pairs={{0,16},{1,17},{2,18},{3,19},{4,20},{5,21},{6,22},{7,23},{8,24},{9,... | collective-permute-start | bytes 6152 | tf_op jit(solution)/shard_map/ppermute | solution.py:390

commit v5 on v4

--- a/solution.py
+++ b/solution.py
@@ -268,7 +268,8 @@
 
 
 def final_kernel(half, slim, me_ref, q_ref, k_ref, v_ref, g_ref, *refs):
-    firsts, seconds = refs[:half], refs[half : 2 * half]
+    firsts = [refs[0], *refs[half - 1 : 0 : -1]]
+    seconds = [refs[half], *refs[2 * half - 1 : half : -1]]
     outs = refs[2 * half : 2 * half + 4]
     held, sems = refs[2 * half + 4 :]
     rows = q_ref.shape[0]
@@ -386,7 +387,7 @@
         8 * own * slim,
         where, *inner, *outer[:2],
     )
-    second = [second[0]] + [swap(second[k], k, count) for k in range(1, half)]
+    second = [second[0]] + [swap(second[k], k, count) for k in range(half - 1, 0, -1)][::-1]
     across = lambda value, move, turn: lax.ppermute(
         value,
         ("chan", "ctx"),
@@ -418,7 +419,7 @@
         32 * slim * half,
         where, lags, *first, alias=half, far_out=True,
     )
-    first = [first[0]] + [swap(first[k], k, count) for k in range(1, half)]
+    first = [first[0]] + [swap(first[k], k, count) for k in range(half - 1, 0, -1)][::-1]
     sums = sum(value[rows:, 0:LANES].astype(jnp.float32) for value in first)
     sums = sums[: 2 * nfil] + sums[2 * nfil :]
     mine, other = sums[:nfil], sums[nfil:]
@@ -432,7 +433,7 @@
         [pltpu.VMEM((half, 4, rows, slim), low), pltpu.SemaphoreType.DMA((half, 4))],
         4 * rows * rows * width,
         20 * rows * width,
-        where, queries, keys, values, cotangent, *first, *second, far_out=True,
+        where, queries, keys, values, cotangent, first[0], *first[:0:-1], second[0], *second[:0:-1], far_out=True,
     )
     return (*outs, filter_grad)
 

time: 58.2 us -> 57.7 us (level)
  starting transfers between devices: 33.2 us -> 31.4 us
  waiting for transfers between devices: 13.1 us -> 14.4 us
    ppermute x14, starting transfers between devices: 28.4 us -> 26.6 us  [swap(): return lax.ppermute(value, 'ctx', [(i, i ^ step) for i in range(count)])]
    ppermute x14, waiting for transfers between devices: 10.9 us -> 12.2 us  [swap(): return lax.ppermute(value, 'ctx', [(i, i ^ step) for i in range(count)])]
  transfers between devices with their start and end apart: 18 -> 18, of which waited for: 10 -> 12; matrix products, arithmetic and copies ran while one was open for 0% -> 0% of each run, Pallas kernels for 16% -> 16%
where the time goes in v5:
time: 57.7 us; the launch traced here: 57.5 us
  starting transfers between devices  31.4 us (54%)
  waiting for transfers between devices  14.4 us (25%)
  Pallas kernels  10.3 us (18%)
  between operations  0.79 us (1%)
  other arithmetic  0.6 us (1%)
    ppermute x14, starting transfers between devices, swap(): return lax.ppermute(value, 'ctx', [(i, i ^ step) for i in range(count)])  26.6 us
    ppermute x14, waiting for transfers between devices, swap(): return lax.ppermute(value, 'ctx', [(i, i ^ step) for i in range(count)])  12.2 us
    pallas_call x7, Pallas kernels, call(): pl.pallas_call(kernel, out_shape=outs, in_specs=[pl.BlockSpec(memory_spac...  10.3 us
    ppermute x4, starting transfers between devices, halves_plan(): lax.ppermute(value, ('chan', 'ctx'), [(c * count + i, (c ^ move) * count...  4.83 us
    ppermute x4, waiting for transfers between devices, halves_plan(): lax.ppermute(value, ('chan', 'ctx'), [(c * count + i, (c ^ move) * count...  2.13 us
  transfers between devices with their start and end apart: 18, of which 12 were waited for; matrix products, arithmetic and copies ran while one was open for 0% of the time, Pallas kernels for 16%

profile of v5, /device:TPU:0, one launch (start us, length us, event | category | flops | bytes accessed | tf_op | source)
XLA Modules:
  0.0 57.5 jit_solution(323773902372977926)
XLA Ops:
  0.6 4.1 %collective-permute-start = (bf16[4,128]{1,0:T(4,128)(2,1)}, bf16[4,128]{1,0:T(4,128)(2,1)S(1)}, u32[]{:S(2)}, u32[]{:S(2)}) collective-permute-start(bf16[4,128]{1,0:T(4,128)(2,1)} %mine_ref.1), channel_id=1, source_target_pairs={{0,4},{1,5},{2,6},{3,7},{4,0},{5,1},{6,2},{7,3},{8,12},{9,13},{10,... | collective-permute-start | bytes 3080 | tf_op jit(solution)/shard_map/ppermute | solution.py:301
  4.7 1.9 %shard_map.92 = (bf16[128,512]{1,0:T(8,128)(2,1)S(1)}, bf16[128,512]{1,0:T(8,128)(2,1)S(1)}, bf16[128,512]{1,0:T(8,128)(2,1)S(1)}, bf16[128,512]{1,0:T(8,128)(2,1)S(1)}, bf16[4,2,128,512]{3,2,1,0:T(8,128)(2,1)S(1)}) custom-call(s32[1]{0:T(128)} %bitcast.me_ref, bf16[128,2048]{1,0:T(8,128)(2,1)} %q_ref.3, bf16[128,2048]{1,0:T(8,128)(2,1)} %k_ref.3, ...), custom_call_target="tpu_custom_call" | custom-call | flops 67108864 | bytes 3670016 | tf_op jit(solution)/shard_map/pallas_call | solution.py:311
  6.7 0.4 shard_map.93
  7.1 1.7 %collective-permute-start.1 = (bf16[272,512]{1,0:T(8,128)(2,1)S(1)}, bf16[272,512]{1,0:T(8,128)(2,1)S(1)}, u32[]{:S(2)}, u32[]{:S(2)}) collective-permute-start(bf16[272,512]{1,0:T(8,128)(2,1)S(1)} %get-tuple-element.42), channel_id=1, source_target_pairs={{0,1},{1,0},{2,3},{3,2},{4,5},{5,4},{6,7},{7,6},{8,9},{9,8},{10,11... | collective-permute-start | bytes 835592 | tf_op jit(solution)/shard_map/ppermute | solution.py:301
  8.8 1.6 %collective-permute-start.3 = (bf16[272,512]{1,0:T(8,128)(2,1)S(1)}, bf16[272,512]{1,0:T(8,128)(2,1)S(1)}, u32[]{:S(2)}, u32[]{:S(2)}) collective-permute-start(bf16[272,512]{1,0:T(8,128)(2,1)S(1)} %get-tuple-element.45), channel_id=1, source_target_pairs={{0,2},{1,3},{2,0},{3,1},{4,6},{5,7},{6,4},{7,5},{8,10},{9,11},{10,... | collective-permute-start | bytes 835592 | tf_op jit(solution)/shard_map/ppermute | solution.py:301
  10.4 0.2 collective-permute-start.5
  10.7 2.7 %collective-permute-start.6 = (bf16[128,512]{1,0:T(8,128)(2,1)S(1)}, bf16[128,512]{1,0:T(8,128)(2,1)S(1)}, u32[]{:S(2)}, u32[]{:S(2)}) collective-permute-start(bf16[128,512]{1,0:T(8,128)(2,1)S(1)} %get-tuple-element.51), channel_id=1, source_target_pairs={{0,4},{1,5},{2,6},{3,7},{4,0},{5,1},{6,2},{7,3},{8,12},{9,13},{10,... | collective-permute-start | bytes 393224 | tf_op jit(solution)/shard_map/ppermute | solution.py:301
  13.4 1.3 %collective-permute-start.7 = (bf16[128,512]{1,0:T(8,128)(2,1)S(1)}, bf16[128,512]{1,0:T(8,128)(2,1)S(1)}, u32[]{:S(2)}, u32[]{:S(2)}) collective-permute-start(bf16[128,512]{1,0:T(8,128)(2,1)S(1)} %get-tuple-element.52), channel_id=1, source_target_pairs={{0,5},{1,4},{2,7},{3,6},{4,1},{5,0},{6,3},{7,2},{8,13},{9,12},{10,... | collective-permute-start | bytes 393224 | tf_op jit(solution)/shard_map/ppermute | solution.py:301
  14.7 0.6 %collective-permute-done.1.refs_1_ = bf16[272,512]{1,0:T(8,128)(2,1)S(1)} collective-permute-done((bf16[272,512]{1,0:T(8,128)(2,1)S(1)}, bf16[272,512]{1,0:T(8,128)(2,1)S(1)}, u32[]{:S(2)}, u32[]{:S(2)}) %collective-permute-start.1) | collective-permute-done | bytes 278560 | tf_op jit(solution)/shard_map/ppermute | solution.py:301
  15.3 3.3 %collective-permute-start.2 = (bf16[128,512]{1,0:T(8,128)(2,1)S(1)}, bf16[128,512]{1,0:T(8,128)(2,1)S(1)}, u32[]{:S(2)}, u32[]{:S(2)}) collective-permute-start(bf16[128,512]{1,0:T(8,128)(2,1)S(1)} %get-tuple-element.43), channel_id=1, source_target_pairs={{0,6},{1,7},{2,4},{3,5},{4,2},{5,3},{6,0},{7,1},{8,14},{9,15},{10,... | collective-permute-start | bytes 393224 | tf_op jit(solution)/shard_map/ppermute | solution.py:301
  18.6 5.4 %collective-permute-done.3.refs_2_ = bf16[272,512]{1,0:T(8,128)(2,1)S(1)} collective-permute-done((bf16[272,512]{1,0:T(8,128)(2,1)S(1)}, bf16[272,512]{1,0:T(8,128)(2,1)S(1)}, u32[]{:S(2)}, u32[]{:S(2)}) %collective-permute-start.3) | collective-permute-done | bytes 278560 | tf_op jit(solution)/shard_map/ppermute | solution.py:301
  24.1 3.5 %collective-permute-start.4 = (bf16[128,512]{1,0:T(8,128)(2,1)S(1)}, bf16[128,512]{1,0:T(8,128)(2,1)S(1)}, u32[]{:S(2)}, u32[]{:S(2)}) collective-permute-start(bf16[128,512]{1,0:T(8,128)(2,1)S(1)} %get-tuple-element.46), channel_id=1, source_target_pairs={{0,7},{1,6},{2,5},{3,4},{4,3},{5,2},{6,1},{7,0},{8,15},{9,14},{10,... | collective-permute-start | bytes 393224 | tf_op jit(solution)/shard_map/ppermute | solution.py:301
  27.6 1.6 %collective-permute-done.7.refs_5_ = bf16[128,512]{1,0:T(8,128)(2,1)S(1)} collective-permute-done((bf16[128,512]{1,0:T(8,128)(2,1)S(1)}, bf16[128,512]{1,0:T(8,128)(2,1)S(1)}, u32[]{:S(2)}, u32[]{:S(2)}) %collective-permute-start.7) | collective-permute-done | bytes 131104 | tf_op jit(solution)/shard_map/ppermute | solution.py:301
  29.3 4.5 %shard_map.94 = (bf16[128,512]{1,0:T(8,128)(2,1)S(1)}, bf16[128,512]{1,0:T(8,128)(2,1)S(1)}, bf16[128,512]{1,0:T(8,128)(2,1)S(1)}, bf16[128,512]{1,0:T(8,128)(2,...) custom-call(s32[1]{0:T(128)} %bitcast.me_ref, ...), custom_call_target="tpu_custom_call" | custom-call | flops 4294967296 | bytes 2097152 | tf_op jit(solution)/shard_map/pallas_call | solution.py:311
  33.9 1.2 %collective-permute-done.4.refs_1_ = bf16[128,512]{1,0:T(8,128)(2,1)S(1)} collective-permute-done((bf16[128,512]{1,0:T(8,128)(2,1)S(1)}, bf16[128,512]{1,0:T(8,128)(2,1)S(1)}, u32[]{:S(2)}, u32[]{:S(2)}) %collective-permute-start.4) | collective-permute-done | bytes 131104 | tf_op jit(solution)/shard_map/ppermute | solution.py:301
  35.1 0.8 %shard_map.95 = f32[8,1024]{1,0:T(8,128)S(1)} custom-call(s32[1]{0:T(128)} %bitcast.me_ref, bf16[128,512]{1,0:T(8,128)(2,1)S(1)} %collective-permute-done.2.refs_0_, bf16[128,512]{1,0:T(8,128)(2,1)S(1)} %collective-permute-done.4.refs_1_, bf16[512,512]{1,0:T(8,128)(2,1)S(1)} %get-tuple-element.53.refs_2_, f32[8,1024]{1,0:T(8,128)S(1)} %get-tuple-element.54.refs_3_), custom_call_target="tpu_custom_call" | custom-call | flops 268435456 | bytes 262144 | tf_op jit(solution)/shard_map/pallas_call | solution.py:311
  36.0 0.8 %shard_map.96 = (bf16[144,512]{1,0:T(8,128)(2,1)S(1)}, bf16[144,512]{1,0:T(8,128)(2,1)S(1)}, bf16[144,512]{1,0:T(8,128)(2,1)S(1)}, bf16[144,512]{1,0:T(8,128)(2,1)S(1)}) custom-call(s32[1]{0:T(128)} %bitcast.me_ref, bf16[128,512]{1,0:T(8,128)(2,1)S(1)} %collective-permute-done.2.refs_0_, bf16[128,512]{1,0:T(8,128)(2,1)S(1)} %collective-permute-done.4.refs_1_, ...), custom_call_target="tpu_custom_call" | custom-call | flops 536870912 | bytes 1048576 | tf_op jit(solution)/shard_map/pallas_call | solution.py:311
  36.8 0.3 collective-permute-done.8
  37.3 3.1 %collective-permute-start.9 = (bf16[144,512]{1,0:T(8,128)(2,1)S(1)}, bf16[144,512]{1,0:T(8,128)(2,1)S(1)}, u32[]{:S(2)}, u32[]{:S(2)}) collective-permute-start(bf16[144,512]{1,0:T(8,128)(2,1)S(1)} %get-tuple-element.64), channel_id=1, source_target_pairs={{0,3},{1,2},{2,1},{3,0},{4,7},{5,6},{6,5},{7,4},{8,11},{9,10},{10,... | collective-permute-start | bytes 442376 | tf_op jit(solution)/shard_map/ppermute | solution.py:301
  40.4 0.6 %collective-permute-start.11 = (bf16[144,512]{1,0:T(8,128)(2,1)S(1)}, bf16[144,512]{1,0:T(8,128)(2,1)S(1)}, u32[]{:S(2)}, u32[]{:S(2)}) collective-permute-start(bf16[144,512]{1,0:T(8,128)(2,1)S(1)} %get-tuple-element.66), channel_id=1, source_target_pairs={{0,1},{1,0},{2,3},{3,2},{4,5},{5,4},{6,7},{7,6},{8,9},{9,8},{10,11... | collective-permute-start | bytes 442376 | tf_op jit(solution)/shard_map/ppermute | solution.py:301
  41.1 2.8 %collective-permute-start.12 = (bf16[128,512]{1,0:T(8,128)(2,1)S(1)}, bf16[128,512]{1,0:T(8,128)(2,1)S(1)}, u32[]{:S(2)}, u32[]{:S(2)}) collective-permute-start(bf16[128,512]{1,0:T(8,128)(2,1)S(1)} %get-tuple-element.68), channel_id=1, source_target_pairs={{0,3},{1,2},{2,1},{3,0},{4,7},{5,6},{6,5},{7,4},{8,11},{9,10},{10,... | collective-permute-start | bytes 393224 | tf_op jit(solution)/shard_map/ppermute | solution.py:301
  43.9 1.1 %collective-permute-done.9.refs_1_ = bf16[144,512]{1,0:T(8,128)(2,1)S(1)} collective-permute-done((bf16[144,512]{1,0:T(8,128)(2,1)S(1)}, bf16[144,512]{1,0:T(8,128)(2,1)S(1)}, u32[]{:S(2)}, u32[]{:S(2)}) %collective-permute-start.9) | collective-permute-done | bytes 147488 | tf_op jit(solution)/shard_map/ppermute | solution.py:301
  45.1 1.4 %collective-permute-start.14 = (bf16[128,512]{1,0:T(8,128)(2,1)S(1)}, bf16[128,512]{1,0:T(8,128)(2,1)S(1)}, u32[]{:S(2)}, u32[]{:S(2)}) collective-permute-start(bf16[128,512]{1,0:T(8,128)(2,1)S(1)} %get-tuple-element.70), channel_id=1, source_target_pairs={{0,1},{1,0},{2,3},{3,2},{4,5},{5,4},{6,7},{7,6},{8,9},{9,8},{10,11... | collective-permute-start | bytes 393224 | tf_op jit(solution)/shard_map/ppermute | solution.py:301
  46.5 1.7 %collective-permute-done.10.refs_2_ = bf16[144,512]{1,0:T(8,128)(2,1)S(1)} collective-permute-done((bf16[144,512]{1,0:T(8,128)(2,1)S(1)}, bf16[144,512]{1,0:T(8,128)(2,1)S(1)}, u32[]{:S(2)}, u32[]{:S(2)}) %collective-permute-start.10) | collective-permute-done | bytes 147488 | tf_op jit(solution)/shard_map/ppermute | solution.py:301
  48.2 0.2 collective-permute-done.11.refs_3_
  48.4 4.1 %collective-permute-start.17 = (f32[4,128]{1,0:T(4,128)S(1)}, f32[4,128]{1,0:T(4,128)S(1)}, u32[]{:S(2)}, u32[]{:S(2)}) collective-permute-start(f32[4,128]{1,0:T(4,128)S(1)} %get-tuple-element.76), channel_id=1, source_target_pairs={{0,20},{1,21},{2,22},{3,23},{4,16},{5,17},{6,18},{7,19},{8,28},{9,... | collective-permute-start | bytes 6152 | tf_op jit(solution)/shard_map/ppermute | solution.py:391
  52.5 0.6 %collective-permute-start.16 = (f32[4,128]{1,0:T(4,128)S(1)}, f32[4,128]{1,0:T(4,128)S(1)}, u32[]{:S(2)}, u32[]{:S(2)}) collective-permute-start(f32[4,128]{1,0:T(4,128)S(1)} %get-tuple-element.75), channel_id=1, source_target_pairs={{0,16},{1,17},{2,18},{3,19},{4,20},{5,21},{6,22},{7,23},{8,24},{9,... | collective-permute-start | bytes 6152 | tf_op jit(solution)/shard_map/ppermute | solution.py:391
  53.1 0.3 collective-permute-done.14.refs_7_
  53.4 1.8 %shard_map.98 = (bf16[128,2048]{1,0:T(8,128)(2,1)}, bf16[128,2048]{1,0:T(8,128)(2,1)}, bf16[128,2048]{1,0:T(8,128)(2,1)}, bf16[128,2048]{1,0:T(8,128)(2,1)}) custom-call(s32[1]{0:T(128)} %bitcast.me_ref, bf16[128,2048]{1,0:T(8,128)(2,1)S(1)} %copy-done, bf16[128,2048]{1,0:T(8,128)(2,1)S(1)} %copy-done.1, bf16[128,2048]{1,0:T(8,128)(2,1)S(1)} %copy-done.2, ...), custom_call_target="tpu_custom_call" | custom-call | flops 134217728 | bytes 5242880 | tf_op jit(solution)/shard_map/pallas_call | solution.py:311
  55.2 0.9 %collective-permute-done.16 = f32[4,128]{1,0:T(4,128)S(1)} collective-permute-done((f32[4,128]{1,0:T(4,128)S(1)}, f32[4,128]{1,0:T(4,128)S(1)}, u32[]{:S(2)}, u32[]{:S(2)}) %collective-permute-start.16) | collective-permute-done | bytes 2080 | tf_op jit(solution)/shard_map/ppermute | solution.py:391
  56.1 0.9 %collective-permute-done.15 = f32[4,128]{1,0:T(4,128)S(1)} collective-permute-done((f32[4,128]{1,0:T(4,128)S(1)}, f32[4,128]{1,0:T(4,128)S(1)}, u32[]{:S(2)}, u32[]{:S(2)}) %collective-permute-start.15) | collective-permute-done | bytes 2080 | tf_op jit(solution)/shard_map/ppermute | solution.py:391
  57.0 0.6 %add_multiply_fusion = f32[4,128]{1,0:T(4,128)} fusion(f32[4,128]{1,0:T(4,128)S(1)} %collective-permute-done.17, f32[4,128]{1,0:T(4,128)S(1)} %collective-permute-done.15, f32[4,128]{1,0:T(4,128)S(1)} %collective-permute-done.16, f32[8,128]{1,0:T(8,128)S(1)} %slice_add_fusion), kind=kLoop, calls=%fused_computation.2 | loop fusion | flops 2048 | bytes 10240 | tf_op jit(solution)/shard_map/mul | solution.py:428
  (26 shorter events, 0.4 us)
Async XLA Ops:
  0.6 6.1 %copy-start.4 = (bf16[4,128]{1,0:T(4,128)(2,1)S(1)}, bf16[4,128]{1,0:T(4,128)(2,1)}, u32[]{:S(2)}) copy-start(bf16[4,128]{1,0:T(4,128)(2,1)} %mine_ref.1) | copy-start | bytes 3076
  0.6 6.0 %collective-permute-start = (bf16[4,128]{1,0:T(4,128)(2,1)}, bf16[4,128]{1,0:T(4,128)(2,1)S(1)}, u32[]{:S(2)}, u32[]{:S(2)}) collective-permute-start(bf16[4,128]{1,0:T(4,128)(2,1)} %mine_ref.1), channel_id=1, source_target_pairs={{0,4},{1,5},{2,6},{3,7},{4,0},{5,1},{6,2},{7,3},{8,12},{9,13},{10,... | collective-permute-start | bytes 3080 | tf_op jit(solution)/shard_map/ppermute | solution.py:301
  7.1 8.2 %collective-permute-start.1 = (bf16[272,512]{1,0:T(8,128)(2,1)S(1)}, bf16[272,512]{1,0:T(8,128)(2,1)S(1)}, u32[]{:S(2)}, u32[]{:S(2)}) collective-permute-start(bf16[272,512]{1,0:T(8,128)(2,1)S(1)} %get-tuple-element.42), channel_id=1, source_target_pairs={{0,1},{1,0},{2,3},{3,2},{4,5},{5,4},{6,7},{7,6},{8,9},{9,8},{10,11... | collective-permute-start | bytes 835592 | tf_op jit(solution)/shard_map/ppermute | solution.py:301
  8.8 15.2 %collective-permute-start.3 = (bf16[272,512]{1,0:T(8,128)(2,1)S(1)}, bf16[272,512]{1,0:T(8,128)(2,1)S(1)}, u32[]{:S(2)}, u32[]{:S(2)}) collective-permute-start(bf16[272,512]{1,0:T(8,128)(2,1)S(1)} %get-tuple-element.45), channel_id=1, source_target_pairs={{0,2},{1,3},{2,0},{3,1},{4,6},{5,7},{6,4},{7,5},{8,10},{9,11},{10,... | collective-permute-start | bytes 835592 | tf_op jit(solution)/shard_map/ppermute | solution.py:301
  10.4 18.9 %collective-permute-start.5 = (bf16[272,512]{1,0:T(8,128)(2,1)S(1)}, bf16[272,512]{1,0:T(8,128)(2,1)S(1)}, u32[]{:S(2)}, u32[]{:S(2)}) collective-permute-start(bf16[272,512]{1,0:T(8,128)(2,1)S(1)} %get-tuple-element.50), channel_id=1, source_target_pairs={{0,3},{1,2},{2,1},{3,0},{4,7},{5,6},{6,5},{7,4},{8,11},{9,10},{10,... | collective-permute-start | bytes 835592 | tf_op jit(solution)/shard_map/ppermute | solution.py:301
  10.7 16.9 %collective-permute-start.6 = (bf16[128,512]{1,0:T(8,128)(2,1)S(1)}, bf16[128,512]{1,0:T(8,128)(2,1)S(1)}, u32[]{:S(2)}, u32[]{:S(2)}) collective-permute-start(bf16[128,512]{1,0:T(8,128)(2,1)S(1)} %get-tuple-element.51), channel_id=1, source_target_pairs={{0,4},{1,5},{2,6},{3,7},{4,0},{5,1},{6,2},{7,3},{8,12},{9,13},{10,... | collective-permute-start | bytes 393224 | tf_op jit(solution)/shard_map/ppermute | solution.py:301
  13.4 15.8 %collective-permute-start.7 = (bf16[128,512]{1,0:T(8,128)(2,1)S(1)}, bf16[128,512]{1,0:T(8,128)(2,1)S(1)}, u32[]{:S(2)}, u32[]{:S(2)}) collective-permute-start(bf16[128,512]{1,0:T(8,128)(2,1)S(1)} %get-tuple-element.52), channel_id=1, source_target_pairs={{0,5},{1,4},{2,7},{3,6},{4,1},{5,0},{6,3},{7,2},{8,13},{9,12},{10,... | collective-permute-start | bytes 393224 | tf_op jit(solution)/shard_map/ppermute | solution.py:301
  15.3 18.5 %collective-permute-start.2 = (bf16[128,512]{1,0:T(8,128)(2,1)S(1)}, bf16[128,512]{1,0:T(8,128)(2,1)S(1)}, u32[]{:S(2)}, u32[]{:S(2)}) collective-permute-start(bf16[128,512]{1,0:T(8,128)(2,1)S(1)} %get-tuple-element.43), channel_id=1, source_target_pairs={{0,6},{1,7},{2,4},{3,5},{4,2},{5,3},{6,0},{7,1},{8,14},{9,15},{10,... | collective-permute-start | bytes 393224 | tf_op jit(solution)/shard_map/ppermute | solution.py:301
  24.1 11.0 %collective-permute-start.4 = (bf16[128,512]{1,0:T(8,128)(2,1)S(1)}, bf16[128,512]{1,0:T(8,128)(2,1)S(1)}, u32[]{:S(2)}, u32[]{:S(2)}) collective-permute-start(bf16[128,512]{1,0:T(8,128)(2,1)S(1)} %get-tuple-element.46), channel_id=1, source_target_pairs={{0,7},{1,6},{2,5},{3,4},{4,3},{5,2},{6,1},{7,0},{8,15},{9,14},{10,... | collective-permute-start | bytes 393224 | tf_op jit(solution)/shard_map/ppermute | solution.py:301
  35.8 1.3 %collective-permute-start.8 = (f32[8,1024]{1,0:T(8,128)S(1)}, f32[8,1024]{1,0:T(8,128)S(1)}, u32[]{:S(2)}, u32[]{:S(2)}) collective-permute-start(f32[8,1024]{1,0:T(8,128)S(1)} %shard_map.95), channel_id=1, source_target_pairs={{0,8},{1,9},{2,10},{3,11},{4,12},{5,13},{6,14},{7,15},{8,0},{9,1},... | collective-permute-start | bytes 98312 | tf_op jit(solution)/shard_map/ppermute | solution.py:391
  35.9 17.5 %copy-start = (bf16[128,2048]{1,0:T(8,128)(2,1)S(1)}, bf16[128,2048]{1,0:T(8,128)(2,1)}, u32[]{:S(2)}) copy-start(bf16[128,2048]{1,0:T(8,128)(2,1)} %q_ref.3) | copy-start | bytes 1572868
  35.9 17.4 %copy-start.1 = (bf16[128,2048]{1,0:T(8,128)(2,1)S(1)}, bf16[128,2048]{1,0:T(8,128)(2,1)}, u32[]{:S(2)}) copy-start(bf16[128,2048]{1,0:T(8,128)(2,1)} %k_ref.3) | copy-start | bytes 1572868
  36.0 17.4 %copy-start.2 = (bf16[128,2048]{1,0:T(8,128)(2,1)S(1)}, bf16[128,2048]{1,0:T(8,128)(2,1)}, u32[]{:S(2)}) copy-start(bf16[128,2048]{1,0:T(8,128)(2,1)} %v_ref.3) | copy-start | bytes 1572868
  36.0 17.4 %copy-start.3 = (bf16[128,2048]{1,0:T(8,128)(2,1)S(1)}, bf16[128,2048]{1,0:T(8,128)(2,1)}, u32[]{:S(2)}) copy-start(bf16[128,2048]{1,0:T(8,128)(2,1)} %g_ref.3) | copy-start | bytes 1572868
  37.3 7.8 %collective-permute-start.9 = (bf16[144,512]{1,0:T(8,128)(2,1)S(1)}, bf16[144,512]{1,0:T(8,128)(2,1)S(1)}, u32[]{:S(2)}, u32[]{:S(2)}) collective-permute-start(bf16[144,512]{1,0:T(8,128)(2,1)S(1)} %get-tuple-element.64), channel_id=1, source_target_pairs={{0,3},{1,2},{2,1},{3,0},{4,7},{5,6},{6,5},{7,4},{8,11},{9,10},{10,... | collective-permute-start | bytes 442376 | tf_op jit(solution)/shard_map/ppermute | solution.py:301
  40.4 7.7 %collective-permute-start.10 = (bf16[144,512]{1,0:T(8,128)(2,1)S(1)}, bf16[144,512]{1,0:T(8,128)(2,1)S(1)}, u32[]{:S(2)}, u32[]{:S(2)}) collective-permute-start(bf16[144,512]{1,0:T(8,128)(2,1)S(1)} %get-tuple-element.65), channel_id=1, source_target_pairs={{0,2},{1,3},{2,0},{3,1},{4,6},{5,7},{6,4},{7,5},{8,10},{9,11},{10,... | collective-permute-start | bytes 442376 | tf_op jit(solution)/shard_map/ppermute | solution.py:301
  40.4 7.9 %collective-permute-start.11 = (bf16[144,512]{1,0:T(8,128)(2,1)S(1)}, bf16[144,512]{1,0:T(8,128)(2,1)S(1)}, u32[]{:S(2)}, u32[]{:S(2)}) collective-permute-start(bf16[144,512]{1,0:T(8,128)(2,1)S(1)} %get-tuple-element.66), channel_id=1, source_target_pairs={{0,1},{1,0},{2,3},{3,2},{4,5},{5,4},{6,7},{7,6},{8,9},{9,8},{10,11... | collective-permute-start | bytes 442376 | tf_op jit(solution)/shard_map/ppermute | solution.py:301
  41.1 11.4 %collective-permute-start.12 = (bf16[128,512]{1,0:T(8,128)(2,1)S(1)}, bf16[128,512]{1,0:T(8,128)(2,1)S(1)}, u32[]{:S(2)}, u32[]{:S(2)}) collective-permute-start(bf16[128,512]{1,0:T(8,128)(2,1)S(1)} %get-tuple-element.68), channel_id=1, source_target_pairs={{0,3},{1,2},{2,1},{3,0},{4,7},{5,6},{6,5},{7,4},{8,11},{9,10},{10,... | collective-permute-start | bytes 393224 | tf_op jit(solution)/shard_map/ppermute | solution.py:301
  43.9 9.2 %collective-permute-start.13 = (bf16[128,512]{1,0:T(8,128)(2,1)S(1)}, bf16[128,512]{1,0:T(8,128)(2,1)S(1)}, u32[]{:S(2)}, u32[]{:S(2)}) collective-permute-start(bf16[128,512]{1,0:T(8,128)(2,1)S(1)} %get-tuple-element.69), channel_id=1, source_target_pairs={{0,2},{1,3},{2,0},{3,1},{4,6},{5,7},{6,4},{7,5},{8,10},{9,11},{10,... | collective-permute-start | bytes 393224 | tf_op jit(solution)/shard_map/ppermute | solution.py:301
  45.1 8.3 %collective-permute-start.14 = (bf16[128,512]{1,0:T(8,128)(2,1)S(1)}, bf16[128,512]{1,0:T(8,128)(2,1)S(1)}, u32[]{:S(2)}, u32[]{:S(2)}) collective-permute-start(bf16[128,512]{1,0:T(8,128)(2,1)S(1)} %get-tuple-element.70), channel_id=1, source_target_pairs={{0,1},{1,0},{2,3},{3,2},{4,5},{5,4},{6,7},{7,6},{8,9},{9,8},{10,11... | collective-permute-start | bytes 393224 | tf_op jit(solution)/shard_map/ppermute | solution.py:301
  48.4 7.7 %collective-permute-start.17 = (f32[4,128]{1,0:T(4,128)S(1)}, f32[4,128]{1,0:T(4,128)S(1)}, u32[]{:S(2)}, u32[]{:S(2)}) collective-permute-start(f32[4,128]{1,0:T(4,128)S(1)} %get-tuple-element.76), channel_id=1, source_target_pairs={{0,20},{1,21},{2,22},{3,23},{4,16},{5,17},{6,18},{7,19},{8,28},{9,... | collective-permute-start | bytes 6152 | tf_op jit(solution)/shard_map/ppermute | solution.py:391
  52.5 4.5 %collective-permute-start.15 = (f32[4,128]{1,0:T(4,128)S(1)}, f32[4,128]{1,0:T(4,128)S(1)}, u32[]{:S(2)}, u32[]{:S(2)}) collective-permute-start(f32[4,128]{1,0:T(4,128)S(1)} %get-tuple-element.76), channel_id=1, source_target_pairs={{0,4},{1,5},{2,6},{3,7},{4,0},{5,1},{6,2},{7,3},{8,12},{9,13},{10,... | collective-permute-start | bytes 6152 | tf_op jit(solution)/shard_map/ppermute | solution.py:391
  52.5 3.6 %collective-permute-start.16 = (f32[4,128]{1,0:T(4,128)S(1)}, f32[4,128]{1,0:T(4,128)S(1)}, u32[]{:S(2)}, u32[]{:S(2)}) collective-permute-start(f32[4,128]{1,0:T(4,128)S(1)} %get-tuple-element.75), channel_id=1, source_target_pairs={{0,16},{1,17},{2,18},{3,19},{4,20},{5,21},{6,22},{7,23},{8,24},{9,... | collective-permute-start | bytes 6152 | tf_op jit(solution)/shard_map/ppermute | solution.py:391

commit v6 on v5

--- a/solution.py
+++ b/solution.py
@@ -25,7 +25,7 @@
 
 
 def gate_kernel(half, slim, me_ref, q_ref, k_ref, v_ref, g_ref, *refs):
-    outs, (pair_ref, held, sems) = refs[:-3], refs[-3:]
+    outs, (held, sems) = refs[:-2], refs[-2:]
     rows = q_ref.shape[0]
     me = me_ref[0]
     upper = me >= half
@@ -40,6 +40,7 @@
             )
             copy.start()
             copies[chunk].append(copy)
+    turn = exchange(rows, upper, jnp.bfloat16)
     turn_other = exchange(rows, jnp.logical_not(upper), jnp.bfloat16)
     for step in range(half):
         if step % 2 == 0:
@@ -50,22 +51,27 @@
         gated = (k * v).astype(jnp.bfloat16)
         back = (g * q).astype(jnp.bfloat16)
         second = jnp.where(upper, back, gated)
-        pair_ref[step, 0] = jnp.where(upper, gated, back)
-        pair_ref[step, 1] = second
         outs[step][...] = exact_rows(turn_other, second)
-
-
-def bundle_kernel(half, me_ref, mine_ref, other_ref, pair_ref, *outs):
-    rows = pair_ref.shape[2]
-    turn = exchange(rows, me_ref[0] >= half, jnp.bfloat16)
+        bundle = outs[half + step]
+        bundle[0:rows, :] = exact_rows(turn, jnp.where(upper, gated, back))
+        bundle[rows : 2 * rows, :] = exact_rows(turn, second)
+
+
+def label_kernel(half, me_ref, mine_ref, other_ref, *refs):
+    outs, (held, sems) = refs[half : 2 * half], refs[2 * half :]
+    rows = outs[0].shape[0] - 16
     mine, other = mine_ref[...].astype(jnp.float32), other_ref[...].astype(jnp.float32)
     gap = jnp.zeros((8 - mine.shape[0], LANES), jnp.float32)
-    both = jnp.concatenate([mine, gap, other, gap], axis=0).astype(jnp.bfloat16)
-    for step in range(half):
-        outs[step][0:rows, :] = exact_rows(turn, pair_ref[step, 0])
-        outs[step][rows : 2 * rows, :] = exact_rows(turn, pair_ref[step, 1])
-        outs[step][2 * rows :, :] = jnp.zeros((16, outs[step].shape[1]), jnp.bfloat16)
-        outs[step][2 * rows :, 0:LANES] = both
+    held[...] = jnp.zeros(held.shape, jnp.bfloat16)
+    held[:, 0:LANES] = jnp.concatenate([mine, gap, other, gap], axis=0).astype(jnp.bfloat16)
+    copies = [
+        pltpu.make_async_copy(held, outs[step].at[rows : rows + 16], sems.at[step])
+        for step in range(half)
+    ]
+    for copy in copies:
+        copy.start()
+    for copy in copies:
+        copy.wait()
 
 
 def fill_bands(half, me, arrived, near_ref, far_ref, line):
@@ -341,21 +347,22 @@
         pltpu.with_memory_space_constraint(x, pltpu.HBM)
         for x in (queries, keys, values, cotangent)
     ]
-    *sent, pair = call(
+    made = call(
         functools.partial(gate_kernel, half, slim),
-        [shape((rows, slim), low)] * half + [shape((half, 2, rows, slim), low)],
+        [shape((rows, slim), low)] * half + [shape((2 * rows + 16, slim), low)] * half,
         [pltpu.VMEM((half // 2, 4, rows, 2 * slim), low), pltpu.SemaphoreType.DMA((half // 2, 4))],
         2 * rows * rows * width,
         14 * rows * width,
         where, *branches, far=4,
     )
+    sent = made[:half]
     inner = call(
-        functools.partial(bundle_kernel, half),
+        functools.partial(label_kernel, half),
         [shape((2 * rows + 16, slim), low)] * half,
-        [],
-        4 * rows * rows * width,
-        8 * rows * width,
-        where, filters, other_taps, pair,
+        [pltpu.VMEM((16, slim), low), pltpu.SemaphoreType.DMA((half,))],
+        0,
+        64 * slim * half,
+        where, filters, other_taps, *made[half:], alias=half, far_out=True,
     )
     inner = [inner[0]] + [swap(inner[k], k, count) for k in range(1, half)]
     outer = list(sent)

time: 57.7 us -> 57.7 us (level)
  transfers between devices with their start and end apart: 18 -> 18, of which waited for: 12 -> 11; matrix products, arithmetic and copies ran while one was open for 0% -> 0% of each run, Pallas kernels for 16% -> 16%
where the time goes in v6:
time: 57.7 us; the launch traced here: 57.5 us
  starting transfers between devices  31.3 us (54%)
  waiting for transfers between devices  14.5 us (25%)
  Pallas kernels  10.2 us (18%)
  between operations  0.8 us (1%)
  other arithmetic  0.6 us (1%)
    ppermute x14, starting transfers between devices, swap(): return lax.ppermute(value, 'ctx', [(i, i ^ step) for i in range(count)])  26.2 us
    ppermute x14, waiting for transfers between devices, swap(): return lax.ppermute(value, 'ctx', [(i, i ^ step) for i in range(count)])  12.2 us
    pallas_call x7, Pallas kernels, call(): pl.pallas_call(kernel, out_shape=outs, in_specs=[pl.BlockSpec(memory_spac...  10.2 us
    ppermute x4, starting transfers between devices, halves_plan(): lax.ppermute(value, ('chan', 'ctx'), [(c * count + i, (c ^ move) * count...  5.09 us
    ppermute x4, waiting for transfers between devices, halves_plan(): lax.ppermute(value, ('chan', 'ctx'), [(c * count + i, (c ^ move) * count...  2.37 us
  transfers between devices with their start and end apart: 18, of which 11 were waited for; matrix products, arithmetic and copies ran while one was open for 0% of the time, Pallas kernels for 16%

profile of v6, /device:TPU:0, one launch (start us, length us, event | category | flops | bytes accessed | tf_op | source)
XLA Modules:
  0.0 57.5 jit_solution(7132090697333272437)
XLA Ops:
  0.6 4.1 %collective-permute-start = (bf16[4,128]{1,0:T(4,128)(2,1)}, bf16[4,128]{1,0:T(4,128)(2,1)S(1)}, u32[]{:S(2)}, u32[]{:S(2)}) collective-permute-start(bf16[4,128]{1,0:T(4,128)(2,1)} %mine_ref.1), channel_id=1, source_target_pairs={{0,4},{1,5},{2,6},{3,7},{4,0},{5,1},{6,2},{7,3},{8,12},{9,13},{10,... | collective-permute-start | bytes 3080 | tf_op jit(solution)/shard_map/ppermute | solution.py:307
  4.7 2.1 %shard_map.92 = (bf16[128,512]{1,0:T(8,128)(2,1)S(1)}, bf16[128,512]{1,0:T(8,128)(2,1)S(1)}, bf16[128,512]{1,0:T(8,128)(2,1)S(1)}, bf16[128,512]{1,0:T(8,128)(2,...) custom-call(s32[1]{0:T(128)} %bitcast.me_ref, ...), custom_call_target="tpu_custom_call" | custom-call | flops 67108864 | bytes 3670016 | tf_op jit(solution)/shard_map/pallas_call | solution.py:317
  7.0 1.6 %collective-permute-start.1 = (bf16[272,512]{1,0:T(8,128)(2,1)S(1)}, bf16[272,512]{1,0:T(8,128)(2,1)S(1)}, u32[]{:S(2)}, u32[]{:S(2)}) collective-permute-start(bf16[272,512]{1,0:T(8,128)(2,1)S(1)} %get-tuple-element.48), channel_id=1, source_target_pairs={{0,1},{1,0},{2,3},{3,2},{4,5},{5,4},{6,7},{7,6},{8,9},{9,8},{10,11... | collective-permute-start | bytes 835592 | tf_op jit(solution)/shard_map/ppermute | solution.py:307
  8.6 1.6 %collective-permute-start.3 = (bf16[272,512]{1,0:T(8,128)(2,1)S(1)}, bf16[272,512]{1,0:T(8,128)(2,1)S(1)}, u32[]{:S(2)}, u32[]{:S(2)}) collective-permute-start(bf16[272,512]{1,0:T(8,128)(2,1)S(1)} %get-tuple-element.51), channel_id=1, source_target_pairs={{0,2},{1,3},{2,0},{3,1},{4,6},{5,7},{6,4},{7,5},{8,10},{9,11},{10,... | collective-permute-start | bytes 835592 | tf_op jit(solution)/shard_map/ppermute | solution.py:307
  10.2 0.4 collective-permute-start.5
  10.6 2.5 %collective-permute-start.6 = (bf16[128,512]{1,0:T(8,128)(2,1)S(1)}, bf16[128,512]{1,0:T(8,128)(2,1)S(1)}, u32[]{:S(2)}, u32[]{:S(2)}) collective-permute-start(bf16[128,512]{1,0:T(8,128)(2,1)S(1)} %get-tuple-element.57), channel_id=1, source_target_pairs={{0,4},{1,5},{2,6},{3,7},{4,0},{5,1},{6,2},{7,3},{8,12},{9,13},{10,... | collective-permute-start | bytes 393224 | tf_op jit(solution)/shard_map/ppermute | solution.py:307
  13.1 1.3 %collective-permute-start.7 = (bf16[128,512]{1,0:T(8,128)(2,1)S(1)}, bf16[128,512]{1,0:T(8,128)(2,1)S(1)}, u32[]{:S(2)}, u32[]{:S(2)}) collective-permute-start(bf16[128,512]{1,0:T(8,128)(2,1)S(1)} %get-tuple-element.58), channel_id=1, source_target_pairs={{0,5},{1,4},{2,7},{3,6},{4,1},{5,0},{6,3},{7,2},{8,13},{9,12},{10,... | collective-permute-start | bytes 393224 | tf_op jit(solution)/shard_map/ppermute | solution.py:307
  14.4 0.8 %collective-permute-done.1.refs_1_ = bf16[272,512]{1,0:T(8,128)(2,1)S(1)} collective-permute-done((bf16[272,512]{1,0:T(8,128)(2,1)S(1)}, bf16[272,512]{1,0:T(8,128)(2,1)S(1)}, u32[]{:S(2)}, u32[]{:S(2)}) %collective-permute-start.1) | collective-permute-done | bytes 278560 | tf_op jit(solution)/shard_map/ppermute | solution.py:307
  15.2 3.2 %collective-permute-start.2 = (bf16[128,512]{1,0:T(8,128)(2,1)S(1)}, bf16[128,512]{1,0:T(8,128)(2,1)S(1)}, u32[]{:S(2)}, u32[]{:S(2)}) collective-permute-start(bf16[128,512]{1,0:T(8,128)(2,1)S(1)} %get-tuple-element.49), channel_id=1, source_target_pairs={{0,6},{1,7},{2,4},{3,5},{4,2},{5,3},{6,0},{7,1},{8,14},{9,15},{10,... | collective-permute-start | bytes 393224 | tf_op jit(solution)/shard_map/ppermute | solution.py:307
  18.4 5.4 %collective-permute-done.3.refs_2_ = bf16[272,512]{1,0:T(8,128)(2,1)S(1)} collective-permute-done((bf16[272,512]{1,0:T(8,128)(2,1)S(1)}, bf16[272,512]{1,0:T(8,128)(2,1)S(1)}, u32[]{:S(2)}, u32[]{:S(2)}) %collective-permute-start.3) | collective-permute-done | bytes 278560 | tf_op jit(solution)/shard_map/ppermute | solution.py:307
  23.8 3.5 %collective-permute-start.4 = (bf16[128,512]{1,0:T(8,128)(2,1)S(1)}, bf16[128,512]{1,0:T(8,128)(2,1)S(1)}, u32[]{:S(2)}, u32[]{:S(2)}) collective-permute-start(bf16[128,512]{1,0:T(8,128)(2,1)S(1)} %get-tuple-element.52), channel_id=1, source_target_pairs={{0,7},{1,6},{2,5},{3,4},{4,3},{5,2},{6,1},{7,0},{8,15},{9,14},{10,... | collective-permute-start | bytes 393224 | tf_op jit(solution)/shard_map/ppermute | solution.py:307
  27.3 1.7 %collective-permute-done.7.refs_5_ = bf16[128,512]{1,0:T(8,128)(2,1)S(1)} collective-permute-done((bf16[128,512]{1,0:T(8,128)(2,1)S(1)}, bf16[128,512]{1,0:T(8,128)(2,1)S(1)}, u32[]{:S(2)}, u32[]{:S(2)}) %collective-permute-start.7) | collective-permute-done | bytes 131104 | tf_op jit(solution)/shard_map/ppermute | solution.py:307
  29.0 0.4 collective-permute-done.5.refs_3_
  29.4 4.5 %shard_map.94 = (bf16[128,512]{1,0:T(8,128)(2,1)S(1)}, bf16[128,512]{1,0:T(8,128)(2,1)S(1)}, bf16[128,512]{1,0:T(8,128)(2,1)S(1)}, bf16[128,512]{1,0:T(8,128)(2,...) custom-call(s32[1]{0:T(128)} %bitcast.me_ref, ...), custom_call_target="tpu_custom_call" | custom-call | flops 4294967296 | bytes 2097152 | tf_op jit(solution)/shard_map/pallas_call | solution.py:317
  33.9 0.9 %collective-permute-done.4.refs_1_ = bf16[128,512]{1,0:T(8,128)(2,1)S(1)} collective-permute-done((bf16[128,512]{1,0:T(8,128)(2,1)S(1)}, bf16[128,512]{1,0:T(8,128)(2,1)S(1)}, u32[]{:S(2)}, u32[]{:S(2)}) %collective-permute-start.4) | collective-permute-done | bytes 131104 | tf_op jit(solution)/shard_map/ppermute | solution.py:307
  34.8 0.8 %shard_map.95 = f32[8,1024]{1,0:T(8,128)S(1)} custom-call(s32[1]{0:T(128)} %bitcast.me_ref, bf16[128,512]{1,0:T(8,128)(2,1)S(1)} %collective-permute-done.2.refs_0_, bf16[128,512]{1,0:T(8,128)(2,1)S(1)} %collective-permute-done.4.refs_1_, bf16[512,512]{1,0:T(8,128)(2,1)S(1)} %get-tuple-element.59.refs_2_, f32[8,1024]{1,0:T(8,128)S(1)} %get-tuple-element.60.refs_3_), custom_call_target="tpu_custom_call" | custom-call | flops 268435456 | bytes 262144 | tf_op jit(solution)/shard_map/pallas_call | solution.py:317
  35.7 0.8 %shard_map.96 = (bf16[144,512]{1,0:T(8,128)(2,1)S(1)}, bf16[144,512]{1,0:T(8,128)(2,1)S(1)}, bf16[144,512]{1,0:T(8,128)(2,1)S(1)}, bf16[144,512]{1,0:T(8,128)(2,1)S(1)}) custom-call(s32[1]{0:T(128)} %bitcast.me_ref, bf16[128,512]{1,0:T(8,128)(2,1)S(1)} %collective-permute-done.2.refs_0_, bf16[128,512]{1,0:T(8,128)(2,1)S(1)} %collective-permute-done.4.refs_1_, ...), custom_call_target="tpu_custom_call" | custom-call | flops 536870912 | bytes 1048576 | tf_op jit(solution)/shard_map/pallas_call | solution.py:317
  36.5 0.3 collective-permute-done.8
  36.8 0.2 shard_map.97
  37.0 3.1 %collective-permute-start.9 = (bf16[144,512]{1,0:T(8,128)(2,1)S(1)}, bf16[144,512]{1,0:T(8,128)(2,1)S(1)}, u32[]{:S(2)}, u32[]{:S(2)}) collective-permute-start(bf16[144,512]{1,0:T(8,128)(2,1)S(1)} %get-tuple-element.70), channel_id=1, source_target_pairs={{0,3},{1,2},{2,1},{3,0},{4,7},{5,6},{6,5},{7,4},{8,11},{9,10},{10,... | collective-permute-start | bytes 442376 | tf_op jit(solution)/shard_map/ppermute | solution.py:307
  40.1 0.8 %collective-permute-start.11 = (bf16[144,512]{1,0:T(8,128)(2,1)S(1)}, bf16[144,512]{1,0:T(8,128)(2,1)S(1)}, u32[]{:S(2)}, u32[]{:S(2)}) collective-permute-start(bf16[144,512]{1,0:T(8,128)(2,1)S(1)} %get-tuple-element.72), channel_id=1, source_target_pairs={{0,1},{1,0},{2,3},{3,2},{4,5},{5,4},{6,7},{7,6},{8,9},{9,8},{10,11... | collective-permute-start | bytes 442376 | tf_op jit(solution)/shard_map/ppermute | solution.py:307
  41.0 2.7 %collective-permute-start.12 = (bf16[128,512]{1,0:T(8,128)(2,1)S(1)}, bf16[128,512]{1,0:T(8,128)(2,1)S(1)}, u32[]{:S(2)}, u32[]{:S(2)}) collective-permute-start(bf16[128,512]{1,0:T(8,128)(2,1)S(1)} %get-tuple-element.74), channel_id=1, source_target_pairs={{0,3},{1,2},{2,1},{3,0},{4,7},{5,6},{6,5},{7,4},{8,11},{9,10},{10,... | collective-permute-start | bytes 393224 | tf_op jit(solution)/shard_map/ppermute | solution.py:307
  43.6 1.1 %collective-permute-done.9.refs_1_ = bf16[144,512]{1,0:T(8,128)(2,1)S(1)} collective-permute-done((bf16[144,512]{1,0:T(8,128)(2,1)S(1)}, bf16[144,512]{1,0:T(8,128)(2,1)S(1)}, u32[]{:S(2)}, u32[]{:S(2)}) %collective-permute-start.9) | collective-permute-done | bytes 147488 | tf_op jit(solution)/shard_map/ppermute | solution.py:307
  44.8 1.4 %collective-permute-start.14 = (bf16[128,512]{1,0:T(8,128)(2,1)S(1)}, bf16[128,512]{1,0:T(8,128)(2,1)S(1)}, u32[]{:S(2)}, u32[]{:S(2)}) collective-permute-start(bf16[128,512]{1,0:T(8,128)(2,1)S(1)} %get-tuple-element.76), channel_id=1, source_target_pairs={{0,1},{1,0},{2,3},{3,2},{4,5},{5,4},{6,7},{7,6},{8,9},{9,8},{10,11... | collective-permute-start | bytes 393224 | tf_op jit(solution)/shard_map/ppermute | solution.py:307
  46.2 1.7 %collective-permute-done.10.refs_2_ = bf16[144,512]{1,0:T(8,128)(2,1)S(1)} collective-permute-done((bf16[144,512]{1,0:T(8,128)(2,1)S(1)}, bf16[144,512]{1,0:T(8,128)(2,1)S(1)}, u32[]{:S(2)}, u32[]{:S(2)}) %collective-permute-start.10) | collective-permute-done | bytes 147488 | tf_op jit(solution)/shard_map/ppermute | solution.py:307
  47.9 0.2 collective-permute-done.11.refs_3_
  48.1 4.4 %collective-permute-start.17 = (f32[4,128]{1,0:T(4,128)S(1)}, f32[4,128]{1,0:T(4,128)S(1)}, u32[]{:S(2)}, u32[]{:S(2)}) collective-permute-start(f32[4,128]{1,0:T(4,128)S(1)} %get-tuple-element.82), channel_id=1, source_target_pairs={{0,20},{1,21},{2,22},{3,23},{4,16},{5,17},{6,18},{7,19},{8,28},{9,... | collective-permute-start | bytes 6152 | tf_op jit(solution)/shard_map/ppermute | solution.py:398
  52.5 0.6 %collective-permute-start.16 = (f32[4,128]{1,0:T(4,128)S(1)}, f32[4,128]{1,0:T(4,128)S(1)}, u32[]{:S(2)}, u32[]{:S(2)}) collective-permute-start(f32[4,128]{1,0:T(4,128)S(1)} %get-tuple-element.81), channel_id=1, source_target_pairs={{0,16},{1,17},{2,18},{3,19},{4,20},{5,21},{6,22},{7,23},{8,24},{9,... | collective-permute-start | bytes 6152 | tf_op jit(solution)/shard_map/ppermute | solution.py:398
  53.1 1.8 %shard_map.98 = (bf16[128,2048]{1,0:T(8,128)(2,1)}, bf16[128,2048]{1,0:T(8,128)(2,1)}, bf16[128,2048]{1,0:T(8,128)(2,1)}, bf16[128,2048]{1,0:T(8,128)(2,1)}) custom-call(s32[1]{0:T(128)} %bitcast.me_ref, bf16[128,2048]{1,0:T(8,128)(2,1)S(1)} %copy-done, bf16[128,2048]{1,0:T(8,128)(2,1)S(1)} %copy-done.1, bf16[128,2048]{1,0:T(8,128)(2,1)S(1)} %copy-done.2, ...), custom_call_target="tpu_custom_call" | custom-call | flops 134217728 | bytes 5242880 | tf_op jit(solution)/shard_map/pallas_call | solution.py:317
  54.9 1.1 %collective-permute-done.16 = f32[4,128]{1,0:T(4,128)S(1)} collective-permute-done((f32[4,128]{1,0:T(4,128)S(1)}, f32[4,128]{1,0:T(4,128)S(1)}, u32[]{:S(2)}, u32[]{:S(2)}) %collective-permute-start.16) | collective-permute-done | bytes 2080 | tf_op jit(solution)/shard_map/ppermute | solution.py:398
  56.0 0.9 %collective-permute-done.15 = f32[4,128]{1,0:T(4,128)S(1)} collective-permute-done((f32[4,128]{1,0:T(4,128)S(1)}, f32[4,128]{1,0:T(4,128)S(1)}, u32[]{:S(2)}, u32[]{:S(2)}) %collective-permute-start.15) | collective-permute-done | bytes 2080 | tf_op jit(solution)/shard_map/ppermute | solution.py:398
  56.9 0.6 %add_multiply_fusion = f32[4,128]{1,0:T(4,128)} fusion(f32[4,128]{1,0:T(4,128)S(1)} %collective-permute-done.17, f32[4,128]{1,0:T(4,128)S(1)} %collective-permute-done.15, f32[4,128]{1,0:T(4,128)S(1)} %collective-permute-done.16, f32[8,128]{1,0:T(8,128)S(1)} %slice_add_fusion), kind=kLoop, calls=%fused_computation.2 | loop fusion | flops 2048 | bytes 10240 | tf_op jit(solution)/shard_map/mul | solution.py:435
  (26 shorter events, 0.3 us)
Async XLA Ops:
  0.6 6.2 %copy-start.4 = (bf16[4,128]{1,0:T(4,128)(2,1)S(1)}, bf16[4,128]{1,0:T(4,128)(2,1)}, u32[]{:S(2)}) copy-start(bf16[4,128]{1,0:T(4,128)(2,1)} %mine_ref.1) | copy-start | bytes 3076
  0.6 6.2 %collective-permute-start = (bf16[4,128]{1,0:T(4,128)(2,1)}, bf16[4,128]{1,0:T(4,128)(2,1)S(1)}, u32[]{:S(2)}, u32[]{:S(2)}) collective-permute-start(bf16[4,128]{1,0:T(4,128)(2,1)} %mine_ref.1), channel_id=1, source_target_pairs={{0,4},{1,5},{2,6},{3,7},{4,0},{5,1},{6,2},{7,3},{8,12},{9,13},{10,... | collective-permute-start | bytes 3080 | tf_op jit(solution)/shard_map/ppermute | solution.py:307
  7.0 8.2 %collective-permute-start.1 = (bf16[272,512]{1,0:T(8,128)(2,1)S(1)}, bf16[272,512]{1,0:T(8,128)(2,1)S(1)}, u32[]{:S(2)}, u32[]{:S(2)}) collective-permute-start(bf16[272,512]{1,0:T(8,128)(2,1)S(1)} %get-tuple-element.48), channel_id=1, source_target_pairs={{0,1},{1,0},{2,3},{3,2},{4,5},{5,4},{6,7},{7,6},{8,9},{9,8},{10,11... | collective-permute-start | bytes 835592 | tf_op jit(solution)/shard_map/ppermute | solution.py:307
  8.6 15.2 %collective-permute-start.3 = (bf16[272,512]{1,0:T(8,128)(2,1)S(1)}, bf16[272,512]{1,0:T(8,128)(2,1)S(1)}, u32[]{:S(2)}, u32[]{:S(2)}) collective-permute-start(bf16[272,512]{1,0:T(8,128)(2,1)S(1)} %get-tuple-element.51), channel_id=1, source_target_pairs={{0,2},{1,3},{2,0},{3,1},{4,6},{5,7},{6,4},{7,5},{8,10},{9,11},{10,... | collective-permute-start | bytes 835592 | tf_op jit(solution)/shard_map/ppermute | solution.py:307
  10.2 19.2 %collective-permute-start.5 = (bf16[272,512]{1,0:T(8,128)(2,1)S(1)}, bf16[272,512]{1,0:T(8,128)(2,1)S(1)}, u32[]{:S(2)}, u32[]{:S(2)}) collective-permute-start(bf16[272,512]{1,0:T(8,128)(2,1)S(1)} %get-tuple-element.56), channel_id=1, source_target_pairs={{0,3},{1,2},{2,1},{3,0},{4,7},{5,6},{6,5},{7,4},{8,11},{9,10},{10,... | collective-permute-start | bytes 835592 | tf_op jit(solution)/shard_map/ppermute | solution.py:307
  10.6 16.7 %collective-permute-start.6 = (bf16[128,512]{1,0:T(8,128)(2,1)S(1)}, bf16[128,512]{1,0:T(8,128)(2,1)S(1)}, u32[]{:S(2)}, u32[]{:S(2)}) collective-permute-start(bf16[128,512]{1,0:T(8,128)(2,1)S(1)} %get-tuple-element.57), channel_id=1, source_target_pairs={{0,4},{1,5},{2,6},{3,7},{4,0},{5,1},{6,2},{7,3},{8,12},{9,13},{10,... | collective-permute-start | bytes 393224 | tf_op jit(solution)/shard_map/ppermute | solution.py:307
  13.1 15.9 %collective-permute-start.7 = (bf16[128,512]{1,0:T(8,128)(2,1)S(1)}, bf16[128,512]{1,0:T(8,128)(2,1)S(1)}, u32[]{:S(2)}, u32[]{:S(2)}) collective-permute-start(bf16[128,512]{1,0:T(8,128)(2,1)S(1)} %get-tuple-element.58), channel_id=1, source_target_pairs={{0,5},{1,4},{2,7},{3,6},{4,1},{5,0},{6,3},{7,2},{8,13},{9,12},{10,... | collective-permute-start | bytes 393224 | tf_op jit(solution)/shard_map/ppermute | solution.py:307
  15.2 18.7 %collective-permute-start.2 = (bf16[128,512]{1,0:T(8,128)(2,1)S(1)}, bf16[128,512]{1,0:T(8,128)(2,1)S(1)}, u32[]{:S(2)}, u32[]{:S(2)}) collective-permute-start(bf16[128,512]{1,0:T(8,128)(2,1)S(1)} %get-tuple-element.49), channel_id=1, source_target_pairs={{0,6},{1,7},{2,4},{3,5},{4,2},{5,3},{6,0},{7,1},{8,14},{9,15},{10,... | collective-permute-start | bytes 393224 | tf_op jit(solution)/shard_map/ppermute | solution.py:307
  23.8 11.0 %collective-permute-start.4 = (bf16[128,512]{1,0:T(8,128)(2,1)S(1)}, bf16[128,512]{1,0:T(8,128)(2,1)S(1)}, u32[]{:S(2)}, u32[]{:S(2)}) collective-permute-start(bf16[128,512]{1,0:T(8,128)(2,1)S(1)} %get-tuple-element.52), channel_id=1, source_target_pairs={{0,7},{1,6},{2,5},{3,4},{4,3},{5,2},{6,1},{7,0},{8,15},{9,14},{10,... | collective-permute-start | bytes 393224 | tf_op jit(solution)/shard_map/ppermute | solution.py:307
  35.6 1.3 %collective-permute-start.8 = (f32[8,1024]{1,0:T(8,128)S(1)}, f32[8,1024]{1,0:T(8,128)S(1)}, u32[]{:S(2)}, u32[]{:S(2)}) collective-permute-start(f32[8,1024]{1,0:T(8,128)S(1)} %shard_map.95), channel_id=1, source_target_pairs={{0,8},{1,9},{2,10},{3,11},{4,12},{5,13},{6,14},{7,15},{8,0},{9,1},... | collective-permute-start | bytes 98312 | tf_op jit(solution)/shard_map/ppermute | solution.py:398
  35.6 17.5 %copy-start = (bf16[128,2048]{1,0:T(8,128)(2,1)S(1)}, bf16[128,2048]{1,0:T(8,128)(2,1)}, u32[]{:S(2)}) copy-start(bf16[128,2048]{1,0:T(8,128)(2,1)} %q_ref.3) | copy-start | bytes 1572868
  35.7 17.5 %copy-start.1 = (bf16[128,2048]{1,0:T(8,128)(2,1)S(1)}, bf16[128,2048]{1,0:T(8,128)(2,1)}, u32[]{:S(2)}) copy-start(bf16[128,2048]{1,0:T(8,128)(2,1)} %k_ref.3) | copy-start | bytes 1572868
  35.7 17.5 %copy-start.2 = (bf16[128,2048]{1,0:T(8,128)(2,1)S(1)}, bf16[128,2048]{1,0:T(8,128)(2,1)}, u32[]{:S(2)}) copy-start(bf16[128,2048]{1,0:T(8,128)(2,1)} %v_ref.3) | copy-start | bytes 1572868
  35.7 17.4 %copy-start.3 = (bf16[128,2048]{1,0:T(8,128)(2,1)S(1)}, bf16[128,2048]{1,0:T(8,128)(2,1)}, u32[]{:S(2)}) copy-start(bf16[128,2048]{1,0:T(8,128)(2,1)} %g_ref.3) | copy-start | bytes 1572868
  37.0 7.8 %collective-permute-start.9 = (bf16[144,512]{1,0:T(8,128)(2,1)S(1)}, bf16[144,512]{1,0:T(8,128)(2,1)S(1)}, u32[]{:S(2)}, u32[]{:S(2)}) collective-permute-start(bf16[144,512]{1,0:T(8,128)(2,1)S(1)} %get-tuple-element.70), channel_id=1, source_target_pairs={{0,3},{1,2},{2,1},{3,0},{4,7},{5,6},{6,5},{7,4},{8,11},{9,10},{10,... | collective-permute-start | bytes 442376 | tf_op jit(solution)/shard_map/ppermute | solution.py:307
  40.1 7.7 %collective-permute-start.10 = (bf16[144,512]{1,0:T(8,128)(2,1)S(1)}, bf16[144,512]{1,0:T(8,128)(2,1)S(1)}, u32[]{:S(2)}, u32[]{:S(2)}) collective-permute-start(bf16[144,512]{1,0:T(8,128)(2,1)S(1)} %get-tuple-element.71), channel_id=1, source_target_pairs={{0,2},{1,3},{2,0},{3,1},{4,6},{5,7},{6,4},{7,5},{8,10},{9,11},{10,... | collective-permute-start | bytes 442376 | tf_op jit(solution)/shard_map/ppermute | solution.py:307
  40.1 7.9 %collective-permute-start.11 = (bf16[144,512]{1,0:T(8,128)(2,1)S(1)}, bf16[144,512]{1,0:T(8,128)(2,1)S(1)}, u32[]{:S(2)}, u32[]{:S(2)}) collective-permute-start(bf16[144,512]{1,0:T(8,128)(2,1)S(1)} %get-tuple-element.72), channel_id=1, source_target_pairs={{0,1},{1,0},{2,3},{3,2},{4,5},{5,4},{6,7},{7,6},{8,9},{9,8},{10,11... | collective-permute-start | bytes 442376 | tf_op jit(solution)/shard_map/ppermute | solution.py:307
  41.0 11.5 %collective-permute-start.12 = (bf16[128,512]{1,0:T(8,128)(2,1)S(1)}, bf16[128,512]{1,0:T(8,128)(2,1)S(1)}, u32[]{:S(2)}, u32[]{:S(2)}) collective-permute-start(bf16[128,512]{1,0:T(8,128)(2,1)S(1)} %get-tuple-element.74), channel_id=1, source_target_pairs={{0,3},{1,2},{2,1},{3,0},{4,7},{5,6},{6,5},{7,4},{8,11},{9,10},{10,... | collective-permute-start | bytes 393224 | tf_op jit(solution)/shard_map/ppermute | solution.py:307
  43.6 9.5 %collective-permute-start.13 = (bf16[128,512]{1,0:T(8,128)(2,1)S(1)}, bf16[128,512]{1,0:T(8,128)(2,1)S(1)}, u32[]{:S(2)}, u32[]{:S(2)}) collective-permute-start(bf16[128,512]{1,0:T(8,128)(2,1)S(1)} %get-tuple-element.75), channel_id=1, source_target_pairs={{0,2},{1,3},{2,0},{3,1},{4,6},{5,7},{6,4},{7,5},{8,10},{9,11},{10,... | collective-permute-start | bytes 393224 | tf_op jit(solution)/shard_map/ppermute | solution.py:307
  44.8 8.3 %collective-permute-start.14 = (bf16[128,512]{1,0:T(8,128)(2,1)S(1)}, bf16[128,512]{1,0:T(8,128)(2,1)S(1)}, u32[]{:S(2)}, u32[]{:S(2)}) collective-permute-start(bf16[128,512]{1,0:T(8,128)(2,1)S(1)} %get-tuple-element.76), channel_id=1, source_target_pairs={{0,1},{1,0},{2,3},{3,2},{4,5},{5,4},{6,7},{7,6},{8,9},{9,8},{10,11... | collective-permute-start | bytes 393224 | tf_op jit(solution)/shard_map/ppermute | solution.py:307
  48.1 8.0 %collective-permute-start.17 = (f32[4,128]{1,0:T(4,128)S(1)}, f32[4,128]{1,0:T(4,128)S(1)}, u32[]{:S(2)}, u32[]{:S(2)}) collective-permute-start(f32[4,128]{1,0:T(4,128)S(1)} %get-tuple-element.82), channel_id=1, source_target_pairs={{0,20},{1,21},{2,22},{3,23},{4,16},{5,17},{6,18},{7,19},{8,28},{9,... | collective-permute-start | bytes 6152 | tf_op jit(solution)/shard_map/ppermute | solution.py:398
  52.4 4.5 %collective-permute-start.15 = (f32[4,128]{1,0:T(4,128)S(1)}, f32[4,128]{1,0:T(4,128)S(1)}, u32[]{:S(2)}, u32[]{:S(2)}) collective-permute-start(f32[4,128]{1,0:T(4,128)S(1)} %get-tuple-element.82), channel_id=1, source_target_pairs={{0,4},{1,5},{2,6},{3,7},{4,0},{5,1},{6,2},{7,3},{8,12},{9,13},{10,... | collective-permute-start | bytes 6152 | tf_op jit(solution)/shard_map/ppermute | solution.py:398
  52.5 3.6 %collective-permute-start.16 = (f32[4,128]{1,0:T(4,128)S(1)}, f32[4,128]{1,0:T(4,128)S(1)}, u32[]{:S(2)}, u32[]{:S(2)}) collective-permute-start(f32[4,128]{1,0:T(4,128)S(1)} %get-tuple-element.81), channel_id=1, source_target_pairs={{0,16},{1,17},{2,18},{3,19},{4,20},{5,21},{6,22},{7,23},{8,24},{9,... | collective-permute-start | bytes 6152 | tf_op jit(solution)/shard_map/ppermute | solution.py:398

commit v7 on v6

--- a/solution.py
+++ b/solution.py
@@ -173,7 +173,7 @@
 
 
 def inner_kernel(half, me_ref, *refs):
-    arrived, across = refs[:half], refs[half : half + 2]
+    arrived, across = refs[:half], (refs[half + 1], refs[half])
     outs = refs[half + 2 : 2 * half + 2]
     near_ref, part_ref, flip_ref, lag_ref = refs[2 * half + 2 : 2 * half + 6]
     far_ref, line, first_ref, second_ref, pair_ref, result_ref = refs[2 * half + 6 :]
@@ -366,8 +366,8 @@
     )
     inner = [inner[0]] + [swap(inner[k], k, count) for k in range(1, half)]
     outer = list(sent)
+    outer[1] = swap(outer[1], half + 1, count)
     outer[0] = swap(outer[0], half, count)
-    outer[1] = swap(outer[1], half + 1, count)
     outer[2], inner[1] = after(outer[2], inner[1])
     outer[2] = swap(outer[2], half + 2, count)
     outer[3], inner[2] = after(outer[3], inner[2])
@@ -392,7 +392,7 @@
         ],
         8 * nfil * own * slim * own,
         8 * own * slim,
-        where, *inner, *outer[:2],
+        where, *inner, outer[1], outer[0],
     )
     second = [second[0]] + [swap(second[k], k, count) for k in range(half - 1, 0, -1)][::-1]
     across = lambda value, move, turn: lax.ppermute(

time: 57.7 us -> 58.9 us (1.021)
  waiting for transfers between devices: 14.5 us -> 16 us
    ppermute x14, waiting for transfers between devices: 12.2 us -> 13.6 us  [swap(): return lax.ppermute(value, 'ctx', [(i, i ^ step) for i in range(count)])]
    ppermute x14, starting transfers between devices: 26.2 us -> 25.2 us  [swap(): return lax.ppermute(value, 'ctx', [(i, i ^ step) for i in range(count)])]
    ppermute x4, starting transfers between devices: 5.09 us -> 5.87 us  [halves_plan(): lax.ppermute(value, ('chan', 'ctx'), [(c * count + i, (c ^ move) * count...]
where the time goes in v7:
time: 58.9 us; the launch traced here: 58.8 us
  starting transfers between devices  31.1 us (53%)
  waiting for transfers between devices  16 us (27%)
  Pallas kernels  10.2 us (17%)
  between operations  0.8 us (1%)
  other arithmetic  0.6 us (1%)
    ppermute x14, starting transfers between devices, swap(): return lax.ppermute(value, 'ctx', [(i, i ^ step) for i in range(count)])  25.2 us
    ppermute x14, waiting for transfers between devices, swap(): return lax.ppermute(value, 'ctx', [(i, i ^ step) for i in range(count)])  13.6 us
    pallas_call x7, Pallas kernels, call(): pl.pallas_call(kernel, out_shape=outs, in_specs=[pl.BlockSpec(memory_spac...  10.2 us
    ppermute x4, starting transfers between devices, halves_plan(): lax.ppermute(value, ('chan', 'ctx'), [(c * count + i, (c ^ move) * count...  5.87 us
    ppermute x4, waiting for transfers between devices, halves_plan(): lax.ppermute(value, ('chan', 'ctx'), [(c * count + i, (c ^ move) * count...  2.37 us
  transfers between devices with their start and end apart: 18, of which 11 were waited for; matrix products, arithmetic and copies ran while one was open for 0% of the time, Pallas kernels for 16%

profile of v7, /device:TPU:0, one launch (start us, length us, event | category | flops | bytes accessed | tf_op | source)
XLA Modules:
  0.0 58.8 jit_solution(9771463185629935771)
XLA Ops:
  0.6 4.1 %collective-permute-start = (bf16[4,128]{1,0:T(4,128)(2,1)}, bf16[4,128]{1,0:T(4,128)(2,1)S(1)}, u32[]{:S(2)}, u32[]{:S(2)}) collective-permute-start(bf16[4,128]{1,0:T(4,128)(2,1)} %mine_ref.1), channel_id=1, source_target_pairs={{0,4},{1,5},{2,6},{3,7},{4,0},{5,1},{6,2},{7,3},{8,12},{9,13},{10,... | collective-permute-start | bytes 3080 | tf_op jit(solution)/shard_map/ppermute | solution.py:307
  4.7 2.1 %shard_map.92 = (bf16[128,512]{1,0:T(8,128)(2,1)S(1)}, bf16[128,512]{1,0:T(8,128)(2,1)S(1)}, bf16[128,512]{1,0:T(8,128)(2,1)S(1)}, bf16[128,512]{1,0:T(8,128)(2,...) custom-call(s32[1]{0:T(128)} %bitcast.me_ref, ...), custom_call_target="tpu_custom_call" | custom-call | flops 67108864 | bytes 3670016 | tf_op jit(solution)/shard_map/pallas_call | solution.py:317
  7.0 1.6 %collective-permute-start.1 = (bf16[272,512]{1,0:T(8,128)(2,1)S(1)}, bf16[272,512]{1,0:T(8,128)(2,1)S(1)}, u32[]{:S(2)}, u32[]{:S(2)}) collective-permute-start(bf16[272,512]{1,0:T(8,128)(2,1)S(1)} %get-tuple-element.48), channel_id=1, source_target_pairs={{0,1},{1,0},{2,3},{3,2},{4,5},{5,4},{6,7},{7,6},{8,9},{9,8},{10,11... | collective-permute-start | bytes 835592 | tf_op jit(solution)/shard_map/ppermute | solution.py:307
  8.6 1.6 %collective-permute-start.3 = (bf16[272,512]{1,0:T(8,128)(2,1)S(1)}, bf16[272,512]{1,0:T(8,128)(2,1)S(1)}, u32[]{:S(2)}, u32[]{:S(2)}) collective-permute-start(bf16[272,512]{1,0:T(8,128)(2,1)S(1)} %get-tuple-element.51), channel_id=1, source_target_pairs={{0,2},{1,3},{2,0},{3,1},{4,6},{5,7},{6,4},{7,5},{8,10},{9,11},{10,... | collective-permute-start | bytes 835592 | tf_op jit(solution)/shard_map/ppermute | solution.py:307
  10.2 0.4 collective-permute-start.5
  10.6 3.5 %collective-permute-start.6 = (bf16[128,512]{1,0:T(8,128)(2,1)S(1)}, bf16[128,512]{1,0:T(8,128)(2,1)S(1)}, u32[]{:S(2)}, u32[]{:S(2)}) collective-permute-start(bf16[128,512]{1,0:T(8,128)(2,1)S(1)} %get-tuple-element.57), channel_id=1, source_target_pairs={{0,5},{1,4},{2,7},{3,6},{4,1},{5,0},{6,3},{7,2},{8,13},{9,12},{10,... | collective-permute-start | bytes 393224 | tf_op jit(solution)/shard_map/ppermute | solution.py:307
  14.1 0.4 collective-permute-start.7
  14.4 2.7 %collective-permute-done.1.refs_1_ = bf16[272,512]{1,0:T(8,128)(2,1)S(1)} collective-permute-done((bf16[272,512]{1,0:T(8,128)(2,1)S(1)}, bf16[272,512]{1,0:T(8,128)(2,1)S(1)}, u32[]{:S(2)}, u32[]{:S(2)}) %collective-permute-start.1) | collective-permute-done | bytes 278560 | tf_op jit(solution)/shard_map/ppermute | solution.py:307
  17.1 2.2 %collective-permute-start.2 = (bf16[128,512]{1,0:T(8,128)(2,1)S(1)}, bf16[128,512]{1,0:T(8,128)(2,1)S(1)}, u32[]{:S(2)}, u32[]{:S(2)}) collective-permute-start(bf16[128,512]{1,0:T(8,128)(2,1)S(1)} %get-tuple-element.49), channel_id=1, source_target_pairs={{0,6},{1,7},{2,4},{3,5},{4,2},{5,3},{6,0},{7,1},{8,14},{9,15},{10,... | collective-permute-start | bytes 393224 | tf_op jit(solution)/shard_map/ppermute | solution.py:307
  19.3 4.5 %collective-permute-done.3.refs_2_ = bf16[272,512]{1,0:T(8,128)(2,1)S(1)} collective-permute-done((bf16[272,512]{1,0:T(8,128)(2,1)S(1)}, bf16[272,512]{1,0:T(8,128)(2,1)S(1)}, u32[]{:S(2)}, u32[]{:S(2)}) %collective-permute-start.3) | collective-permute-done | bytes 278560 | tf_op jit(solution)/shard_map/ppermute | solution.py:307
  23.8 3.5 %collective-permute-start.4 = (bf16[128,512]{1,0:T(8,128)(2,1)S(1)}, bf16[128,512]{1,0:T(8,128)(2,1)S(1)}, u32[]{:S(2)}, u32[]{:S(2)}) collective-permute-start(bf16[128,512]{1,0:T(8,128)(2,1)S(1)} %get-tuple-element.52), channel_id=1, source_target_pairs={{0,7},{1,6},{2,5},{3,4},{4,3},{5,2},{6,1},{7,0},{8,15},{9,14},{10,... | collective-permute-start | bytes 393224 | tf_op jit(solution)/shard_map/ppermute | solution.py:307
  27.3 1.7 %collective-permute-done.7.refs_5_ = bf16[128,512]{1,0:T(8,128)(2,1)S(1)} collective-permute-done((bf16[128,512]{1,0:T(8,128)(2,1)S(1)}, bf16[128,512]{1,0:T(8,128)(2,1)S(1)}, u32[]{:S(2)}, u32[]{:S(2)}) %collective-permute-start.7) | collective-permute-done | bytes 131104 | tf_op jit(solution)/shard_map/ppermute | solution.py:307
  29.0 0.5 collective-permute-done.5.refs_3_
  29.5 4.5 %shard_map.94 = (bf16[128,512]{1,0:T(8,128)(2,1)S(1)}, bf16[128,512]{1,0:T(8,128)(2,1)S(1)}, bf16[128,512]{1,0:T(8,128)(2,1)S(1)}, bf16[128,512]{1,0:T(8,128)(2,...) custom-call(s32[1]{0:T(128)} %bitcast.me_ref, ...), custom_call_target="tpu_custom_call" | custom-call | flops 4294967296 | bytes 2097152 | tf_op jit(solution)/shard_map/pallas_call | solution.py:317
  34.0 0.7 %collective-permute-done.4.refs_1_ = bf16[128,512]{1,0:T(8,128)(2,1)S(1)} collective-permute-done((bf16[128,512]{1,0:T(8,128)(2,1)S(1)}, bf16[128,512]{1,0:T(8,128)(2,1)S(1)}, u32[]{:S(2)}, u32[]{:S(2)}) %collective-permute-start.4) | collective-permute-done | bytes 131104 | tf_op jit(solution)/shard_map/ppermute | solution.py:307
  34.7 0.8 %shard_map.95 = f32[8,1024]{1,0:T(8,128)S(1)} custom-call(s32[1]{0:T(128)} %bitcast.me_ref, bf16[128,512]{1,0:T(8,128)(2,1)S(1)} %collective-permute-done.2.refs_0_, bf16[128,512]{1,0:T(8,128)(2,1)S(1)} %collective-permute-done.4.refs_1_, bf16[512,512]{1,0:T(8,128)(2,1)S(1)} %get-tuple-element.59.refs_2_, f32[8,1024]{1,0:T(8,128)S(1)} %get-tuple-element.60.refs_3_), custom_call_target="tpu_custom_call" | custom-call | flops 268435456 | bytes 262144 | tf_op jit(solution)/shard_map/pallas_call | solution.py:317
  35.6 0.8 %shard_map.96 = (bf16[144,512]{1,0:T(8,128)(2,1)S(1)}, bf16[144,512]{1,0:T(8,128)(2,1)S(1)}, bf16[144,512]{1,0:T(8,128)(2,1)S(1)}, bf16[144,512]{1,0:T(8,128)(2,1)S(1)}) custom-call(s32[1]{0:T(128)} %bitcast.me_ref, bf16[128,512]{1,0:T(8,128)(2,1)S(1)} %collective-permute-done.2.refs_0_, bf16[128,512]{1,0:T(8,128)(2,1)S(1)} %collective-permute-done.4.refs_1_, ...), custom_call_target="tpu_custom_call" | custom-call | flops 536870912 | bytes 1048576 | tf_op jit(solution)/shard_map/pallas_call | solution.py:317
  36.4 0.3 collective-permute-done.8
  36.7 0.2 shard_map.97
  36.9 3.7 %collective-permute-start.9 = (bf16[144,512]{1,0:T(8,128)(2,1)S(1)}, bf16[144,512]{1,0:T(8,128)(2,1)S(1)}, u32[]{:S(2)}, u32[]{:S(2)}) collective-permute-start(bf16[144,512]{1,0:T(8,128)(2,1)S(1)} %get-tuple-element.70), channel_id=1, source_target_pairs={{0,3},{1,2},{2,1},{3,0},{4,7},{5,6},{6,5},{7,4},{8,11},{9,10},{10,... | collective-permute-start | bytes 442376 | tf_op jit(solution)/shard_map/ppermute | solution.py:307
  40.6 0.6 %collective-permute-start.11 = (bf16[144,512]{1,0:T(8,128)(2,1)S(1)}, bf16[144,512]{1,0:T(8,128)(2,1)S(1)}, u32[]{:S(2)}, u32[]{:S(2)}) collective-permute-start(bf16[144,512]{1,0:T(8,128)(2,1)S(1)} %get-tuple-element.72), channel_id=1, source_target_pairs={{0,1},{1,0},{2,3},{3,2},{4,5},{5,4},{6,7},{7,6},{8,9},{9,8},{10,11... | collective-permute-start | bytes 442376 | tf_op jit(solution)/shard_map/ppermute | solution.py:307
  41.3 2.8 %collective-permute-start.12 = (bf16[128,512]{1,0:T(8,128)(2,1)S(1)}, bf16[128,512]{1,0:T(8,128)(2,1)S(1)}, u32[]{:S(2)}, u32[]{:S(2)}) collective-permute-start(bf16[128,512]{1,0:T(8,128)(2,1)S(1)} %get-tuple-element.74), channel_id=1, source_target_pairs={{0,3},{1,2},{2,1},{3,0},{4,7},{5,6},{6,5},{7,4},{8,11},{9,10},{10,... | collective-permute-start | bytes 393224 | tf_op jit(solution)/shard_map/ppermute | solution.py:307
  44.1 1.1 %collective-permute-done.9.refs_1_ = bf16[144,512]{1,0:T(8,128)(2,1)S(1)} collective-permute-done((bf16[144,512]{1,0:T(8,128)(2,1)S(1)}, bf16[144,512]{1,0:T(8,128)(2,1)S(1)}, u32[]{:S(2)}, u32[]{:S(2)}) %collective-permute-start.9) | collective-permute-done | bytes 147488 | tf_op jit(solution)/shard_map/ppermute | solution.py:307
  45.3 0.8 %collective-permute-start.14 = (bf16[128,512]{1,0:T(8,128)(2,1)S(1)}, bf16[128,512]{1,0:T(8,128)(2,1)S(1)}, u32[]{:S(2)}, u32[]{:S(2)}) collective-permute-start(bf16[128,512]{1,0:T(8,128)(2,1)S(1)} %get-tuple-element.76), channel_id=1, source_target_pairs={{0,1},{1,0},{2,3},{3,2},{4,5},{5,4},{6,7},{7,6},{8,9},{9,8},{10,11... | collective-permute-start | bytes 393224 | tf_op jit(solution)/shard_map/ppermute | solution.py:307
  46.1 2.0 %collective-permute-done.10.refs_2_ = bf16[144,512]{1,0:T(8,128)(2,1)S(1)} collective-permute-done((bf16[144,512]{1,0:T(8,128)(2,1)S(1)}, bf16[144,512]{1,0:T(8,128)(2,1)S(1)}, u32[]{:S(2)}, u32[]{:S(2)}) %collective-permute-start.10) | collective-permute-done | bytes 147488 | tf_op jit(solution)/shard_map/ppermute | solution.py:307
  48.0 0.5 collective-permute-done.11.refs_3_
  48.6 5.2 %collective-permute-start.17 = (f32[4,128]{1,0:T(4,128)S(1)}, f32[4,128]{1,0:T(4,128)S(1)}, u32[]{:S(2)}, u32[]{:S(2)}) collective-permute-start(f32[4,128]{1,0:T(4,128)S(1)} %get-tuple-element.82), channel_id=1, source_target_pairs={{0,20},{1,21},{2,22},{3,23},{4,16},{5,17},{6,18},{7,19},{8,28},{9,... | collective-permute-start | bytes 6152 | tf_op jit(solution)/shard_map/ppermute | solution.py:398
  53.7 0.6 %collective-permute-start.16 = (f32[4,128]{1,0:T(4,128)S(1)}, f32[4,128]{1,0:T(4,128)S(1)}, u32[]{:S(2)}, u32[]{:S(2)}) collective-permute-start(f32[4,128]{1,0:T(4,128)S(1)} %get-tuple-element.81), channel_id=1, source_target_pairs={{0,16},{1,17},{2,18},{3,19},{4,20},{5,21},{6,22},{7,23},{8,24},{9,... | collective-permute-start | bytes 6152 | tf_op jit(solution)/shard_map/ppermute | solution.py:398
  54.4 1.8 %shard_map.98 = (bf16[128,2048]{1,0:T(8,128)(2,1)}, bf16[128,2048]{1,0:T(8,128)(2,1)}, bf16[128,2048]{1,0:T(8,128)(2,1)}, bf16[128,2048]{1,0:T(8,128)(2,1)}) custom-call(s32[1]{0:T(128)} %bitcast.me_ref, bf16[128,2048]{1,0:T(8,128)(2,1)S(1)} %copy-done, bf16[128,2048]{1,0:T(8,128)(2,1)S(1)} %copy-done.1, bf16[128,2048]{1,0:T(8,128)(2,1)S(1)} %copy-done.2, ...), custom_call_target="tpu_custom_call" | custom-call | flops 134217728 | bytes 5242880 | tf_op jit(solution)/shard_map/pallas_call | solution.py:317
  56.2 1.1 %collective-permute-done.16 = f32[4,128]{1,0:T(4,128)S(1)} collective-permute-done((f32[4,128]{1,0:T(4,128)S(1)}, f32[4,128]{1,0:T(4,128)S(1)}, u32[]{:S(2)}, u32[]{:S(2)}) %collective-permute-start.16) | collective-permute-done | bytes 2080 | tf_op jit(solution)/shard_map/ppermute | solution.py:398
  57.3 0.9 %collective-permute-done.15 = f32[4,128]{1,0:T(4,128)S(1)} collective-permute-done((f32[4,128]{1,0:T(4,128)S(1)}, f32[4,128]{1,0:T(4,128)S(1)}, u32[]{:S(2)}, u32[]{:S(2)}) %collective-permute-start.15) | collective-permute-done | bytes 2080 | tf_op jit(solution)/shard_map/ppermute | solution.py:398
  58.2 0.6 add_multiply_fusion
  (26 shorter events, 0.3 us)
Async XLA Ops:
  0.6 6.2 %copy-start.4 = (bf16[4,128]{1,0:T(4,128)(2,1)S(1)}, bf16[4,128]{1,0:T(4,128)(2,1)}, u32[]{:S(2)}) copy-start(bf16[4,128]{1,0:T(4,128)(2,1)} %mine_ref.1) | copy-start | bytes 3076
  0.6 6.2 %collective-permute-start = (bf16[4,128]{1,0:T(4,128)(2,1)}, bf16[4,128]{1,0:T(4,128)(2,1)S(1)}, u32[]{:S(2)}, u32[]{:S(2)}) collective-permute-start(bf16[4,128]{1,0:T(4,128)(2,1)} %mine_ref.1), channel_id=1, source_target_pairs={{0,4},{1,5},{2,6},{3,7},{4,0},{5,1},{6,2},{7,3},{8,12},{9,13},{10,... | collective-permute-start | bytes 3080 | tf_op jit(solution)/shard_map/ppermute | solution.py:307
  7.0 10.1 %collective-permute-start.1 = (bf16[272,512]{1,0:T(8,128)(2,1)S(1)}, bf16[272,512]{1,0:T(8,128)(2,1)S(1)}, u32[]{:S(2)}, u32[]{:S(2)}) collective-permute-start(bf16[272,512]{1,0:T(8,128)(2,1)S(1)} %get-tuple-element.48), channel_id=1, source_target_pairs={{0,1},{1,0},{2,3},{3,2},{4,5},{5,4},{6,7},{7,6},{8,9},{9,8},{10,11... | collective-permute-start | bytes 835592 | tf_op jit(solution)/shard_map/ppermute | solution.py:307
  8.6 15.2 %collective-permute-start.3 = (bf16[272,512]{1,0:T(8,128)(2,1)S(1)}, bf16[272,512]{1,0:T(8,128)(2,1)S(1)}, u32[]{:S(2)}, u32[]{:S(2)}) collective-permute-start(bf16[272,512]{1,0:T(8,128)(2,1)S(1)} %get-tuple-element.51), channel_id=1, source_target_pairs={{0,2},{1,3},{2,0},{3,1},{4,6},{5,7},{6,4},{7,5},{8,10},{9,11},{10,... | collective-permute-start | bytes 835592 | tf_op jit(solution)/shard_map/ppermute | solution.py:307
  10.2 19.3 %collective-permute-start.5 = (bf16[272,512]{1,0:T(8,128)(2,1)S(1)}, bf16[272,512]{1,0:T(8,128)(2,1)S(1)}, u32[]{:S(2)}, u32[]{:S(2)}) collective-permute-start(bf16[272,512]{1,0:T(8,128)(2,1)S(1)} %get-tuple-element.56), channel_id=1, source_target_pairs={{0,3},{1,2},{2,1},{3,0},{4,7},{5,6},{6,5},{7,4},{8,11},{9,10},{10,... | collective-permute-start | bytes 835592 | tf_op jit(solution)/shard_map/ppermute | solution.py:307
  10.6 16.7 %collective-permute-start.6 = (bf16[128,512]{1,0:T(8,128)(2,1)S(1)}, bf16[128,512]{1,0:T(8,128)(2,1)S(1)}, u32[]{:S(2)}, u32[]{:S(2)}) collective-permute-start(bf16[128,512]{1,0:T(8,128)(2,1)S(1)} %get-tuple-element.57), channel_id=1, source_target_pairs={{0,5},{1,4},{2,7},{3,6},{4,1},{5,0},{6,3},{7,2},{8,13},{9,12},{10,... | collective-permute-start | bytes 393224 | tf_op jit(solution)/shard_map/ppermute | solution.py:307
  14.1 14.9 %collective-permute-start.7 = (bf16[128,512]{1,0:T(8,128)(2,1)S(1)}, bf16[128,512]{1,0:T(8,128)(2,1)S(1)}, u32[]{:S(2)}, u32[]{:S(2)}) collective-permute-start(bf16[128,512]{1,0:T(8,128)(2,1)S(1)} %get-tuple-element.58), channel_id=1, source_target_pairs={{0,4},{1,5},{2,6},{3,7},{4,0},{5,1},{6,2},{7,3},{8,12},{9,13},{10,... | collective-permute-start | bytes 393224 | tf_op jit(solution)/shard_map/ppermute | solution.py:307
  17.1 16.9 %collective-permute-start.2 = (bf16[128,512]{1,0:T(8,128)(2,1)S(1)}, bf16[128,512]{1,0:T(8,128)(2,1)S(1)}, u32[]{:S(2)}, u32[]{:S(2)}) collective-permute-start(bf16[128,512]{1,0:T(8,128)(2,1)S(1)} %get-tuple-element.49), channel_id=1, source_target_pairs={{0,6},{1,7},{2,4},{3,5},{4,2},{5,3},{6,0},{7,1},{8,14},{9,15},{10,... | collective-permute-start | bytes 393224 | tf_op jit(solution)/shard_map/ppermute | solution.py:307
  23.8 10.9 %collective-permute-start.4 = (bf16[128,512]{1,0:T(8,128)(2,1)S(1)}, bf16[128,512]{1,0:T(8,128)(2,1)S(1)}, u32[]{:S(2)}, u32[]{:S(2)}) collective-permute-start(bf16[128,512]{1,0:T(8,128)(2,1)S(1)} %get-tuple-element.52), channel_id=1, source_target_pairs={{0,7},{1,6},{2,5},{3,4},{4,3},{5,2},{6,1},{7,0},{8,15},{9,14},{10,... | collective-permute-start | bytes 393224 | tf_op jit(solution)/shard_map/ppermute | solution.py:307
  35.5 1.3 %collective-permute-start.8 = (f32[8,1024]{1,0:T(8,128)S(1)}, f32[8,1024]{1,0:T(8,128)S(1)}, u32[]{:S(2)}, u32[]{:S(2)}) collective-permute-start(f32[8,1024]{1,0:T(8,128)S(1)} %shard_map.95), channel_id=1, source_target_pairs={{0,8},{1,9},{2,10},{3,11},{4,12},{5,13},{6,14},{7,15},{8,0},{9,1},... | collective-permute-start | bytes 98312 | tf_op jit(solution)/shard_map/ppermute | solution.py:398
  35.5 18.8 %copy-start = (bf16[128,2048]{1,0:T(8,128)(2,1)S(1)}, bf16[128,2048]{1,0:T(8,128)(2,1)}, u32[]{:S(2)}) copy-start(bf16[128,2048]{1,0:T(8,128)(2,1)} %q_ref.3) | copy-start | bytes 1572868
  35.6 18.8 %copy-start.1 = (bf16[128,2048]{1,0:T(8,128)(2,1)S(1)}, bf16[128,2048]{1,0:T(8,128)(2,1)}, u32[]{:S(2)}) copy-start(bf16[128,2048]{1,0:T(8,128)(2,1)} %k_ref.3) | copy-start | bytes 1572868
  35.6 18.8 %copy-start.2 = (bf16[128,2048]{1,0:T(8,128)(2,1)S(1)}, bf16[128,2048]{1,0:T(8,128)(2,1)}, u32[]{:S(2)}) copy-start(bf16[128,2048]{1,0:T(8,128)(2,1)} %v_ref.3) | copy-start | bytes 1572868
  35.6 18.8 %copy-start.3 = (bf16[128,2048]{1,0:T(8,128)(2,1)S(1)}, bf16[128,2048]{1,0:T(8,128)(2,1)}, u32[]{:S(2)}) copy-start(bf16[128,2048]{1,0:T(8,128)(2,1)} %g_ref.3) | copy-start | bytes 1572868
  36.9 8.4 %collective-permute-start.9 = (bf16[144,512]{1,0:T(8,128)(2,1)S(1)}, bf16[144,512]{1,0:T(8,128)(2,1)S(1)}, u32[]{:S(2)}, u32[]{:S(2)}) collective-permute-start(bf16[144,512]{1,0:T(8,128)(2,1)S(1)} %get-tuple-element.70), channel_id=1, source_target_pairs={{0,3},{1,2},{2,1},{3,0},{4,7},{5,6},{6,5},{7,4},{8,11},{9,10},{10,... | collective-permute-start | bytes 442376 | tf_op jit(solution)/shard_map/ppermute | solution.py:307
  40.6 7.4 %collective-permute-start.10 = (bf16[144,512]{1,0:T(8,128)(2,1)S(1)}, bf16[144,512]{1,0:T(8,128)(2,1)S(1)}, u32[]{:S(2)}, u32[]{:S(2)}) collective-permute-start(bf16[144,512]{1,0:T(8,128)(2,1)S(1)} %get-tuple-element.71), channel_id=1, source_target_pairs={{0,2},{1,3},{2,0},{3,1},{4,6},{5,7},{6,4},{7,5},{8,10},{9,11},{10,... | collective-permute-start | bytes 442376 | tf_op jit(solution)/shard_map/ppermute | solution.py:307
  40.6 7.9 %collective-permute-start.11 = (bf16[144,512]{1,0:T(8,128)(2,1)S(1)}, bf16[144,512]{1,0:T(8,128)(2,1)S(1)}, u32[]{:S(2)}, u32[]{:S(2)}) collective-permute-start(bf16[144,512]{1,0:T(8,128)(2,1)S(1)} %get-tuple-element.72), channel_id=1, source_target_pairs={{0,1},{1,0},{2,3},{3,2},{4,5},{5,4},{6,7},{7,6},{8,9},{9,8},{10,11... | collective-permute-start | bytes 442376 | tf_op jit(solution)/shard_map/ppermute | solution.py:307
  41.3 12.4 %collective-permute-start.12 = (bf16[128,512]{1,0:T(8,128)(2,1)S(1)}, bf16[128,512]{1,0:T(8,128)(2,1)S(1)}, u32[]{:S(2)}, u32[]{:S(2)}) collective-permute-start(bf16[128,512]{1,0:T(8,128)(2,1)S(1)} %get-tuple-element.74), channel_id=1, source_target_pairs={{0,3},{1,2},{2,1},{3,0},{4,7},{5,6},{6,5},{7,4},{8,11},{9,10},{10,... | collective-permute-start | bytes 393224 | tf_op jit(solution)/shard_map/ppermute | solution.py:307
  44.1 10.2 %collective-permute-start.13 = (bf16[128,512]{1,0:T(8,128)(2,1)S(1)}, bf16[128,512]{1,0:T(8,128)(2,1)S(1)}, u32[]{:S(2)}, u32[]{:S(2)}) collective-permute-start(bf16[128,512]{1,0:T(8,128)(2,1)S(1)} %get-tuple-element.75), channel_id=1, source_target_pairs={{0,2},{1,3},{2,0},{3,1},{4,6},{5,7},{6,4},{7,5},{8,10},{9,11},{10,... | collective-permute-start | bytes 393224 | tf_op jit(solution)/shard_map/ppermute | solution.py:307
  45.3 9.1 %collective-permute-start.14 = (bf16[128,512]{1,0:T(8,128)(2,1)S(1)}, bf16[128,512]{1,0:T(8,128)(2,1)S(1)}, u32[]{:S(2)}, u32[]{:S(2)}) collective-permute-start(bf16[128,512]{1,0:T(8,128)(2,1)S(1)} %get-tuple-element.76), channel_id=1, source_target_pairs={{0,1},{1,0},{2,3},{3,2},{4,5},{5,4},{6,7},{7,6},{8,9},{9,8},{10,11... | collective-permute-start | bytes 393224 | tf_op jit(solution)/shard_map/ppermute | solution.py:307
  48.6 8.8 %collective-permute-start.17 = (f32[4,128]{1,0:T(4,128)S(1)}, f32[4,128]{1,0:T(4,128)S(1)}, u32[]{:S(2)}, u32[]{:S(2)}) collective-permute-start(f32[4,128]{1,0:T(4,128)S(1)} %get-tuple-element.82), channel_id=1, source_target_pairs={{0,20},{1,21},{2,22},{3,23},{4,16},{5,17},{6,18},{7,19},{8,28},{9,... | collective-permute-start | bytes 6152 | tf_op jit(solution)/shard_map/ppermute | solution.py:398
  53.7 4.5 %collective-permute-start.15 = (f32[4,128]{1,0:T(4,128)S(1)}, f32[4,128]{1,0:T(4,128)S(1)}, u32[]{:S(2)}, u32[]{:S(2)}) collective-permute-start(f32[4,128]{1,0:T(4,128)S(1)} %get-tuple-element.82), channel_id=1, source_target_pairs={{0,4},{1,5},{2,6},{3,7},{4,0},{5,1},{6,2},{7,3},{8,12},{9,13},{10,... | collective-permute-start | bytes 6152 | tf_op jit(solution)/shard_map/ppermute | solution.py:398
  53.7 3.6 %collective-permute-start.16 = (f32[4,128]{1,0:T(4,128)S(1)}, f32[4,128]{1,0:T(4,128)S(1)}, u32[]{:S(2)}, u32[]{:S(2)}) collective-permute-start(f32[4,128]{1,0:T(4,128)S(1)} %get-tuple-element.81), channel_id=1, source_target_pairs={{0,16},{1,17},{2,18},{3,19},{4,20},{5,21},{6,22},{7,23},{8,24},{9,... | collective-permute-start | bytes 6152 | tf_op jit(solution)/shard_map/ppermute | solution.py:398
